TPU v7x, 32 devices: a whole 2x2x4 slice. The times are simulated.
32 devices in a mesh: seq: 2 (over x), tp: 16 (over z, y, core).
Axes of the slice: x: 2, y: 2, z: 4, core: 2. Of those that a mesh axis runs over, the one named last changes fastest.
Arguments:
- text_states: bfloat16 [8192, 768], P(('seq', 'tp')), may hold values from -6 to 6
- visual_maps: bfloat16 [1024, 256], P(('seq', 'tp'))
- text_boxes: int32 [2, 8192], P(None, ('seq', 'tp')), may hold values from 0 to 999
- text_lengths: int32 [16], replicated, may hold values from 64 to 512, as said below
- qkv_weight: bfloat16 [2, 3, 768, 768], replicated, may hold values from -0.21875 to 0.21875
- out_weight: bfloat16 [2, 768, 768], replicated, may hold values from -2.5 to 2.5
- attn_bias: float32 [2, 3, 768], replicated, may hold values from -3 to 3
- ffn_in: bfloat16 [2, 3072, 768], P(None, 'tp'), may hold values from -0.21875 to 0.21875
- ffn_in_bias: bfloat16 [2, 3072], P(None, 'tp'), may hold values from -3 to 3
- ffn_out: bfloat16 [2, 3072, 768], P(None, 'tp'), may hold values from -0.109375 to 0.109375
- ffn_out_bias: float32 [2, 768], replicated, may hold values from -3 to 3
- norm_gain: float32 [2, 2, 768], replicated, may hold values from 0.25 to 1.75
- norm_shift: float32 [2, 2, 768], replicated, may hold values from -3 to 3
- bias_table: float32 [160, 12], replicated, may hold values from -3 to 3
- vis_weight: bfloat16 [256, 768], replicated, may hold values from -0.375 to 0.375
- vis_bias: float32 [768], replicated, may hold values from -3 to 3
- bn_gain: float32 [256], replicated, may hold values from 0.25 to 1.75
- bn_shift: float32 [256], replicated, may hold values from -3 to 3
- cotangent: bfloat16 [9216, 768], P(('seq', 'tp')), may hold values from -6 to 6
Outputs:
- out_states: bfloat16 [9216, 768], P(('seq', 'tp'))
- grad_text: float32 [8192, 768], P(('seq', 'tp'))
- grad_maps: float32 [1024, 256], P(('seq', 'tp'))
- grad_qkv: float32 [2, 3, 768, 768], P(None, None, 'tp')
- grad_out_weight: float32 [2, 768, 768], P(None, 'tp')
- grad_attn_bias: float32 [2, 3, 768], replicated
- grad_ffn_in: float32 [2, 3072, 768], P(None, 'tp')
- grad_ffn_in_bias: float32 [2, 3072], P(None, 'tp')
- grad_ffn_out: float32 [2, 3072, 768], P(None, 'tp')
- grad_ffn_out_bias: float32 [2, 768], replicated
- grad_norm_gain: float32 [2, 2, 768], replicated
- grad_norm_shift: float32 [2, 2, 768], replicated
- grad_bias_table: float32 [160, 12], replicated
- grad_vis_weight: float32 [256, 768], replicated
- grad_vis_bias: float32 [768], replicated
- grad_bn_gain: float32 [256], replicated
- grad_bn_shift: float32 [256], replicated
Inputs may be any that keep to these rules, and one draw needn't show every extreme that they name: `text_lengths`: some page has all 512 text slots used.
All inputs are finite; a program needn't handle non-finite values.
Results may differ from a plain program's by a relative error of at most 0.035.
Values may be sent and summed in bfloat16 or wider, within the bound.
No kernel may reach another device: no remote copies, remote signals or barrier semaphores. Data moves between devices by JAX's collectives and lax.ppermute only.
A program may use at most 256 MiB of HBM per device.

v0:
```python
import functools

import jax
import jax.numpy as jnp
import numpy as np
from jax import lax
from jax.experimental import pallas as pl
from jax.experimental.pallas import tpu as pltpu
from jax.sharding import PartitionSpec as P

HEADS = 12
HEAD_DIM = 64
VIS_TOK = 49
VIS_SLOTS = 64
POS_BINS = 32
BOX_BINS = 64
LAYERS = 2
BUCKETS = POS_BINS + 2 * BOX_BINS

HALF_TEXT = 256
HALF_SLOTS = VIS_SLOTS // 2
ROWS = HALF_TEXT + HALF_SLOTS
KEYS = 640
PAIRS = HEADS // 2
LANES = 128
FOLDS = 2
BLOCKS = 4
HALF = BLOCKS // 2
norm_epsilon = 1e-05
NEVER = -1e30
bf16 = jnp.bfloat16
f32 = jnp.float32
MIB = 1 << 20
brief = pl.CostEstimate(flops=1, bytes_accessed=1, transcendentals=0)


def mesh_bits(axis):
    return (lax.axis_size(axis) - 1).bit_length()


def flipped(block, axis, bit):
    count = lax.axis_size(axis)
    return lax.ppermute(block, axis, [(i, i ^ (1 << bit)) for i in range(count)])


def total_over_all(value):
    for axis in ("tp", "seq"):
        for bit in range(mesh_bits(axis)):
            value = value + flipped(value, axis, bit)
    return value


def add_low(left, right):
    return (left.astype(f32) + right.astype(f32)).astype(bf16)


def tied(values, after):
    return lax.optimization_barrier((tuple(values), tuple(after)))[0]


class Shards:
    def __init__(self, near_keep, near_send, seq_keep, seq_send):
        self.near = near_keep
        self.seq = seq_keep
        self.near_came = flipped(near_send, "tp", 1)
        self.seq_came = flipped(seq_send, "seq", 0)

    def underway(self):
        return [self.near_came, self.seq_came]

    def second(self, *after):
        near, near_came, seq, seq_came = tied(
            (self.near, self.near_came, self.seq, self.seq_came), after
        )
        turn = lax.axis_index("seq") % 2
        middle = near.shape[-1] // 2
        pick = lambda block, which: jnp.where(
            turn == which, block[..., :middle], block[..., middle:]
        )
        self.near = add_low(pick(near, 0), pick(near_came, 0))
        self.near_came = flipped(add_low(pick(near, 1), pick(near_came, 1)), "seq", 0)
        far = seq.shape[0] // 2
        self.seq = add_low(seq[:far], seq_came[:far])
        self.seq_came = flipped(add_low(seq[far:], seq_came[far:]), "tp", 1)

    def scatter(self, *after):
        near, near_came, seq, seq_came = tied(
            (self.near, self.near_came, self.seq, self.seq_came), after
        )
        both = jnp.concatenate([add_low(near, near_came), add_low(seq, seq_came)], axis=1)
        count = lax.axis_size("tp")
        groups = [list(range(first, count, 4)) for first in range(4)]
        self.shard = lax.psum_scatter(both, "tp", scatter_dimension=0, axis_index_groups=groups)

    def halve(self, *after):
        near, near_came, seq, seq_came = tied(
            (self.near, self.near_came, self.seq, self.seq_came), after
        )
        bit = mesh_bits("tp") - (near.shape[0] - 1).bit_length()
        pick = lambda block, which: block.reshape((-1, 2) + block.shape[1:])[:, which]
        add = lambda which: jnp.concatenate(
            [
                add_low(pick(near, which), pick(near_came, which)),
                add_low(pick(seq, which), pick(seq_came, which)),
            ],
            axis=1,
        )
        self.shard, self.came = add(0), flipped(add(1), "tp", bit)
        self.bit = bit + 1

    def halve_more(self, *after):
        shard, came = tied((self.shard, self.came), after)
        if shard.shape[0] == 1:
            self.shard = add_low(shard, came)[0]
            return
        pick = lambda block, which: block.reshape((-1, 2) + block.shape[1:])[:, which]
        self.shard = add_low(pick(shard, 0), pick(came, 0))
        self.came = flipped(add_low(pick(shard, 1), pick(came, 1)), "tp", self.bit)
        self.bit += 1

    def join(self, *after):
        (shard,) = tied((self.shard,), after)
        for bit in range(1, mesh_bits("seq")):
            shard = add_low(shard, flipped(shard, "seq", bit))
        self.shard = shard
        self.other = flipped(shard, "seq", 0)


class Tree:
    def __init__(self, value, ways, join=None, add=add_low):
        self.lefts = [value]
        self.rights = []
        self.steps = list(ways) + ([join] if join else [])
        self.add = add

    def step(self, *after):
        if after:
            both = tied(self.lefts + self.rights, after)
            self.lefts, self.rights = list(both[:1]), list(both[1:])
        if self.rights:
            self.lefts = [self.add(self.lefts[0], self.rights[0])]
        self.rights = [flipped(self.lefts[0], *self.steps.pop(0))]

    def result(self):
        return self.lefts[0], self.rights[0]


def page_places(half, length, own_boxes, other_boxes):
    def slots(width, first, second):
        lane = lax.broadcasted_iota(jnp.int32, (1, width), 1)
        place = jnp.where(lane < HALF_SLOTS, first + lane, second + lane - HALF_SLOTS)
        place = jnp.where(lane < VIS_SLOTS, place, VIS_SLOTS - 1)
        row = (place * 37) >> 8
        return place, 71 + 143 * (place - 7 * row), 71 + 143 * row

    text = lax.broadcasted_iota(jnp.int32, (1, HALF_TEXT), 1)
    own_text = half * HALF_TEXT + text
    other_text = (1 - half) * HALF_TEXT + text
    slot = slots(LANES, half * HALF_SLOTS, (1 - half) * HALF_SLOTS)
    lane = lax.broadcasted_iota(jnp.int32, (1, LANES), 1)
    slot_used = jnp.where((slot[0] < VIS_TOK) & (lane < VIS_SLOTS), 1, 0)
    keys = (
        jnp.concatenate([own_text, other_text, slot[0]], axis=1),
        jnp.concatenate([own_boxes[0:1], other_boxes[0:1], slot[1]], axis=1),
        jnp.concatenate([own_boxes[1:2], other_boxes[1:2], slot[2]], axis=1),
        jnp.concatenate(
            [
                jnp.where(own_text < length, 1, 0),
                jnp.where(other_text < length, 1, 0),
                slot_used,
            ],
            axis=1,
        ),
    )
    queries = (
        jnp.concatenate([own_text, slot[0]], axis=1),
        jnp.concatenate([own_boxes[0:1], slot[1]], axis=1),
        jnp.concatenate([own_boxes[1:2], slot[2]], axis=1),
    )
    return keys, queries


def as_columns(rows):
    stacked = jnp.concatenate(list(rows) + [rows[0]] * (8 - len(rows)), axis=0)
    turned = jnp.transpose(stacked.astype(f32), (1, 0)).astype(jnp.int32)
    return [turned[:ROWS, i : i + 1] for i in range(len(rows))]


def bias_kernel(facts, own_boxes, other_boxes, table_a, table_b, out, near_s, across_s, down_s):
    @pl.when(pl.program_id(0) == 0)
    def _():
        keys, queries = page_places(facts[0], facts[1], own_boxes[...], other_boxes[...])
        place, x, y = as_columns(queries)
        near_s[...] = jnp.clip(keys[0] - place, -16, 15) + 16
        across_s[...] = jnp.clip((keys[1] - x) >> 4, -32, 31) + 64
        down_s[...] = jnp.where(
            keys[3] > 0, jnp.clip((keys[2] - y) >> 4, -32, 31) + 32, BOX_BINS
        )

    a = jnp.broadcast_to(table_a[0, 0:1, :], (ROWS, LANES))
    b = jnp.broadcast_to(table_b[0, 0:1, :], (ROWS, LANES))
    for tile in range(KEYS // LANES):
        span = slice(tile * LANES, (tile + 1) * LANES)

        def look(table, codes):
            return jnp.take_along_axis(table, codes, axis=1, mode="promise_in_bounds")

        out[0, :, span] = (
            look(a, near_s[:, span]) + look(a, across_s[:, span]) + look(b, down_s[:, span])
        )


def make_bias(facts, own_boxes, other_boxes, bias_table):
    columns = bias_table.T
    table_a = jnp.pad(columns[:, : POS_BINS + BOX_BINS], ((0, 0), (0, LANES - POS_BINS - BOX_BINS)))
    table_b = jnp.pad(
        columns[:, POS_BINS + BOX_BINS :],
        ((0, 0), (0, LANES - BOX_BINS)),
        constant_values=NEVER,
    )
    spread = lambda t: jnp.broadcast_to(t[:, None, :], (HEADS, 8, LANES))
    whole = lambda h, facts: (0, 0)
    return pl.pallas_call(
        bias_kernel,
        out_shape=jax.ShapeDtypeStruct((HEADS, ROWS, KEYS), f32),
        grid_spec=pltpu.PrefetchScalarGridSpec(
            num_scalar_prefetch=1,
            grid=(HEADS,),
            in_specs=[
                pl.BlockSpec((2, HALF_TEXT), whole),
                pl.BlockSpec((2, HALF_TEXT), whole),
                pl.BlockSpec((1, 8, LANES), lambda h, facts: (h, 0, 0)),
                pl.BlockSpec((1, 8, LANES), lambda h, facts: (h, 0, 0)),
            ],
            out_specs=pl.BlockSpec((1, ROWS, KEYS), lambda h, facts: (h, 0, 0)),
            scratch_shapes=[pltpu.VMEM((ROWS, KEYS), jnp.int32)] * 3,
        ),
        compiler_params=pltpu.CompilerParams(vmem_limit_bytes=50 * MIB),
        cost_estimate=brief,
        name="score_bias",
    )(facts, own_boxes, other_boxes, spread(table_a), spread(table_b))


def pairs_kernel(facts, own_boxes, other_boxes, right, left, masks):
    keys, queries = page_places(facts[0], facts[1], own_boxes[...], other_boxes[...])
    place, x, y = as_columns(queries)
    diff = keys[0] - place
    for index, holds in enumerate(
        (
            (diff >= -16) & (diff <= 15),
            (keys[1] & 15) < (x & 15),
            (keys[2] & 15) < (y & 15),
            diff > 15,
        )
    ):
        masks[index] = jnp.where(holds, 1.0, 0.0).astype(bf16)
    row = lax.broadcasted_iota(jnp.int32, (64, KEYS), 0)
    key_hot = [
        jnp.where((63 - row) == (code & 63), 1.0, 0.0)
        for code in (keys[1] >> 4, keys[2] >> 4, keys[0])
    ]
    key_hot.append(jnp.zeros((64, KEYS), f32))
    right[...] = jnp.transpose(jnp.concatenate(key_hot, axis=0), (1, 0)).astype(bf16)
    row = lax.broadcasted_iota(jnp.int32, (64, 384), 0)
    query_hot = [
        jnp.where(row == queries[1] >> 4, 1.0, 0.0),
        jnp.where(row == queries[2] >> 4, 1.0, 0.0),
        jnp.where(row[:32] + 64 == queries[2] >> 4, 1.0, 0.0),
        jnp.where(row == (queries[0] & 63), 1.0, 0.0),
    ]
    left[...] = jnp.concatenate(query_hot, axis=0)[:, :ROWS].astype(bf16)


def page_pairs(facts, own_boxes, other_boxes):
    vmem = pl.BlockSpec(memory_space=pltpu.VMEM)
    return pl.pallas_call(
        pairs_kernel,
        in_specs=[pl.BlockSpec(memory_space=pltpu.SMEM), vmem, vmem],
        out_specs=[vmem] * 3,
        out_shape=[
            jax.ShapeDtypeStruct((KEYS, 256), bf16),
            jax.ShapeDtypeStruct((224, ROWS), bf16),
            jax.ShapeDtypeStruct((4, ROWS, KEYS), bf16),
        ],
        compiler_params=pltpu.CompilerParams(vmem_limit_bytes=24 * MIB),
        cost_estimate=brief,
        name="page_pairs",
    )(facts, own_boxes, other_boxes)


def table_kernel(right, left, masks, ds_a, ds_b, *rest):
    out = rest[-1]
    total = (ds_a[0].astype(f32) + ds_b[0].astype(f32)).astype(bf16)
    hot = right[...]
    query_hot = left[...]

    def fold(values, columns, rows):
        inner = jnp.dot(values, hot[:, columns], preferred_element_type=f32).astype(bf16)
        return jnp.dot(query_hot[rows], inner, preferred_element_type=f32)

    plain = fold(total, slice(0, 128), slice(0, 160))
    near = fold(total * masks[0], slice(128, 256), slice(160, 224))
    by_x = fold(total * masks[1], slice(0, 128), slice(0, 64))
    by_y = fold(total * masks[2], slice(0, 128), slice(64, 160))

    def diagonals(square):
        lane = lax.broadcasted_iota(jnp.int32, square.shape, 1)
        square = jnp.where(lane < 64, square, 0.0)
        turned = pltpu.roll(square, 0, axis=1, stride=1, stride_axis=0)
        return jnp.sum(turned, axis=0, keepdims=True)

    def second(square):
        return pltpu.roll(square, 64, axis=1)

    above = jnp.sum((total * masks[3]).astype(f32), axis=0, keepdims=True)
    above = sum(above[:, t * LANES : (t + 1) * LANES] for t in range(KEYS // LANES))
    out[0] = jnp.concatenate(
        [
            diagonals(plain[:64]),
            diagonals(by_x),
            diagonals(second(plain[64:128])),
            diagonals(second(by_y[:64])),
            diagonals(near),
            above,
            diagonals(second(plain[128:])),
            diagonals(second(by_y[64:])),
        ],
        axis=0,
    )


def table_bins():
    bins = np.zeros((8, LANES, BUCKETS), np.float32)
    for c in range(127):
        diff = 63 - c
        for kind, base in ((0, POS_BINS), (1, POS_BINS + BOX_BINS)):
            here = base + 32 + min(max(diff, -32), 31)
            below = base + 32 + min(max(diff - 1, -32), 31)
            bins[2 * kind, c, here] += 1
            bins[2 * kind + 1, c, below] += 1
            bins[2 * kind + 1, c, here] -= 1
        far = -1 - c
        bins[6, c, 128 + max(far, -32)] += 1
        bins[7, c, 128 + max(far - 1, -32)] += 1
        bins[7, c, 128 + max(far, -32)] -= 1
        near = (diff + 32) % 64 - 32
        if -16 <= near <= 15:
            bins[4, c, near + 16] += 1
        bins[0, c, 0] += 1
        bins[4, c, 0] -= 1
    bins[5, :, 31] += 1
    bins[5, :, 0] -= 1
    return bins


def fold_table(pairs, ds_a, ds_b, part, parts, after=()):
    count = HEADS // parts
    head = pl.BlockSpec((1, ROWS, KEYS), lambda h: (h + part * count, 0, 0))
    return pl.pallas_call(
        table_kernel,
        out_shape=jax.ShapeDtypeStruct((count, 8, LANES), f32),
        grid=(count,),
        in_specs=[full(array) for array in pairs]
        + [head, head]
        + [pl.BlockSpec(memory_space=pl.ANY)] * len(after),
        out_specs=pl.BlockSpec((1, 8, LANES), lambda h: (h, 0, 0)),
        compiler_params=pltpu.CompilerParams(vmem_limit_bytes=58 * MIB),
        cost_estimate=brief,
        name="table_grad",
    )(*pairs, ds_a, ds_b, *after)


def visual_kernel(half, grad_ref, normal_low, hat, weight, keep, send, normal_grad, sums):
    rows = normal_low.shape[0]
    column = lambda block: jnp.sum(block, axis=0, keepdims=True)
    token_grad = grad_ref[...].astype(bf16)
    whole = tn_dot(normal_low[...], token_grad)
    mid = whole.shape[0] // 2
    first = half[0] == 0
    keep[...] = jnp.where(first, whole[:mid], whole[mid:]).astype(bf16)
    send[...] = jnp.where(first, whole[mid:], whole[:mid]).astype(bf16)
    place = half[0] * rows + lax.broadcasted_iota(jnp.int32, (rows, 1), 0)
    grad = jnp.where(place < VIS_TOK, nt_dot(token_grad, weight[...]), 0.0)
    normal_grad[...] = grad
    total = column(token_grad.astype(f32))
    put_row(sums, 0, total)
    at = total.shape[1] // LANES
    count = grad.shape[1] // LANES
    put_row(sums.at[at : at + count], 0, column(grad * hat[...]))
    put_row(sums.at[at + count : at + 2 * count], 0, column(grad))


def visual_back(half, gradient, normal_low, hat, weight):
    slots, channels = normal_low.shape
    width = weight.shape[1]
    return pl.pallas_call(
        visual_kernel,
        grid_spec=pltpu.PrefetchScalarGridSpec(
            num_scalar_prefetch=1,
            grid=(1,),
            in_specs=[
                pl.BlockSpec(
                    (slots, width), lambda i, half: (gradient.shape[0] // slots - 1, 0)
                ),
                full(normal_low),
                full(hat),
                full(weight),
            ],
            out_specs=[
                pl.BlockSpec((channels // 2, width), lambda i, half: (0, 0)),
                pl.BlockSpec((channels // 2, width), lambda i, half: (0, 0)),
                pl.BlockSpec((slots, channels), lambda i, half: (0, 0)),
                pl.BlockSpec(((width + 2 * channels) // LANES, LANES), lambda i, half: (0, 0)),
            ],
        ),
        out_shape=[
            jax.ShapeDtypeStruct((channels // 2, width), bf16),
            jax.ShapeDtypeStruct((channels // 2, width), bf16),
            jax.ShapeDtypeStruct((slots, channels), f32),
            jax.ShapeDtypeStruct(((width + 2 * channels) // LANES, LANES), f32),
        ],
        cost_estimate=brief,
        name="visual_back",
    )(half, gradient, normal_low, hat, weight)


def join_kernel(*refs):
    out = refs[-1]
    out[...] = jnp.zeros_like(out)
    at = 0
    for ref in refs[:-1]:
        values = ref[...]
        if len(values.shape) == 3 and values.shape[1] > 1:
            for head in range(values.shape[0]):
                out[at : at + values.shape[1], :] = values[head]
                at += values.shape[1]
        elif len(values.shape) == 3:
            for group in range(values.shape[0]):
                for start in range(0, values.shape[2], LANES):
                    size = min(LANES, values.shape[2] - start)
                    out[at : at + 1, :size] = ref[group, :, start : start + size]
                    at += 1
        else:
            out[at : at + values.shape[0], :] = values
            at += values.shape[0]


def bin_rows(units):
    return -(-units // LANES)


def join(parts):
    rows = 0
    for part in parts:
        if part.ndim == 3 and part.shape[1] == 1:
            rows += part.shape[0] * bin_rows(part.shape[2])
        else:
            rows += part.size // LANES
    vmem = pl.BlockSpec(memory_space=pltpu.VMEM)
    return pl.pallas_call(
        join_kernel,
        out_shape=jax.ShapeDtypeStruct((rows, LANES), f32),
        in_specs=[vmem] * len(parts),
        out_specs=vmem,
        cost_estimate=brief,
        name="join",
    )(*parts)


def split_kernel(
    sizes,
    count,
    me,
    left,
    right,
    bins,
    normal_grad,
    hat,
    inverse_std,
    bn_gain,
    attn,
    out_bias,
    gain,
    shift,
    table,
    vis_bias,
    gain_grad,
    shift_grad,
    hidden_bias,
    maps,
    total,
):
    total[...] = left[...] + right[...]
    units = hidden_bias.shape[1]
    width = out_bias.shape[1]
    channels = gain_grad.shape[1]
    starts = [0]
    for size in sizes:
        starts.append(starts[-1] + size)

    def take(start, index, wide):
        per = wide // LANES
        begin = start + index * per
        return jnp.concatenate([total[begin + i : begin + i + 1, :] for i in range(per)], axis=1)

    for layer in range(LAYERS):
        norm = functools.partial(take, starts[layer])
        gain[layer, 1:2, :] = norm(0, width)
        shift[layer, 1:2, :] = norm(1, width)
        out_bias[layer : layer + 1, :] = norm(2, width)
        gain[layer, 0:1, :] = norm(3, width)
        shift[layer, 0:1, :] = norm(4, width)
        attn[2, layer : layer + 1, :] = norm(5, width)
        rows = functools.partial(take, starts[LAYERS + layer])
        attn[0, layer : layer + 1, :] = rows(0, width)
        attn[1, layer : layer + 1, :] = rows(1, width)
        per = bin_rows(units)
        begin = starts[2 * LAYERS + layer] + me[0] * per
        for part in range(per):
            span = min(LANES, units - part * LANES)
            hidden_bias[layer : layer + 1, part * LANES : part * LANES + span] = total[
                pl.ds(begin + part, 1), :span
            ]
    at = starts[3 * LAYERS]
    vis_bias[...] = total[at : at + width // LANES, :]
    at += width // LANES
    by_gain = take(at, 0, channels)
    by_shift = take(at, 1, channels)
    gain_grad[...] = by_gain
    shift_grad[...] = by_shift
    scale = inverse_std[...] * bn_gain[...]
    slots = normal_grad.shape[0]
    place = (me[0] & 1) * slots + lax.broadcasted_iota(jnp.int32, (slots, 1), 0)
    maps[...] = jnp.where(
        place < VIS_TOK,
        scale * (normal_grad[...] - by_shift / count - hat[...] * (by_gain / count)),
        0.0,
    )
    at = starts[3 * LAYERS + 1]
    folded = jnp.zeros((16, BUCKETS), f32)
    for kind in range(8):
        rows = jnp.concatenate(
            [total[at + 8 * head + kind : at + 8 * head + kind + 1, :] for head in range(HEADS)]
            + [jnp.zeros((16 - HEADS, LANES), f32)],
            axis=0,
        )
        high = rows.astype(bf16)
        middle = (rows - high.astype(f32)).astype(bf16)
        low = (rows - high.astype(f32) - middle.astype(f32)).astype(bf16)
        for part in (high, middle, low):
            folded = folded + nt_dot(part, bins[kind])
    table[...] = folded[:HEADS]


def split(me, left, right, sizes, count, normal_grad, hat, inverse_std, bn_gain, units, width):
    slots, channels = normal_grad.shape
    bins = jnp.asarray(table_bins().transpose(0, 2, 1), bf16)
    row = lambda value: value.reshape(1, -1)
    vmem = pl.BlockSpec(memory_space=pltpu.VMEM)
    shape = lambda *size: jax.ShapeDtypeStruct(size, f32)
    return pl.pallas_call(
        functools.partial(split_kernel, sizes, count),
        in_specs=[pl.BlockSpec(memory_space=pltpu.SMEM)] + [vmem] * 7,
        out_specs=[vmem] * 10,
        out_shape=[
            shape(3, LAYERS, width),
            shape(LAYERS, width),
            shape(LAYERS, 2, width),
            shape(LAYERS, 2, width),
            shape(HEADS, BUCKETS),
            shape(width // LANES, LANES),
            shape(1, channels),
            shape(1, channels),
            shape(LAYERS, units),
            shape(slots, channels),
        ],
        scratch_shapes=[pltpu.VMEM(left.shape, f32)],
        cost_estimate=brief,
        name="split",
    )(me, left, right, bins, normal_grad, hat, row(inverse_std), row(bn_gain))


def whole_page(own, other):
    return jnp.concatenate(
        [
            own[:HALF_TEXT],
            other[:HALF_TEXT],
            own[HALF_TEXT:],
            other[HALF_TEXT:],
            jnp.zeros((KEYS - 2 * ROWS, own.shape[1]), own.dtype),
        ],
        axis=0,
    )


def page_split(both):
    mid = 2 * HALF_TEXT
    own = jnp.concatenate([both[:HALF_TEXT], both[mid : mid + HALF_SLOTS]], axis=0)
    other = jnp.concatenate(
        [both[HALF_TEXT:mid], both[mid + HALF_SLOTS : mid + VIS_SLOTS]], axis=0
    )
    return own, other


def nt_dot(left, right):
    return lax.dot_general(left, right, (((1,), (1,)), ((), ())), preferred_element_type=f32)


def tn_dot(left, right):
    return lax.dot_general(left, right, (((0,), (0,)), ((), ())), preferred_element_type=f32)


def put_row(target, index, row):
    count = row.shape[1] // LANES
    for part in range(count):
        at = index * count + part
        target[at : at + 1, :] = row[:, part * LANES : (part + 1) * LANES]


def centred(values):
    center = values - jnp.mean(values, axis=1, keepdims=True)
    spread = jnp.mean(center * center, axis=1, keepdims=True)
    rate = lax.rsqrt(spread + norm_epsilon)
    return center * rate, rate


def norm_back(grad, values, gain_row):
    hat, rate = centred(values)
    scaled = grad * gain_row
    mean = jnp.mean(scaled, axis=1, keepdims=True)
    along = jnp.mean(scaled * hat, axis=1, keepdims=True)
    column = lambda block: jnp.sum(block, axis=0, keepdims=True)
    return rate * (scaled - mean - hat * along), column(grad * hat), column(grad)


def attend_kernel(
    layer,
    q_ref,
    ko,
    kp,
    vo,
    vp,
    bias,
    x_ref,
    weight,
    attn_bias,
    gain,
    shift,
    soft,
    pair,
    residual,
    normed,
):
    step = pl.program_id(0)
    q = q_ref[...] * jnp.asarray(HEAD_DIM**-0.5, bf16)
    keys = whole_page(ko[...], kp[...])
    values = whole_page(vo[...], vp[...])
    first = lax.broadcasted_iota(jnp.int32, (ROWS, LANES), 1) < HEAD_DIM
    parts = []
    for head in range(2):
        mine = jnp.where(first if head == 0 else ~first, q, jnp.zeros_like(q))
        scores = nt_dot(mine, keys) + bias[head]
        raised = jnp.exp(scores - jnp.max(scores, axis=1, keepdims=True))
        weights = (raised * (1.0 / jnp.sum(raised, axis=1, keepdims=True))).astype(bf16)
        soft[head] = weights
        parts.append(jnp.dot(weights, values, preferred_element_type=f32))
    slab = pl.ds(pl.multiple_of(step * LANES, LANES), LANES)
    pair[0, :, slab] = jnp.where(first, parts[0], parts[1]).astype(bf16)

    @pl.when(step == PAIRS - 1)
    def _():
        attended = jnp.dot(pair[0], weight[0], preferred_element_type=f32)
        summed = x_ref[...] + (attended + attn_bias[layer, 2:3, :])
        residual[...] = summed
        out = centred(summed)[0] * gain[layer, 0:1, :] + shift[layer, 0:1, :]
        normed[...] = out
        pair[1] = out.astype(bf16)


def full(array):
    return pl.BlockSpec(array.shape, lambda *at: (0,) * array.ndim)


def attend(layer, q, kv, other_kv, bias, x, out_weight, attn_bias, gain, shift):
    rows, width = q.shape
    slab = pl.BlockSpec((ROWS, LANES), lambda p: (0, p))
    second = pl.BlockSpec((ROWS, LANES), lambda p: (0, p + PAIRS))
    heads = pl.BlockSpec((2, ROWS, KEYS), lambda p: (p, 0, 0))
    whole = pl.BlockSpec((rows, width), lambda p: (0, 0))
    wide = jax.ShapeDtypeStruct((rows, width), f32)
    low = jax.ShapeDtypeStruct((2, rows, width), bf16)
    return pl.pallas_call(
        functools.partial(attend_kernel, layer),
        grid=(PAIRS,),
        in_specs=[
            slab,
            slab,
            slab,
            second,
            second,
            heads,
            whole,
            pl.BlockSpec((1, width, width), lambda p: (layer, 0, 0)),
            full(attn_bias),
            full(gain),
            full(shift),
        ],
        out_specs=[
            heads,
            pl.BlockSpec((2, rows, width), lambda p: (0, 0, 0)),
            whole,
            whole,
        ],
        out_shape=[jax.ShapeDtypeStruct((HEADS, ROWS, KEYS), bf16), low, wide, wide],
        compiler_params=pltpu.CompilerParams(vmem_limit_bytes=50 * MIB),
        cost_estimate=brief,
        name="attend",
    )(q, kv, other_kv, kv, other_kv, bias, x, out_weight, attn_bias, gain, shift)


def attend_back_kernel(q_ref, ko, kp, vo, vp, dc_ref, soft, *rest):
    ds, *grads = rest[-6:]
    scale = HEAD_DIM**-0.5
    q = q_ref[...]
    dc = dc_ref[...]
    keys = whole_page(ko[...], kp[...])
    values = whole_page(vo[...], vp[...])
    first = lax.broadcasted_iota(jnp.int32, (ROWS, LANES), 1) < HEAD_DIM
    q_turned = jnp.transpose(q.astype(f32), (1, 0)).astype(bf16)
    dc_turned = jnp.transpose(dc.astype(f32), (1, 0)).astype(bf16)
    dq_parts, dk_parts, dv_parts = [], [], []
    for head in range(2):
        span = slice(head * HEAD_DIM, (head + 1) * HEAD_DIM)
        mine = jnp.where(first if head == 0 else ~first, dc, jnp.zeros_like(dc))
        weights = soft[head]
        weights_f = weights.astype(f32)
        flow = nt_dot(mine, values)
        share = jnp.sum(weights_f * flow, axis=1, keepdims=True)
        score_grad = (weights_f * (flow - share)).astype(bf16)
        ds[head] = score_grad
        dq_parts.append(jnp.dot(score_grad, keys, preferred_element_type=f32))
        dk_parts.append(jnp.dot(q_turned[span], score_grad, preferred_element_type=f32))
        dv_parts.append(jnp.dot(dc_turned[span], weights, preferred_element_type=f32))
    grads[0][...] = (jnp.where(first, dq_parts[0], dq_parts[1]) * scale).astype(bf16)
    own, other = page_split(jnp.transpose(jnp.concatenate(dk_parts, axis=0) * scale, (1, 0)))
    grads[1][...] = own.astype(bf16)
    grads[2][...] = other.astype(bf16)
    own, other = page_split(jnp.transpose(jnp.concatenate(dv_parts, axis=0), (1, 0)))
    grads[3][...] = own.astype(bf16)
    grads[4][...] = other.astype(bf16)


def attend_back(q, kv, other_kv, dctx, soft, after=()):
    slab = pl.BlockSpec((ROWS, LANES), lambda p: (0, p))
    second = pl.BlockSpec((ROWS, LANES), lambda p: (0, p + PAIRS))
    heads = pl.BlockSpec((2, ROWS, KEYS), lambda p: (p, 0, 0))
    return pl.pallas_call(
        attend_back_kernel,
        grid=(PAIRS,),
        in_specs=[slab, slab, slab, second, second, slab, heads]
        + [pl.BlockSpec(memory_space=pl.ANY)] * len(after),
        out_specs=[heads] + [slab] * 5,
        out_shape=[
            jax.ShapeDtypeStruct((HEADS, ROWS, KEYS), bf16),
        ]
        + [jax.ShapeDtypeStruct(q.shape, bf16)] * 5,
        compiler_params=pltpu.CompilerParams(vmem_limit_bytes=50 * MIB),
        cost_estimate=brief,
        name="attend_back",
    )(q, kv, other_kv, kv, other_kv, dctx, soft, *after)


def ffn_kernel(layer, more, me, x_ref, *refs):
    step = pl.program_id(0)
    width = x_ref.shape[1]
    blocks, (bias, n_ref, out_bias, gain, shift), rest = refs[:BLOCKS], refs[BLOCKS:][:5], refs[BLOCKS + 5 :]
    units = blocks[0].shape[1]
    own_act, mate_act, slope, residual = rest[-7 if more else -5 :][:4]
    x = x_ref[...]

    total = None
    for index, block in enumerate(blocks):
        weights = block[0]
        row = bias[pl.ds(me[0] ^ (BLOCKS * step + index), 1), layer, :units]
        hidden = nt_dot(x, weights[:, :width]) + row.astype(f32)
        half_cdf = 0.5 + 0.5 * lax.erf(hidden * 0.5**0.5)
        low = (hidden * half_cdf).astype(bf16)
        (mate_act if index % 2 else own_act)[index // 2] = low
        density = jnp.exp(hidden * hidden * -0.5) * (1.0 / (2.0 * np.pi) ** 0.5)
        slope[index] = (half_cdf + hidden * density).astype(bf16)
        term = jnp.dot(low, weights[:, width:], preferred_element_type=f32)
        total = term if total is None else total + term

    @pl.when(step == 0)
    def _():
        residual[...] = n_ref[...] + out_bias[layer : layer + 1, :] + total

    @pl.when(step > 0)
    def _():
        residual[...] += total

    @pl.when(step == pl.num_programs(0) - 1)
    def _():
        states = centred(residual[...])[0] * gain[layer, 1:2, :] + shift[layer, 1:2, :]
        rounded = states.astype(bf16)
        if more:
            weight, attn_bias = rest[:2]
            wide, query, shared = rest[-3:]
            wide[...] = states
            project = lambda index: jnp.dot(
                rounded, weight[0, index], preferred_element_type=f32
            )
            query[...] = (project(0) + attn_bias[layer + 1, 0:1, :]).astype(bf16)
            shared[:, :width] = project(1).astype(bf16)
            shared[:, width : 2 * width] = (
                project(2) + attn_bias[layer + 1, 1:2, :]
            ).astype(bf16)
            shared[:, 2 * width :] = rounded
        else:
            rest[-1][...] = rounded


def weight_blocks(layer, units, width):
    pick = lambda which: pl.BlockSpec(
        (1, units, 2 * width), lambda i, me: (me[0] ^ (BLOCKS * i + which), layer, 0)
    )
    return [pick(which) for which in range(BLOCKS)]


def ffn(me, layer, pair, n, gathered, units, out_bias, gain, shift, qkv_weight, attn_bias):
    groups = gathered.shape[0]
    rows, width = n.shape
    more = layer < LAYERS - 1
    whole = pl.BlockSpec((rows, width), lambda i, me: (0, 0))
    kept = pl.BlockSpec((BLOCKS, rows, units), lambda i, me: (i, 0, 0))
    kept_shape = jax.ShapeDtypeStruct((groups, rows, units), bf16)
    wide = jax.ShapeDtypeStruct((rows, width), f32)
    low = jax.ShapeDtypeStruct((rows, width), bf16)
    half_act = pl.BlockSpec((HALF, rows, units), lambda i, me: (i, 0, 0))
    half_shape = jax.ShapeDtypeStruct((groups // 2, rows, units), bf16)
    inputs = [pair] + [gathered] * (BLOCKS + 1) + [n, out_bias, gain, shift]
    in_specs = [
        pl.BlockSpec((None, rows, width), lambda i, me: (1, 0, 0)),
        *weight_blocks(layer, units, width),
        pl.BlockSpec(
            (groups, 16, 2 * width), lambda i, me: (0, LAYERS * units // 16, 0)
        ),
        whole,
        full(out_bias),
        full(gain),
        full(shift),
    ]
    out_specs = [half_act, half_act, kept, whole]
    out_shape = [half_shape, half_shape, kept_shape, wide]
    if more:
        inputs += [qkv_weight, attn_bias]
        in_specs += [
            pl.BlockSpec((1, 3, width, width), lambda i, me: (layer + 1, 0, 0, 0)),
            full(attn_bias),
        ]
        out_specs += [whole, whole, pl.BlockSpec((rows, 3 * width), lambda i, me: (0, 0))]
        out_shape += [wide, low, jax.ShapeDtypeStruct((rows, 3 * width), bf16)]
    else:
        out_specs += [whole]
        out_shape += [low]
    return pl.pallas_call(
        functools.partial(ffn_kernel, layer, more),
        out_shape=out_shape,
        grid_spec=pltpu.PrefetchScalarGridSpec(
            num_scalar_prefetch=1, grid=(groups // BLOCKS,), in_specs=in_specs, out_specs=out_specs
        ),
        compiler_params=pltpu.CompilerParams(vmem_limit_bytes=50 * MIB),
        cost_estimate=brief,
        name="feed_forward",
    )(me, *inputs)


def ffn_back_kernel(layer, me, grad_ref, r2_ref, r1_ref, *refs):
    blocks, (slope, gain, out_weight), rest = refs[:BLOCKS], refs[BLOCKS:][:3], refs[BLOCKS + 3 :]
    own_dh, mate_dh, low_grads, bias_grad, sums, dx, dctx, total_s = rest
    step = pl.program_id(0)
    width = r2_ref.shape[1]
    column = lambda block: jnp.sum(block, axis=0, keepdims=True)

    @pl.when(step == 0)
    def _():
        grad, gain_grad, shift_grad = norm_back(
            grad_ref[...].astype(f32), r2_ref[...], gain[layer, 1:2, :]
        )
        low = grad.astype(bf16)
        total_s[...] = grad
        low_grads[0] = low
        put_row(sums, 0, gain_grad)
        put_row(sums, 1, shift_grad)
        put_row(sums, 2, column(low.astype(f32)))

    dy = low_grads[0]
    total = None
    for index, block in enumerate(blocks):
        weights = block[0]
        flow = nt_dot(dy, weights[:, width:])
        grad = (flow * slope[index].astype(f32)).astype(bf16)
        (mate_dh if index % 2 else own_dh)[index // 2] = grad
        bias_grad[index ^ (me[0] & (BLOCKS - 1))] = column(grad.astype(f32))
        term = jnp.dot(grad, weights[:, :width], preferred_element_type=f32)
        total = term if total is None else total + term
    total_s[...] += total

    @pl.when(step == pl.num_programs(0) - 1)
    def _():
        grad, gain_grad, shift_grad = norm_back(total_s[...], r1_ref[...], gain[layer, 0:1, :])
        low = grad.astype(bf16)
        dx[...] = grad
        low_grads[1] = low
        dctx[...] = nt_dot(low, out_weight[0]).astype(bf16)
        put_row(sums, 3, gain_grad)
        put_row(sums, 4, shift_grad)
        put_row(sums, 5, column(low.astype(f32)))


def ffn_back(me, layer, grad, r2, r1, gathered, slope, gain, out_weight):
    groups, rows, units = slope.shape
    width = r2.shape[1]
    whole = pl.BlockSpec((rows, width), lambda i, me: (0, 0))
    half = pl.BlockSpec((HALF, rows, units), lambda i, me: (i, 0, 0))
    half_shape = jax.ShapeDtypeStruct((groups // 2, rows, units), bf16)
    return pl.pallas_call(
        functools.partial(ffn_back_kernel, layer),
        out_shape=[
            half_shape,
            half_shape,
            jax.ShapeDtypeStruct((2, rows, width), bf16),
            jax.ShapeDtypeStruct((groups, 1, units), f32),
            jax.ShapeDtypeStruct((6 * width // LANES, LANES), f32),
            jax.ShapeDtypeStruct((rows, width), f32),
            jax.ShapeDtypeStruct((rows, width), bf16),
        ],
        grid_spec=pltpu.PrefetchScalarGridSpec(
            num_scalar_prefetch=1,
            grid=(groups // BLOCKS,),
            in_specs=[
                whole,
                whole,
                whole,
                *weight_blocks(layer, units, width),
                pl.BlockSpec((BLOCKS, rows, units), lambda i, me: (i, 0, 0)),
                full(gain),
                pl.BlockSpec((1, width, width), lambda i, me: (layer, 0, 0)),
            ],
            out_specs=[
                half,
                half,
                pl.BlockSpec((2, rows, width), lambda i, me: (0, 0, 0)),
                pl.BlockSpec((BLOCKS, 1, units), lambda i, me: (me[0] // BLOCKS ^ i, 0, 0)),
                pl.BlockSpec((6 * width // LANES, LANES), lambda i, me: (0, 0)),
                whole,
                whole,
            ],
            scratch_shapes=[pltpu.VMEM((rows, width), f32)],
        ),
        compiler_params=pltpu.CompilerParams(vmem_limit_bytes=50 * MIB),
        cost_estimate=brief,
        name="feed_forward_back",
    )(me, grad, r2, r1, *[gathered] * BLOCKS, slope, gain, out_weight)


def ffn_grads_kernel(me, n, n_mate, dy, dy_mate, dh, dh_mate, act, act_mate, *rest):
    near_keep, near_send, seq_keep, seq_send, n_s, dy_s = rest[-6:]
    rows, width = n.shape
    step = pl.program_id(0)
    near = step < pl.num_programs(0) // 2

    @pl.when(step == 0)
    def _():
        for target, own, mate in ((n_s, n, n_mate), (dy_s, dy, dy_mate)):
            target[:rows] = own[...]
            target[rows:] = mate[...]

    both = lambda own, mate: jnp.concatenate([own[0], mate[0]], axis=0)
    into = tn_dot(both(dh, dh_mate), n_s[...]).astype(bf16)

    @pl.when(near)
    def _():
        near_keep[0] = into

    @pl.when(jnp.logical_not(near))
    def _():
        near_send[0] = into

    out = tn_dot(both(act, act_mate), dy_s[...]).astype(bf16)
    turn = me[1] % 2 == 0
    seq_keep[0] = jnp.where(turn, out[:, : width // 2], out[:, width // 2 :])
    seq_send[0] = jnp.where(turn, out[:, width // 2 :], out[:, : width // 2])


def ffn_grads(me, pair, pair_mate, low_grads, low_grads_mate, dh, dh_mate, act, act_mate):
    groups, rows, units = dh.shape
    width = pair.shape[2]
    far = groups // 2
    row_block = lambda which: pl.BlockSpec((None, rows, width), lambda i, me: (which, 0, 0))
    hidden = pl.BlockSpec((1, rows, units), lambda i, me: ((i % far) * 2 + i // far, 0, 0))
    place = lambda i, me: (me[0] >> 2) ^ i
    near_shape = jax.ShapeDtypeStruct((far, units, width), bf16)
    seq_shape = jax.ShapeDtypeStruct((groups, units, width // 2), bf16)
    seq_block = pl.BlockSpec(
        (1, units, width // 2), lambda i, me: (i // far * far + place(i % far, me), 0, 0)
    )
    return pl.pallas_call(
        ffn_grads_kernel,
        out_shape=[near_shape, near_shape, seq_shape, seq_shape],
        grid_spec=pltpu.PrefetchScalarGridSpec(
            num_scalar_prefetch=1,
            grid=(groups,),
            in_specs=[row_block(1), row_block(1), row_block(0), row_block(0)] + [hidden] * 4,
            out_specs=[
                pl.BlockSpec(
                    (1, units, width), lambda i, me: (place(jnp.minimum(i, far - 1), me), 0, 0)
                ),
                pl.BlockSpec(
                    (1, units, width), lambda i, me: (place(jnp.maximum(i - far, 0), me), 0, 0)
                ),
                seq_block,
                seq_block,
            ],
            scratch_shapes=[pltpu.VMEM((2 * rows, width), bf16)] * 2,
        ),
        compiler_params=pltpu.CompilerParams(vmem_limit_bytes=50 * MIB),
        cost_estimate=brief,
        name="feed_forward_grads",
    )(me, pair, pair_mate, low_grads, low_grads_mate, dh, dh_mate, act, act_mate)


def projection_kernel(by_distance, me, x, x_mate, ctx, ctx_mate, *refs):
    own, mate, refs = refs[:5], refs[5:10], refs[10:]
    da, da_mate, dr_ref, weight = refs[:4]
    near_keep, near_send, seq_keep, seq_send, dx, sums, turned_s, left_s, right_s, shards_s = refs[-10:]
    step = pl.program_id(0)
    far, shard = near_keep.shape[:2]
    rows, width = x.shape
    column = lambda block: jnp.sum(block.astype(f32), axis=0, keepdims=True)

    def place_of(place, near):
        far_place = (me[0] >> 2) ^ place if by_distance else place
        return far_place * 4 + ((me[0] & 3) ^ (2 * near))

    def pick_left(first, second):
        for index, block in enumerate((first, second)):
            turned_s[...] = jnp.transpose(block[...].astype(f32), (1, 0))
            for near in range(2):
                for place in range(far):
                    start = pl.multiple_of(place_of(place, near) * shard, 8)
                    at = (near * far + place) * shard
                    left_s[index, at : at + shard, :] = turned_s[pl.ds(start, shard), :]

    @pl.when(step == 0)
    def _():
        dx[...] = dr_ref[...]
        pick_left(x, x_mate)
        right_s[0] = own[0][...]
        right_s[1] = mate[0][...]
        put_row(sums, 0, column(own[0][...]))

    for index in (1, 2):

        @pl.when(step == index)
        def _():
            right_s[0] = add_low(own[2 * index - 1][...], mate[2 * index][...])
            right_s[1] = add_low(mate[2 * index - 1][...], own[2 * index][...])

    @pl.when(step == 2)
    def _():
        put_row(sums, 1, column(right_s[0]))

    @pl.when(step < 3)
    def _():
        dx[...] += nt_dot(right_s[0], weight[0, 0])

    @pl.when(step == 3)
    def _():
        pick_left(ctx, ctx_mate)
        right_s[0] = da[...]
        right_s[1] = da_mate[...]

    shards_s[...] = sum(
        jnp.dot(left_s[index].astype(bf16), right_s[index], preferred_element_type=f32)
        for index in range(2)
    )

    def put(target, first, near, columns):
        for place in range(far):
            at = (near * far + place) * shard
            target[first + place, :, columns] = shards_s[at : at + shard, :].astype(bf16)

    for index in range(2):

        @pl.when(step == index)
        def _():
            columns = slice(index * width, (index + 1) * width)
            put(near_keep, 0, 0, columns)
            put(near_send, 0, 1, columns)

    def put_seq(target):
        put(target, 0, 0, slice(None))
        put(target, far, 1, slice(None))

    mine = step - 2 == me[1] % 2
    pl.when((step >= 2) & mine)(lambda: put_seq(seq_keep))
    pl.when((step >= 2) & jnp.logical_not(mine))(lambda: put_seq(seq_send))


def projection_grads(
    by_distance,
    me,
    layer,
    shared,
    shared_mate,
    pair,
    pair_mate,
    own,
    mate,
    low,
    low_mate,
    dr,
    weight,
    after=(),
):
    rows, width = dr.shape
    groups = lax.axis_size("tp")
    shard = width // groups
    whole = pl.BlockSpec((rows, width), lambda t, me: (0, 0))
    x_block = pl.BlockSpec((rows, width), lambda t, me: (0, 2))
    layered = lambda which: pl.BlockSpec((None, rows, width), lambda t, me: (which, 0, 0))
    near_shape = jax.ShapeDtypeStruct((groups // 4, shard, 2 * width), bf16)
    near_block = pl.BlockSpec(near_shape.shape, lambda t, me: (0, 0, 0))
    seq_shape = jax.ShapeDtypeStruct((groups // 2, shard, width), bf16)
    seq_block = pl.BlockSpec(seq_shape.shape, lambda t, me: (0, 0, 0))
    return pl.pallas_call(
        functools.partial(projection_kernel, by_distance),
        out_shape=[near_shape, near_shape, seq_shape, seq_shape]
        + [
            jax.ShapeDtypeStruct((rows, width), f32),
            jax.ShapeDtypeStruct((2 * width // LANES, LANES), f32),
        ],
        grid_spec=pltpu.PrefetchScalarGridSpec(
            num_scalar_prefetch=1,
            grid=(4,),
            in_specs=[
                x_block,
                x_block,
                layered(0),
                layered(0),
                *[whole] * 10,
                layered(1),
                layered(1),
                whole,
                pl.BlockSpec(
                    (1, 1, width, width), lambda t, me: (layer, jnp.minimum(t, 2), 0, 0)
                ),
            ]
            + [pl.BlockSpec(memory_space=pl.ANY)] * len(after),
            out_specs=[near_block, near_block, seq_block, seq_block]
            + [
                whole,
                pl.BlockSpec((2 * width // LANES, LANES), lambda t, me: (0, 0)),
            ],
            scratch_shapes=[
                pltpu.VMEM((width, rows), f32),
                pltpu.VMEM((2, width // 2, rows), f32),
                pltpu.VMEM((2, rows, width), bf16),
                pltpu.VMEM((width // 2, width), f32),
            ],
        ),
        compiler_params=pltpu.CompilerParams(vmem_limit_bytes=50 * MIB),
        cost_estimate=brief,
        name="projection_grads",
    )(
        me,
        shared,
        shared_mate,
        pair,
        pair_mate,
        *own,
        *mate,
        low,
        low_mate,
        dr,
        weight,
        *after,
    )


def ordered(turn, mine, other):
    return jnp.where(turn, mine, other), jnp.where(turn, other, mine)


def projection_out_kernel(me, *refs):
    qkv, out = refs[-2:]
    shard, width = out.shape[1:]
    for layer in range(LAYERS):
        mine, other = refs[2 * layer : 2 * layer + 2]
        first, second = ordered(me[1] % 2 == 0, mine[...], other[...])
        low, high = first[:shard].astype(f32), second[:shard].astype(f32)
        qkv[layer, 0] = low
        qkv[layer, 1] = high
        qkv[layer, 2] = first[shard:].astype(f32)
        out[layer] = second[shard:].astype(f32)


def ffn_out_kernel(me, *refs):
    into, out = refs[-2:]
    units, width = out.shape[1:]
    for layer in range(LAYERS):
        mine, other = refs[2 * layer : 2 * layer + 2]
        for index, part in enumerate(ordered(me[1] % 2 == 0, mine[...], other[...])):
            columns = slice(index * (width // 2), (index + 1) * (width // 2))
            into[layer, :, columns] = part[:units].astype(f32)
            out[layer, :, columns] = part[units:].astype(f32)


def write_out(kernel, name, me, parts, shapes):
    vmem = pl.BlockSpec(memory_space=pltpu.VMEM)
    return pl.pallas_call(
        kernel,
        in_specs=[pl.BlockSpec(memory_space=pltpu.SMEM)] + [vmem] * len(parts),
        out_specs=[vmem] * len(shapes),
        out_shape=[jax.ShapeDtypeStruct(shape, f32) for shape in shapes],
        compiler_params=pltpu.CompilerParams(vmem_limit_bytes=24 * MIB),
        cost_estimate=brief,
        name=name,
    )(me, *parts)


def body(
    text_states,
    visual_maps,
    text_boxes,
    text_lengths,
    qkv_weight,
    out_weight,
    attn_bias,
    ffn_in,
    ffn_in_bias,
    ffn_out,
    ffn_out_bias,
    norm_gain,
    norm_shift,
    bias_table,
    vis_weight,
    vis_bias,
    bn_gain,
    bn_shift,
    cotangent,
):
    tp_index = lax.axis_index("tp")
    tp_size = lax.axis_size("tp")
    half = tp_index % 2
    page = (lax.axis_index("seq") * tp_size + tp_index) // 2
    me = jnp.stack([tp_index, lax.axis_index("seq")]).astype(jnp.int32)
    units = ffn_in.shape[1]
    width = text_states.shape[1]
    text_rows = text_states.shape[0]

    bias_rows = jnp.pad(ffn_in_bias, ((0, 16 - LAYERS), (0, 2 * width - units)))
    packed = jnp.concatenate(
        [
            jnp.concatenate([ffn_in, ffn_out], axis=2).reshape(LAYERS * units, 2 * width),
            bias_rows,
        ],
        axis=0,
    )
    gathered = lax.all_gather(packed, "tp", axis=0)

    other_boxes = flipped(text_boxes, "tp", 0)
    length = lax.dynamic_index_in_dim(text_lengths, page, 0, keepdims=False)
    facts = jnp.stack([half.astype(jnp.int32), length])
    score_bias = make_bias(facts, text_boxes, other_boxes, bias_table)

    count_cells = text_lengths.shape[0] * VIS_TOK
    maps_float = visual_maps.astype(f32)
    slot_place = half * HALF_SLOTS + jnp.arange(HALF_SLOTS, dtype=jnp.int32)
    slot_mask = (slot_place < VIS_TOK)[:, None]
    masked_maps = jnp.where(slot_mask, maps_float, 0.0)
    sums = total_over_all(
        jnp.stack([jnp.sum(masked_maps, axis=0), jnp.sum(masked_maps * masked_maps, axis=0)])
    )
    channel_mean = sums[0] / count_cells
    inverse_std = lax.rsqrt(sums[1] / count_cells - channel_mean * channel_mean + norm_epsilon)
    centered_hat = jnp.where(slot_mask, (maps_float - channel_mean) * inverse_std, 0.0)
    normal_low = jnp.where(slot_mask, centered_hat * bn_gain + bn_shift, 0.0).astype(bf16)
    visual_tokens = jnp.dot(normal_low, vis_weight, preferred_element_type=f32) + vis_bias
    states = jnp.concatenate([text_states.astype(f32), visual_tokens], axis=0)

    rounded = states.astype(bf16)
    project = lambda index: jnp.dot(rounded, qkv_weight[0, index], preferred_element_type=f32)
    shared = jnp.concatenate(
        [project(1).astype(bf16), (project(2) + attn_bias[0, 1]).astype(bf16), rounded], axis=1
    )
    query = (project(0) + attn_bias[0, 0]).astype(bf16)
    saved = []
    for layer in range(LAYERS):
        shared_mate = flipped(shared, "tp", 0)
        parts = (query, shared, shared_mate)
        soft, pair, residual_one, normed = attend(
            layer, *parts, score_bias, states, out_weight, attn_bias, norm_gain, norm_shift
        )
        if layer == 0:
            pairs = page_pairs(facts, text_boxes, other_boxes)
            normed, *pairs = tied((normed, *pairs), ())
        act, act_send, slope, residual_two, *onwards = ffn(
            me,
            layer,
            pair,
            normed,
            gathered,
            units,
            ffn_out_bias,
            norm_gain,
            norm_shift,
            qkv_weight,
            attn_bias,
        )
        mates = (flipped(pair, "tp", 0), flipped(act_send, "tp", 0))
        saved.append((parts, soft, pair, residual_one, residual_two, act, slope, mates))
        if layer < LAYERS - 1:
            states, query, shared = onwards
    out_states = onwards[0]

    gradient = cotangent
    norm_sums = [None] * LAYERS
    projection_rows = [None] * LAYERS
    bin_grads = [None] * LAYERS
    score_grads = [None] * LAYERS
    projections = [None] * LAYERS
    ffns = [None] * LAYERS
    for layer in reversed(range(LAYERS)):
        last = layer == LAYERS - 1
        parts, soft, pair, residual_one, residual_two, act, slope, mates = saved[layer]
        dh, dh_send, low, bin_grads[layer], norm_sums[layer], grad_one, context_grad = ffn_back(
            me, layer, gradient, residual_two, residual_one, gathered, slope, norm_gain, out_weight
        )
        if not last:
            context_grad, dh_send = tied((context_grad, dh_send), ffns[-1].underway())
            ffns[-1].second(context_grad)
        dh_mate, low_mate = flipped(dh_send, "tp", 0), flipped(low, "tp", 0)
        score_grads[layer], *grads = attend_back(*parts, context_grad, soft)
        (dh, dh_mate, low_mate, pair_mate, act_mate), grads = (
            tied((dh, dh_mate, low_mate, *mates), grads[:1]),
            tied(grads, (dh_mate, low_mate, *mates)),
        )
        grads_mate = [flipped(part, "tp", 0) for part in grads]
        weights = ffn_grads(me, pair, pair_mate, low, low_mate, dh, dh_mate, act, act_mate)
        if not last:
            weights = tied(weights, projections[-1].underway() + ffns[-1].underway())
            projections[-1].second(weights[0])
            ffns[-1].scatter(weights[0])
        ffns[layer] = Shards(*weights)
        *weights, gradient, projection_rows[layer] = projection_grads(
            not last,
            me,
            layer,
            parts[1],
            parts[2],
            pair,
            mates[0],
            grads,
            grads_mate,
            low,
            low_mate,
            grad_one,
            qkv_weight,
        )
        if last:
            projections[layer] = Shards(*weights)

    half_at = me[:1] % 2
    vis_keep, vis_send, normal_grad, vis_rows = visual_back(
        half_at, gradient, normal_low, centered_hat, vis_weight
    )
    vis_came = flipped(vis_send, "tp", 0)
    seq_ways = [("seq", bit) for bit in range(mesh_bits("seq"))]
    far_ways = [("tp", bit) for bit in range(2, mesh_bits("tp"))]
    vis_ways = far_ways + [("tp", 1)] + seq_ways
    vis_sums = Tree(add_low(vis_keep, vis_came), vis_ways, join=("tp", 0))
    vis_sums.step()
    fold = functools.partial(fold_table, pairs, *score_grads, parts=FOLDS)
    folds = [fold(0, after=vis_sums.lefts)]
    folds[0], *weights = tied(
        (folds[0], *weights),
        ffns[0].underway() + projections[-1].underway() + vis_sums.rights + [ffns[-1].shard],
    )
    ffns[0].second(folds[0])
    projections[-1].scatter(folds[0])
    projections[0] = Shards(*weights)
    vis_sums.step(folds[0])
    folds.append(fold(1, after=folds + vis_sums.lefts))
    (folds[1],) = tied(
        folds[1:], ffns[0].underway() + vis_sums.rights + [projections[-1].shard]
    )
    ffns[0].scatter(folds[1])
    ffns[-1].join(folds[1])
    vis_sums.step(folds[1])
    small = join(norm_sums + projection_rows + bin_grads + [vis_rows, *folds])
    sizes = [part.shape[0] for part in norm_sums + projection_rows]
    sizes += [tp_size * bin_rows(units)] * LAYERS + [vis_rows.shape[0]]
    small_ways = [("tp", 0), ("tp", 1)] + seq_ways + far_ways
    small_sums = Tree(small, small_ways, add=jnp.add)
    small_sums.step()
    small_sums.step(*projections[0].underway())
    behind = small_sums.lefts[0]
    projections[0].second(behind)
    projections[-1].join(behind)
    small_sums.step(*projections[0].underway(), *vis_sums.rights)
    behind = small_sums.lefts[0]
    projections[0].halve(behind)
    vis_sums.step(behind)
    small_sums.step(projections[0].came, *vis_sums.rights)
    behind = small_sums.lefts[0]
    for _ in range(mesh_bits("tp") - 3):
        projections[0].halve_more(behind)
    while vis_sums.steps:
        vis_sums.step(behind)
    ffns[0].join(behind)
    while small_sums.steps:
        small_sums.step(projections[0].came)
    behind = small_sums.lefts[0]
    projections[0].halve_more(behind)
    projections[0].join()
    small, small_came = small_sums.result()
    vis_sum, vis_mate = vis_sums.result()
    vis_weight_grad = jnp.concatenate(
        [
            jnp.where(half == 0, vis_sum, vis_mate),
            jnp.where(half == 0, vis_mate, vis_sum),
        ],
        axis=0,
    ).astype(f32)
    grad_text = gradient[:text_rows]
    attn_total, bout_total, gain_total, shift_total, table_total, visb_total, *rest = split(
        me,
        small,
        small_came,
        sizes,
        count_cells,
        normal_grad,
        centered_hat,
        inverse_std,
        bn_gain,
        units,
        width,
    )
    bn_gain_grad, bn_shift_grad, bin_total, grad_maps = rest
    shard = width // tp_size
    qkv_total, out_total = write_out(
        projection_out_kernel,
        "projections_out",
        me,
        [part for shards in projections for part in (shards.shard, shards.other)],
        [(LAYERS, 3, shard, width), (LAYERS, shard, width)],
    )
    in_total, down_total = write_out(
        ffn_out_kernel,
        "feed_forward_out",
        me,
        [part for shards in ffns for part in (shards.shard, shards.other)],
        [(LAYERS, units, width)] * 2,
    )
    return (
        out_states,
        grad_text,
        grad_maps,
        qkv_total,
        out_total,
        attn_total.transpose(1, 0, 2),
        in_total,
        bin_total,
        down_total,
        bout_total,
        gain_total,
        shift_total,
        table_total.T,
        vis_weight_grad,
        visb_total.reshape(-1),
        bn_gain_grad[0],
        bn_shift_grad[0],
    )


def solution(mesh):
    rows = P(("seq", "tp"), None)
    units = P(None, "tp", None)
    return jax.shard_map(
        body,
        mesh=mesh,
        in_specs=(
            rows,
            rows,
            P(None, ("seq", "tp")),
            P(),
            P(),
            P(),
            P(),
            units,
            P(None, "tp"),
            units,
            P(),
            P(),
            P(),
            P(),
            P(),
            P(),
            P(),
            P(),
            rows,
        ),
        out_specs=(
            rows,
            rows,
            rows,
            P(None, None, "tp", None),
            units,
            P(),
            units,
            P(None, "tp"),
            units,
            P(),
            P(),
            P(),
            P(),
            P(),
            P(),
            P(),
            P(),
        ),
        check_vma=False,
    )
```

profile of v0, /device:TPU:0, one launch (start us, length us, event | category | flops | bytes accessed | tf_op | source)
XLA Modules:
  0.0 403.1 jit_solution(2650925417965011633)
XLA Ops:
  7.2 1.3 pad_maximum_fusion.1
  11.9 2.9 collective-permute-start.1
  14.8 1.6 collective-permute-done.1
  16.4 2.1 collective-permute-start.2
  18.5 1.6 collective-permute-done.2
  20.1 3.0 collective-permute-start.3
  23.1 1.7 collective-permute-done.3
  24.8 1.8 collective-permute-start.4
  26.7 1.7 collective-permute-done.4
  30.0 2.0 convolution_convert_fusion
  31.9 1.9 fusion.2
  36.7 1.2 page_pairs.1
  40.4 21.3 %score_bias.1.bias = f32[12,288,640]{2,1,0:T(8,128)} custom-call(s32[2]{0:T(128)S(1)} %pad_add_fusion.1.facts, s32[2,256]{1,0:T(2,128)S(1)} %copy-done.46, s32[2,256]{1,0:T(2,128)S(1)} %collective-permute-done.6.other_boxes, f32[12,8,128]{2,1,0:T(8,128)S(1)} %broadcast_in_dim.42.table_a, f32[12,8,128]{2,1,0:T(8,128)S(1)} %broadcast_in_dim.43.table_b), custom_call_target="tpu_custom_call" | custom-call | flops 1 | bytes 1 | tf_op jit(solution)/shard_map/score_bias/pallas_call | solution.py:223
  62.8 1.8 fusion.1.q_ref
  64.7 12.9 %attend.2 = (bf16[12,288,640]{2,1,0:T(8,128)(2,1)}, bf16[2,288,768]{2,1,0:T(8,128)(2,1)S(1)}, f32[288,768]{1,0:T(8,128)S(1)}, f32[288,768]{1,0:T(8,128)S(1)}) custom-call(bf16[288,768]{1,0:T(8,128)(2,1)S(1)} %fusion.1.q_ref, bf16[288,2304]{1,0:T(8,128)(2,1)} %copy-done.47, bf16[288,2304]{1,0:T(8,128)(2,1)} %collective-permute-done.5.kp.vp.x_mate, ...), custom_call_target="tpu_custom_call" | custom-call | flops 1 | bytes 1 | tf_op jit(solution)/shard_map/attend/pallas_call | solution.py:692
  78.5 36.8 %all-gather.3.cloned.1.call-done = bf16[6400,1536]{1,0:T(8,128)(2,1)} async-done(((bf16[400,1536]{1,0:T(8,128)(2,1)}), bf16[6400,1536]{1,0:T(8,128)(2,1)}) %all-gather.3.cloned.1.call-update) | async-done | bytes 19660816 | tf_op jit(solution)/shard_map/all_gather | solution.py:1271
  115.3 14.6 %feed_forward.2 = (bf16[8,288,192]{2,1,0:T(8,128)(2,1)}, bf16[8,288,192]{2,1,0:T(8,128)(2,1)}, bf16[16,288,192]{2,1,0:T(8,128)(2,1)}, f32[288,768]{1,0:T(8,128)S...) custom-call(s32[2]{0:T(128)S(1)} %pad_add_fusion.me, ...), custom_call_target="tpu_custom_call" | custom-call | flops 1 | bytes 1 | tf_op jit(solution)/shard_map/feed_forward/pallas_call | solution.py:866
  130.3 3.0 collective-permute-done.7.kp.vp.x_mate
  134.3 12.6 %attend.3 = (bf16[12,288,640]{2,1,0:T(8,128)(2,1)}, bf16[2,288,768]{2,1,0:T(8,128)(2,1)S(1)}, f32[288,768]{1,0:T(8,128)S(1)}, f32[288,768]{1,0:T(8,128)S(1)}) custom-call(bf16[288,768]{1,0:T(8,128)(2,1)S(1)} %get-tuple-element.201.q_ref, bf16[288,2304]{1,0:T(8,128)(2,1)} %get-tuple-element.202.ko.vo.x, bf16[288,2304]{1,0:T(8,128)(2,1)} %copy-done.48, ...), custom_call_target="tpu_custom_call" | custom-call | flops 1 | bytes 1 | tf_op jit(solution)/shard_map/attend/pallas_call | solution.py:692
  146.9 12.0 %feed_forward.3 = (bf16[8,288,192]{2,1,0:T(8,128)(2,1)S(1)}, bf16[8,288,192]{2,1,0:T(8,128)(2,1)}, bf16[16,288,192]{2,1,0:T(8,128)(2,1)}, f32[288,768]{1,0:T(8,128)S(1)}, bf16[288,768]{1,0:T(8,128)(2,1)}) custom-call(s32[2]{0:T(128)S(1)} %pad_add_fusion.me, bf16[2,288,768]{2,1,0:T(8,128)(2,1)S(1)} %get-tuple-element.204.x_ref.ctx.n, ...), custom_call_target="tpu_custom_call" | custom-call | flops 1 | bytes 1 | tf_op jit(solution)/shard_map/feed_forward/pallas_call | solution.py:866
  160.1 13.4 %feed_forward_back.2 = (bf16[8,288,192]{2,1,0:T(8,128)(2,1)}, bf16[8,288,192]{2,1,0:T(8,128)(2,1)}, bf16[2,288,768]{2,1,0:T(8,128)(2,1)S(1)}, f32[16,1,192]{2,1,...) custom-call(s32[2]{0:T(128)S(1)} %pad_add_fusion.me, ...), custom_call_target="tpu_custom_call" | custom-call | flops 1 | bytes 1 | tf_op jit(solution)/shard_map/feed_forward_back/pallas_call | solution.py:927
  175.4 11.0 %attend_back.2 = (bf16[12,288,640]{2,1,0:T(8,128)(2,1)}, bf16[288,768]{1,0:T(8,128)(2,1)S(1)}, bf16[288,768]{1,0:T(8,128)(2,1)S(1)}, bf16[288,768]{1,0:T(8,128)(...) custom-call(bf16[288,768]{1,0:T(8,128)(2,1)S(1)} %get-tuple-element.201.q_ref, ...), custom_call_target="tpu_custom_call" | custom-call | flops 1 | bytes 1 | tf_op jit(solution)/shard_map/attend_back/pallas_call | solution.py:757
  188.1 11.6 %feed_forward_grads.2 = (bf16[4,192,768]{2,1,0:T(8,128)(2,1)}, bf16[4,192,768]{2,1,0:T(8,128)(2,1)}, bf16[8,192,384]{2,1,0:T(8,128)(2,1)}, bf16[8,192,384]{2,1,0:T(8,128)(2,1)}) custom-call(s32[2]{0:T(128)S(1)} %pad_add_fusion.me, bf16[2,288,768]{2,1,0:T(8,128)(2,1)S(1)} %get-tuple-element.204.x_ref.ctx.n, ...), custom_call_target="tpu_custom_call" | custom-call | flops 1 | bytes 1 | tf_op jit(solution)/shard_map/feed_forward_grads/pallas_call | solution.py:1008
  199.7 1.3 collective-permute-start.18
  201.0 1.5 collective-permute-start.19
  203.1 1.2 collective-permute-done.15.refs_7_
  206.3 11.7 %projection_grads.2 = (bf16[4,48,1536]{2,1,0:T(8,128)(2,1)}, bf16[4,48,1536]{2,1,0:T(8,128)(2,1)}, bf16[8,48,768]{2,1,0:T(8,128)(2,1)}, bf16[8,48,768]{2,1,0:T(8...) custom-call(s32[2]{0:T(128)S(1)} %pad_add_fusion.me, bf16[288,2304]{1,0:T(8,128)(2,1)} %get-tuple-element.202.ko.vo.x, ...), custom_call_target="tpu_custom_call" | custom-call | flops 1 | bytes 1 | tf_op jit(solution)/shard_map/projection_grads/pallas_call | solution.py:1137
  218.1 1.2 copy-done.14
  219.3 13.5 %feed_forward_back.3 = (bf16[8,288,192]{2,1,0:T(8,128)(2,1)}, bf16[8,288,192]{2,1,0:T(8,128)(2,1)}, bf16[2,288,768]{2,1,0:T(8,128)(2,1)S(1)}, f32[16,1,192]{2,1,...) custom-call(s32[2]{0:T(128)S(1)} %pad_add_fusion.me, ...), custom_call_target="tpu_custom_call" | custom-call | flops 1 | bytes 1 | tf_op jit(solution)/shard_map/feed_forward_back/pallas_call | solution.py:927
  236.6 2.0 add_convert_fusion.8
  238.7 1.8 add_convert_fusion.9
  241.1 1.3 collective-permute-start.32
  242.4 1.5 collective-permute-start.31
  243.9 11.1 %attend_back.3 = (bf16[12,288,640]{2,1,0:T(8,128)(2,1)}, bf16[288,768]{1,0:T(8,128)(2,1)S(1)}, bf16[288,768]{1,0:T(8,128)(2,1)S(1)}, bf16[288,768]{1,0:T(8,128)(...) custom-call(bf16[288,768]{1,0:T(8,128)(2,1)S(1)} %copy-done.10, bf16[288,2304]{1,0:T(8,128)(2,1)} %copy-done.47, ...), custom_call_target="tpu_custom_call" | custom-call | flops 1 | bytes 1 | tf_op jit(solution)/shard_map/attend_back/pallas_call | solution.py:757
  256.8 11.5 %feed_forward_grads.3 = (bf16[4,192,768]{2,1,0:T(8,128)(2,1)}, bf16[4,192,768]{2,1,0:T(8,128)(2,1)}, bf16[8,192,384]{2,1,0:T(8,128)(2,1)}, bf16[8,192,384]{2,1,0:T(8,128)(2,1)}) custom-call(s32[2]{0:T(128)S(1)} %pad_add_fusion.me, bf16[2,288,768]{2,1,0:T(8,128)(2,1)S(1)} %get-tuple-element.195.x_ref.ctx.n, ...), custom_call_target="tpu_custom_call" | custom-call | flops 1 | bytes 1 | tf_op jit(solution)/shard_map/feed_forward_grads/pallas_call | solution.py:1008
  274.2 2.2 add_convert_fusion.18
  278.2 11.6 %projection_grads.3 = (bf16[4,48,1536]{2,1,0:T(8,128)(2,1)}, bf16[4,48,1536]{2,1,0:T(8,128)(2,1)}, bf16[8,48,768]{2,1,0:T(8,128)(2,1)}, bf16[8,48,768]{2,1,0:T(8...) custom-call(s32[2]{0:T(128)S(1)} %pad_add_fusion.me, bf16[288,2304]{1,0:T(8,128)(2,1)} %copy-done.47, ...), custom_call_target="tpu_custom_call" | custom-call | flops 1 | bytes 1 | tf_op jit(solution)/shard_map/projection_grads/pallas_call | solution.py:1137
  289.8 2.2 visual_back.1
  292.4 1.5 collective-permute-start.35
  294.0 1.6 collective-permute-start.37
  295.6 12.1 %table_grad.2.rest_0_.refs_7_ = f32[6,8,128]{2,1,0:T(8,128)} custom-call(bf16[640,256]{1,0:T(8,128)(2,1)} %copy-done.11, bf16[224,288]{1,0:T(8,128)(2,1)} %copy-done.18, bf16[4,288,640]{2,1,0:T(8,128)(2,1)} %copy-done.2, bf16[12,288,640]{2,1,0:T(8,128)(2,1)} %get-tuple-element.270.ds_a, bf16[12,288,640]{2,1,0:T(8,128)(2,1)} %get-tuple-element.271.ds_b, ...), custom_call_target="tpu_custom_call" | custom-call | flops 1 | bytes 1 | tf_op jit(solution)/shard_map/table_grad/pallas_call | solution.py:359
  311.5 1.7 add_convert_fusion.3
  313.2 1.2 collective-permute-start.38
  314.5 2.2 collective-permute-start.40
  316.7 12.3 %table_grad.3.refs_8_ = f32[6,8,128]{2,1,0:T(8,128)} custom-call(bf16[640,256]{1,0:T(8,128)(2,1)} %copy-done.11, bf16[224,288]{1,0:T(8,128)(2,1)} %copy-done.18, bf16[4,288,640]{2,1,0:T(8,128)(2,1)} %copy-done.2, bf16[12,288,640]{2,1,0:T(8,128)(2,1)} %get-tuple-element.270.ds_a, bf16[12,288,640]{2,1,0:T(8,128)(2,1)} %get-tuple-element.271.ds_b, ...), custom_call_target="tpu_custom_call" | custom-call | flops 1 | bytes 1 | tf_op jit(solution)/shard_map/table_grad/pallas_call | solution.py:359
  330.8 3.8 collective-permute-done.40
  334.6 1.6 reduce-scatter.6.cloned.1.call-done
  336.2 1.6 join.1
  337.8 1.2 add_convert_fusion.1
  340.4 3.2 collective-permute-done.42
  349.7 8.4 %collective-permute-done.47 = bf16[128,768]{1,0:T(8,128)(2,1)S(1)} collective-permute-done((bf16[128,768]{1,0:T(8,128)(2,1)S(1)}, bf16[128,768]{1,0:T(8,128)(2,1)S(1)}, u32[]{:S(2)}, u32[]{:S(2)}) %collective-permute-start.47) | collective-permute-done | bytes 196640 | tf_op jit(solution)/shard_map/ppermute | solution.py:43
  358.0 1.5 collective-permute-done.44
  359.8 1.2 collective-permute-start.49
  361.4 1.7 collective-permute-start.48
  364.3 1.7 collective-permute-start.55
  366.1 5.8 %collective-permute-done.48 = f32[266,128]{1,0:T(8,128)S(1)} collective-permute-done((f32[266,128]{1,0:T(8,128)S(1)}, f32[266,128]{1,0:T(8,128)S(1)}, u32[]{:S(2)}, u32[]{:S(2)}) %collective-permute-start.48) | collective-permute-done | bytes 136224 | tf_op jit(solution)/shard_map/ppermute | solution.py:43
  373.1 2.7 collective-permute-start.52
  375.9 2.4 collective-permute-done.51
  378.4 3.8 collective-permute-done.52
  382.3 1.7 collective-permute-start.54
  385.4 4.2 %collective-permute-done.53.right = f32[266,128]{1,0:T(8,128)S(1)} collective-permute-done((f32[266,128]{1,0:T(8,128)S(1)}, f32[266,128]{1,0:T(8,128)S(1)}, u32[]{:S(2)}, u32[]{:S(2)}) %collective-permute-start.53) | collective-permute-done | bytes 136224 | tf_op jit(solution)/shard_map/ppermute | solution.py:43
  390.3 2.4 split.1
  392.7 1.6 projections_out.1
  394.3 2.1 feed_forward_out.1
  (335 shorter events, 53.7 us)
Async XLA Ops:
  7.2 108.1 %all-gather.3.cloned.1.call-start = ((), (), s32[]{:S(2)}) async-start(), calls=%async_computation.6 | async-start | bytes 20889600 | tf_op jit(solution)/shard_map/all_gather | solution.py:1271
  9.8 298.0 %reduce-scatter.4.cloned.1.call-start = ((), (), s32[]{:S(2)}) async-start(), calls=%async_computation.3 | async-start | bytes 1474560 | tf_op jit(solution)/shard_map/reduce_scatter | solution.py:93
  10.5 1.3 collective-permute-start
  11.9 4.5 %collective-permute-start.1 = (f32[2,256]{1,0:T(2,128)S(1)}, f32[2,256]{1,0:T(2,128)S(1)}, u32[]{:S(2)}, u32[]{:S(2)}) collective-permute-start(f32[2,256]{1,0:T(2,128)S(1)} %fusion.23), channel_id=1, source_target_pairs={{0,2},{1,3},{2,0},{3,1},{4,6},{5,7},{6,4},{7,5},{8,10},{9,11},{10,... | collective-permute-start | bytes 6152 | tf_op jit(solution)/shard_map/ppermute | solution.py:43
  16.4 3.7 collective-permute-start.2
  20.1 4.7 %collective-permute-start.3 = (f32[2,256]{1,0:T(2,128)S(1)}, f32[2,256]{1,0:T(2,128)S(1)}, u32[]{:S(2)}, u32[]{:S(2)}) collective-permute-start(f32[2,256]{1,0:T(2,128)S(1)} %add.243), channel_id=1, source_target_pairs={{0,8},{1,9},{2,10},{3,11},{4,12},{5,13},{6,14},{7,15},{8,0},{9,1},... | collective-permute-start | bytes 6152 | tf_op jit(solution)/shard_map/ppermute | solution.py:43
  24.8 3.6 collective-permute-start.4
  33.9 30.7 %collective-permute-start.5 = (bf16[288,2304]{1,0:T(8,128)(2,1)S(1)}, bf16[288,2304]{1,0:T(8,128)(2,1)}, u32[]{:S(2)}, u32[]{:S(2)}) collective-permute-start(bf16[288,2304]{1,0:T(8,128)(2,1)S(1)} %pad_maximum_fusion.ko.vo.x), channel_id=1, source_target_pairs={{0,1},{1,0},{2,3},{3,2},{4,5},{5,4},{6,7},{7,6},{8,9},{9,8},{10,11... | collective-permute-start | bytes 3981320 | tf_op jit(solution)/shard_map/ppermute | solution.py:43
  34.5 2.2 collective-permute-start.6
  35.9 241.5 %copy-start.37 = (s32[2]{0:T(128)}, s32[2]{0:T(128)S(1)}, u32[]{:S(2)}) copy-start(s32[2]{0:T(128)S(1)} %pad_add_fusion.me) | copy-start | bytes 28
  129.9 3.3 collective-permute-start.7
  174.4 12.1 %collective-permute-start.10 = (bf16[8,288,192]{2,1,0:T(8,128)(2,1)}, bf16[8,288,192]{2,1,0:T(8,128)(2,1)S(1)}, u32[]{:S(2)}, u32[]{:S(2)}) collective-permute-start(bf16[8,288,192]{2,1,0:T(8,128)(2,1)} %get-tuple-element.217), channel_id=1, source_target_pairs={{0,1},{1,0},{2,3},{3,2},{4,5},{5,4},{6,7},{7,6},{8,9},{9,8},{10,11... | collective-permute-start | bytes 2654216 | tf_op jit(solution)/shard_map/ppermute | solution.py:43
  174.6 11.8 %collective-permute-start.11 = (bf16[2,288,768]{2,1,0:T(8,128)(2,1)S(1)}, bf16[2,288,768]{2,1,0:T(8,128)(2,1)S(1)}, u32[]{:S(2)}, u32[]{:S(2)}) collective-permute-start(bf16[2,288,768]{2,1,0:T(8,128)(2,1)S(1)} %get-tuple-element.218.refs_10_.dy), channel_id=1, source_target_pairs={{0,1},{1,0},{2,3},{3,2},{4,5},{5,4},{6,7},{7,6},{8,9},{9,8},{10,11... | collective-permute-start | bytes 2654216 | tf_op jit(solution)/shard_map/ppermute | solution.py:43
  174.9 11.6 %collective-permute-start.12 = (bf16[8,288,192]{2,1,0:T(8,128)(2,1)S(1)}, bf16[8,288,192]{2,1,0:T(8,128)(2,1)S(1)}, u32[]{:S(2)}, u32[]{:S(2)}) collective-permute-start(bf16[8,288,192]{2,1,0:T(8,128)(2,1)S(1)} %copy-done.89), channel_id=1, source_target_pairs={{0,1},{1,0},{2,3},{3,2},{4,5},{5,4},{6,7},{7,6},{8,9},{9,8},{10,11... | collective-permute-start | bytes 2654216 | tf_op jit(solution)/shard_map/ppermute | solution.py:43
  175.1 11.3 %collective-permute-start.9 = (bf16[2,288,768]{2,1,0:T(8,128)(2,1)S(1)}, bf16[2,288,768]{2,1,0:T(8,128)(2,1)S(1)}, u32[]{:S(2)}, u32[]{:S(2)}) collective-permute-start(bf16[2,288,768]{2,1,0:T(8,128)(2,1)S(1)} %get-tuple-element.204.x_ref.ctx.n), channel_id=1, source_target_pairs={{0,1},{1,0},{2,3},{3,2},{4,5},{5,4},{6,7},{7,6},{8,9},{9,8},{10,11... | collective-permute-start | bytes 2654216 | tf_op jit(solution)/shard_map/ppermute | solution.py:43
  186.5 16.0 %collective-permute-start.13 = (bf16[288,768]{1,0:T(8,128)(2,1)S(1)}, bf16[288,768]{1,0:T(8,128)(2,1)S(1)}, u32[]{:S(2)}, u32[]{:S(2)}) collective-permute-start(bf16[288,768]{1,0:T(8,128)(2,1)S(1)} %get-tuple-element.220.refs_0_), channel_id=1, source_target_pairs={{0,1},{1,0},{2,3},{3,2},{4,5},{5,4},{6,7},{7,6},{8,9},{9,8},{10,11... | collective-permute-start | bytes 1327112 | tf_op jit(solution)/shard_map/ppermute | solution.py:43
  186.8 16.2 %collective-permute-start.14 = (bf16[288,768]{1,0:T(8,128)(2,1)S(1)}, bf16[288,768]{1,0:T(8,128)(2,1)S(1)}, u32[]{:S(2)}, u32[]{:S(2)}) collective-permute-start(bf16[288,768]{1,0:T(8,128)(2,1)S(1)} %get-tuple-element.221.refs_1_), channel_id=1, source_target_pairs={{0,1},{1,0},{2,3},{3,2},{4,5},{5,4},{6,7},{7,6},{8,9},{9,8},{10,11... | collective-permute-start | bytes 1327112 | tf_op jit(solution)/shard_map/ppermute | solution.py:43
  199.7 36.2 %collective-permute-start.18 = (bf16[4,192,768]{2,1,0:T(8,128)(2,1)}, bf16[4,192,768]{2,1,0:T(8,128)(2,1)}, u32[]{:S(2)}, u32[]{:S(2)}) collective-permute-start(bf16[4,192,768]{2,1,0:T(8,128)(2,1)} %get-tuple-element.239), channel_id=1, source_target_pairs={{0,2},{1,3},{2,0},{3,1},{4,6},{5,7},{6,4},{7,5},{8,10},{9,11},{10,... | collective-permute-start | bytes 3538952 | tf_op jit(solution)/shard_map/ppermute | solution.py:43
  201.0 35.6 %collective-permute-start.19 = (bf16[8,192,384]{2,1,0:T(8,128)(2,1)}, bf16[8,192,384]{2,1,0:T(8,128)(2,1)}, u32[]{:S(2)}, u32[]{:S(2)}) collective-permute-start(bf16[8,192,384]{2,1,0:T(8,128)(2,1)} %get-tuple-element.240), channel_id=1, source_target_pairs={{0,16},{16,0},{1,17},{17,1},{2,18},{18,2},{3,19},{19,3},{4,20},{20... | collective-permute-start | bytes 3538952 | tf_op jit(solution)/shard_map/ppermute | solution.py:43
  202.5 1.8 collective-permute-start.15
  202.5 2.4 collective-permute-start.16
  203.0 2.5 collective-permute-start.17
  204.3 36.2 %collective-permute-start.8 = (bf16[2,288,768]{2,1,0:T(8,128)(2,1)S(1)}, bf16[2,288,768]{2,1,0:T(8,128)(2,1)S(1)}, u32[]{:S(2)}, u32[]{:S(2)}) collective-permute-start(bf16[2,288,768]{2,1,0:T(8,128)(2,1)S(1)} %get-tuple-element.195.x_ref.ctx.n), channel_id=1, source_target_pairs={{0,1},{1,0},{2,3},{3,2},{4,5},{5,4},{6,7},{7,6},{8,9},{9,8},{10,11... | collective-permute-start | bytes 2654216 | tf_op jit(solution)/shard_map/ppermute | solution.py:43
  204.9 36.2 %collective-permute-start.22 = (bf16[8,288,192]{2,1,0:T(8,128)(2,1)}, bf16[8,288,192]{2,1,0:T(8,128)(2,1)}, u32[]{:S(2)}, u32[]{:S(2)}) collective-permute-start(bf16[8,288,192]{2,1,0:T(8,128)(2,1)} %get-tuple-element.250), channel_id=1, source_target_pairs={{0,1},{1,0},{2,3},{3,2},{4,5},{5,4},{6,7},{7,6},{8,9},{9,8},{10,11... | collective-permute-start | bytes 2654216 | tf_op jit(solution)/shard_map/ppermute | solution.py:43
  235.7 6.7 %collective-permute-start.21 = (bf16[2,288,768]{2,1,0:T(8,128)(2,1)S(1)}, bf16[2,288,768]{2,1,0:T(8,128)(2,1)S(1)}, u32[]{:S(2)}, u32[]{:S(2)}) collective-permute-start(bf16[2,288,768]{2,1,0:T(8,128)(2,1)S(1)} %get-tuple-element.249.refs_10_.dy), channel_id=1, source_target_pairs={{0,1},{1,0},{2,3},{3,2},{4,5},{5,4},{6,7},{7,6},{8,9},{9,8},{10,11... | collective-permute-start | bytes 2654216 | tf_op jit(solution)/shard_map/ppermute | solution.py:43
  235.8 32.5 %collective-permute-start.29 = (bf16[4,48,1536]{2,1,0:T(8,128)(2,1)}, bf16[4,48,1536]{2,1,0:T(8,128)(2,1)S(1)}, u32[]{:S(2)}, u32[]{:S(2)}) collective-permute-start(bf16[4,48,1536]{2,1,0:T(8,128)(2,1)} %get-tuple-element.287), channel_id=1, source_target_pairs={{0,2},{1,3},{2,0},{3,1},{4,6},{5,7},{6,4},{7,5},{8,10},{9,11},{10,... | collective-permute-start | bytes 1769480 | tf_op jit(solution)/shard_map/ppermute | solution.py:43
  236.6 19.1 %collective-permute-start.20 = (bf16[8,288,192]{2,1,0:T(8,128)(2,1)}, bf16[8,288,192]{2,1,0:T(8,128)(2,1)S(1)}, u32[]{:S(2)}, u32[]{:S(2)}) collective-permute-start(bf16[8,288,192]{2,1,0:T(8,128)(2,1)} %get-tuple-element.248), channel_id=1, source_target_pairs={{0,1},{1,0},{2,3},{3,2},{4,5},{5,4},{6,7},{7,6},{8,9},{9,8},{10,11... | collective-permute-start | bytes 2654216 | tf_op jit(solution)/shard_map/ppermute | solution.py:43
  240.5 27.9 %collective-permute-start.30 = (bf16[8,48,768]{2,1,0:T(8,128)(2,1)S(1)}, bf16[8,48,768]{2,1,0:T(8,128)(2,1)S(1)}, u32[]{:S(2)}, u32[]{:S(2)}) collective-permute-start(bf16[8,48,768]{2,1,0:T(8,128)(2,1)S(1)} %copy-done.90), channel_id=1, source_target_pairs={{0,16},{16,0},{1,17},{17,1},{2,18},{18,2},{3,19},{19,3},{4,20},{20... | collective-permute-start | bytes 1769480 | tf_op jit(solution)/shard_map/ppermute | solution.py:43
  241.1 27.3 %collective-permute-start.32 = (bf16[4,192,384]{2,1,0:T(8,128)(2,1)S(1)}, bf16[4,192,384]{2,1,0:T(8,128)(2,1)S(1)}, u32[]{:S(2)}, u32[]{:S(2)}) collective-permute-start(bf16[4,192,384]{2,1,0:T(8,128)(2,1)S(1)} %get-tuple-element.382), channel_id=1, source_target_pairs={{0,2},{1,3},{2,0},{3,1},{4,6},{5,7},{6,4},{7,5},{8,10},{9,11},{10,... | collective-permute-start | bytes 1769480 | tf_op jit(solution)/shard_map/ppermute | solution.py:43
  242.4 26.4 %collective-permute-start.31 = (bf16[4,192,384]{2,1,0:T(8,128)(2,1)S(1)}, bf16[4,192,384]{2,1,0:T(8,128)(2,1)S(1)}, u32[]{:S(2)}, u32[]{:S(2)}) collective-permute-start(bf16[4,192,384]{2,1,0:T(8,128)(2,1)S(1)} %get-tuple-element.384), channel_id=1, source_target_pairs={{0,16},{16,0},{1,17},{17,1},{2,18},{18,2},{3,19},{19,3},{4,20},{20... | collective-permute-start | bytes 1769480 | tf_op jit(solution)/shard_map/ppermute | solution.py:43
  270.5 65.7 %reduce-scatter.6.cloned.1.call-start = ((), (), s32[]{:S(2)}) async-start(), calls=%async_computation.4 | async-start | bytes 737280 | tf_op jit(solution)/shard_map/reduce_scatter | solution.py:93
  271.5 2.1 collective-permute-start.23
  271.6 2.5 collective-permute-start.24
  272.0 35.7 %collective-permute-start.33 = (bf16[4,192,768]{2,1,0:T(8,128)(2,1)}, bf16[4,192,768]{2,1,0:T(8,128)(2,1)}, u32[]{:S(2)}, u32[]{:S(2)}) collective-permute-start(bf16[4,192,768]{2,1,0:T(8,128)(2,1)} %get-tuple-element.295), channel_id=1, source_target_pairs={{0,2},{1,3},{2,0},{3,1},{4,6},{5,7},{6,4},{7,5},{8,10},{9,11},{10,... | collective-permute-start | bytes 3538952 | tf_op jit(solution)/shard_map/ppermute | solution.py:43
  273.1 34.7 %collective-permute-start.34 = (bf16[8,192,384]{2,1,0:T(8,128)(2,1)}, bf16[8,192,384]{2,1,0:T(8,128)(2,1)S(1)}, u32[]{:S(2)}, u32[]{:S(2)}) collective-permute-start(bf16[8,192,384]{2,1,0:T(8,128)(2,1)} %get-tuple-element.296), channel_id=1, source_target_pairs={{0,16},{16,0},{1,17},{17,1},{2,18},{18,2},{3,19},{19,3},{4,20},{20... | collective-permute-start | bytes 3538952 | tf_op jit(solution)/shard_map/ppermute | solution.py:43
  273.6 2.8 collective-permute-start.25
  273.6 3.7 collective-permute-start.26
  274.1 3.2 collective-permute-start.27
  276.4 31.3 %collective-permute-start.36 = (bf16[4,48,768]{2,1,0:T(8,128)(2,1)}, bf16[4,48,768]{2,1,0:T(8,128)(2,1)}, u32[]{:S(2)}, u32[]{:S(2)}) collective-permute-start(bf16[4,48,768]{2,1,0:T(8,128)(2,1)} %get-tuple-element.390), channel_id=1, source_target_pairs={{0,2},{1,3},{2,0},{3,1},{4,6},{5,7},{6,4},{7,5},{8,10},{9,11},{10,... | collective-permute-start | bytes 884744 | tf_op jit(solution)/shard_map/ppermute | solution.py:43
  292.0 1.9 collective-permute-start.28
  292.4 15.3 %collective-permute-start.35 = (bf16[4,48,768]{2,1,0:T(8,128)(2,1)S(1)}, bf16[4,48,768]{2,1,0:T(8,128)(2,1)S(1)}, u32[]{:S(2)}, u32[]{:S(2)}) collective-permute-start(bf16[4,48,768]{2,1,0:T(8,128)(2,1)S(1)} %get-tuple-element.392), channel_id=1, source_target_pairs={{0,16},{16,0},{1,17},{17,1},{2,18},{18,2},{3,19},{19,3},{4,20},{20... | collective-permute-start | bytes 884744 | tf_op jit(solution)/shard_map/ppermute | solution.py:43
  294.0 13.7 %collective-permute-start.37 = (bf16[128,768]{1,0:T(8,128)(2,1)S(1)}, bf16[128,768]{1,0:T(8,128)(2,1)S(1)}, u32[]{:S(2)}, u32[]{:S(2)}) collective-permute-start(bf16[128,768]{1,0:T(8,128)(2,1)S(1)} %add_convert_fusion.26.rest_0_), channel_id=1, source_target_pairs={{0,4},{1,5},{2,6},{3,7},{4,0},{5,1},{6,2},{7,3},{8,12},{9,13},{10,... | collective-permute-start | bytes 589832 | tf_op jit(solution)/shard_map/ppermute | solution.py:43
  309.9 74.1 %reduce-scatter.8.cloned.1.call-start = ((), (), s32[]{:S(2)}) async-start(), calls=%async_computation.5 | async-start | bytes 1474560 | tf_op jit(solution)/shard_map/reduce_scatter | solution.py:93
  310.4 24.3 %collective-permute-start.39 = (bf16[4,192,384]{2,1,0:T(8,128)(2,1)S(1)}, bf16[4,192,384]{2,1,0:T(8,128)(2,1)S(1)}, u32[]{:S(2)}, u32[]{:S(2)}) collective-permute-start(bf16[4,192,384]{2,1,0:T(8,128)(2,1)S(1)} %get-tuple-element.378), channel_id=1, source_target_pairs={{0,2},{1,3},{2,0},{3,1},{4,6},{5,7},{6,4},{7,5},{8,10},{9,11},{10,... | collective-permute-start | bytes 1769480 | tf_op jit(solution)/shard_map/ppermute | solution.py:43
  313.2 21.4 %collective-permute-start.38 = (bf16[4,192,384]{2,1,0:T(8,128)(2,1)S(1)}, bf16[4,192,384]{2,1,0:T(8,128)(2,1)}, u32[]{:S(2)}, u32[]{:S(2)}) collective-permute-start(bf16[4,192,384]{2,1,0:T(8,128)(2,1)S(1)} %get-tuple-element.380), channel_id=1, source_target_pairs={{0,16},{16,0},{1,17},{17,1},{2,18},{18,2},{3,19},{19,3},{4,20},{20... | collective-permute-start | bytes 1769480 | tf_op jit(solution)/shard_map/ppermute | solution.py:43
  314.5 20.1 %collective-permute-start.40 = (bf16[128,768]{1,0:T(8,128)(2,1)S(1)}, bf16[128,768]{1,0:T(8,128)(2,1)S(1)}, u32[]{:S(2)}, u32[]{:S(2)}) collective-permute-start(bf16[128,768]{1,0:T(8,128)(2,1)S(1)} %add_convert_fusion.25.rest_1_), channel_id=1, source_target_pairs={{0,8},{1,9},{2,10},{3,11},{4,12},{5,13},{6,14},{7,15},{8,0},{9,1},... | collective-permute-start | bytes 589832 | tf_op jit(solution)/shard_map/ppermute | solution.py:43
  328.9 14.6 %collective-permute-start.42 = (bf16[4,48,1536]{2,1,0:T(8,128)(2,1)}, bf16[4,48,1536]{2,1,0:T(8,128)(2,1)S(1)}, u32[]{:S(2)}, u32[]{:S(2)}) collective-permute-start(bf16[4,48,1536]{2,1,0:T(8,128)(2,1)} %get-tuple-element.321), channel_id=1, source_target_pairs={{0,2},{1,3},{2,0},{3,1},{4,6},{5,7},{6,4},{7,5},{8,10},{9,11},{10,... | collective-permute-start | bytes 1769480 | tf_op jit(solution)/shard_map/ppermute | solution.py:43
  329.9 14.3 %collective-permute-start.43 = (bf16[8,48,768]{2,1,0:T(8,128)(2,1)}, bf16[8,48,768]{2,1,0:T(8,128)(2,1)S(1)}, u32[]{:S(2)}, u32[]{:S(2)}) collective-permute-start(bf16[8,48,768]{2,1,0:T(8,128)(2,1)} %get-tuple-element.322), channel_id=1, source_target_pairs={{0,16},{16,0},{1,17},{17,1},{2,18},{18,2},{3,19},{19,3},{4,20},{20... | collective-permute-start | bytes 1769480 | tf_op jit(solution)/shard_map/ppermute | solution.py:43
  337.8 6.5 %collective-permute-start.41 = (f32[266,128]{1,0:T(8,128)}, f32[266,128]{1,0:T(8,128)}, u32[]{:S(2)}, u32[]{:S(2)}) collective-permute-start(f32[266,128]{1,0:T(8,128)} %join.1), channel_id=1, source_target_pairs={{0,1},{1,0},{2,3},{3,2},{4,5},{5,4},{6,7},{7,6},{8,9},{9,8},{10,11... | collective-permute-start | bytes 408584 | tf_op jit(solution)/shard_map/ppermute | solution.py:43
  345.4 14.1 %collective-permute-start.46 = (bf16[4,48,768]{2,1,0:T(8,128)(2,1)S(1)}, bf16[4,48,768]{2,1,0:T(8,128)(2,1)S(1)}, u32[]{:S(2)}, u32[]{:S(2)}) collective-permute-start(bf16[4,48,768]{2,1,0:T(8,128)(2,1)S(1)} %get-tuple-element.386), channel_id=1, source_target_pairs={{0,2},{1,3},{2,0},{3,1},{4,6},{5,7},{6,4},{7,5},{8,10},{9,11},{10,... | collective-permute-start | bytes 884744 | tf_op jit(solution)/shard_map/ppermute | solution.py:43
  346.7 12.8 %collective-permute-start.45 = (bf16[4,48,768]{2,1,0:T(8,128)(2,1)S(1)}, bf16[4,48,768]{2,1,0:T(8,128)(2,1)S(1)}, u32[]{:S(2)}, u32[]{:S(2)}) collective-permute-start(bf16[4,48,768]{2,1,0:T(8,128)(2,1)S(1)} %get-tuple-element.388), channel_id=1, source_target_pairs={{0,16},{16,0},{1,17},{17,1},{2,18},{18,2},{3,19},{19,3},{4,20},{20... | collective-permute-start | bytes 884744 | tf_op jit(solution)/shard_map/ppermute | solution.py:43
  347.6 10.5 %collective-permute-start.47 = (bf16[128,768]{1,0:T(8,128)(2,1)S(1)}, bf16[128,768]{1,0:T(8,128)(2,1)S(1)}, u32[]{:S(2)}, u32[]{:S(2)}) collective-permute-start(bf16[128,768]{1,0:T(8,128)(2,1)S(1)} %add_convert_fusion.24), channel_id=1, source_target_pairs={{0,2},{1,3},{2,0},{3,1},{4,6},{5,7},{6,4},{7,5},{8,10},{9,11},{10,... | collective-permute-start | bytes 589832 | tf_op jit(solution)/shard_map/ppermute | solution.py:43
  348.7 10.8 %collective-permute-start.44 = (f32[266,128]{1,0:T(8,128)S(1)}, f32[266,128]{1,0:T(8,128)S(1)}, u32[]{:S(2)}, u32[]{:S(2)}) collective-permute-start(f32[266,128]{1,0:T(8,128)S(1)} %add.278), channel_id=1, source_target_pairs={{0,2},{1,3},{2,0},{3,1},{4,6},{5,7},{6,4},{7,5},{8,10},{9,11},{10,... | collective-permute-start | bytes 408584 | tf_op jit(solution)/shard_map/ppermute | solution.py:43
  359.8 12.3 %collective-permute-start.49 = (bf16[2,96,768]{2,1,0:T(8,128)(2,1)S(1)}, bf16[2,96,768]{2,1,0:T(8,128)(2,1)S(1)}, u32[]{:S(2)}, u32[]{:S(2)}) collective-permute-start(bf16[2,96,768]{2,1,0:T(8,128)(2,1)S(1)} %pad_maximum_fusion.6), channel_id=1, source_target_pairs={{0,4},{1,5},{2,6},{3,7},{4,0},{5,1},{6,2},{7,3},{8,12},{9,13},{10,... | collective-permute-start | bytes 884744 | tf_op jit(solution)/shard_map/ppermute | solution.py:43
  361.0 10.9 %collective-permute-start.50 = (bf16[128,768]{1,0:T(8,128)(2,1)S(1)}, bf16[128,768]{1,0:T(8,128)(2,1)S(1)}, u32[]{:S(2)}, u32[]{:S(2)}) collective-permute-start(bf16[128,768]{1,0:T(8,128)(2,1)S(1)} %add_convert_fusion.23), channel_id=1, source_target_pairs={{0,16},{16,0},{1,17},{17,1},{2,18},{18,2},{3,19},{19,3},{4,20},{20... | collective-permute-start | bytes 589832 | tf_op jit(solution)/shard_map/ppermute | solution.py:43
  361.4 10.5 %collective-permute-start.48 = (f32[266,128]{1,0:T(8,128)S(1)}, f32[266,128]{1,0:T(8,128)S(1)}, u32[]{:S(2)}, u32[]{:S(2)}) collective-permute-start(f32[266,128]{1,0:T(8,128)S(1)} %add.282), channel_id=1, source_target_pairs={{0,16},{16,0},{1,17},{17,1},{2,18},{18,2},{3,19},{19,3},{4,20},{20... | collective-permute-start | bytes 408584 | tf_op jit(solution)/shard_map/ppermute | solution.py:43
  364.0 30.2 %collective-permute-start.57 = (bf16[384,384]{1,0:T(8,128)(2,1)S(1)}, bf16[384,384]{1,0:T(8,128)(2,1)S(1)}, u32[]{:S(2)}, u32[]{:S(2)}) collective-permute-start(bf16[384,384]{1,0:T(8,128)(2,1)S(1)} %bitcast.85), channel_id=1, source_target_pairs={{0,16},{16,0},{1,17},{17,1},{2,18},{18,2},{3,19},{19,3},{4,20},{20... | collective-permute-start | bytes 884744 | tf_op jit(solution)/shard_map/ppermute | solution.py:43
  364.3 28.3 %collective-permute-start.55 = (bf16[96,768]{1,0:T(8,128)(2,1)S(1)}, bf16[96,768]{1,0:T(8,128)(2,1)S(1)}, u32[]{:S(2)}, u32[]{:S(2)}) collective-permute-start(bf16[96,768]{1,0:T(8,128)(2,1)S(1)} %bitcast.89), channel_id=1, source_target_pairs={{0,16},{16,0},{1,17},{17,1},{2,18},{18,2},{3,19},{19,3},{4,20},{20... | collective-permute-start | bytes 442376 | tf_op jit(solution)/shard_map/ppermute | solution.py:43
  372.1 6.3 %collective-permute-start.51 = (f32[266,128]{1,0:T(8,128)S(1)}, f32[266,128]{1,0:T(8,128)S(1)}, u32[]{:S(2)}, u32[]{:S(2)}) collective-permute-start(f32[266,128]{1,0:T(8,128)S(1)} %add.288), channel_id=1, source_target_pairs={{0,4},{1,5},{2,6},{3,7},{4,0},{5,1},{6,2},{7,3},{8,12},{9,13},{10,... | collective-permute-start | bytes 408584 | tf_op jit(solution)/shard_map/ppermute | solution.py:43
  373.1 9.1 %collective-permute-start.52 = (bf16[1,96,768]{2,1,0:T(8,128)(2,1)S(1)}, bf16[1,96,768]{2,1,0:T(8,128)(2,1)S(1)}, u32[]{:S(2)}, u32[]{:S(2)}) collective-permute-start(bf16[1,96,768]{2,1,0:T(8,128)(2,1)S(1)} %get-tuple-element.394), channel_id=1, source_target_pairs={{0,8},{1,9},{2,10},{3,11},{4,12},{5,13},{6,14},{7,15},{8,0},{9,1},... | collective-permute-start | bytes 442376 | tf_op jit(solution)/shard_map/ppermute | solution.py:43
  375.8 8.2 %collective-permute-start.58 = (bf16[128,768]{1,0:T(8,128)(2,1)S(1)}, bf16[128,768]{1,0:T(8,128)(2,1)S(1)}, u32[]{:S(2)}, u32[]{:S(2)}) collective-permute-start(bf16[128,768]{1,0:T(8,128)(2,1)S(1)} %add_convert_fusion.22), channel_id=1, source_target_pairs={{0,1},{1,0},{2,3},{3,2},{4,5},{5,4},{6,7},{7,6},{8,9},{9,8},{10,11... | collective-permute-start | bytes 589832 | tf_op jit(solution)/shard_map/ppermute | solution.py:43
  382.2 7.4 %collective-permute-start.53 = (f32[266,128]{1,0:T(8,128)S(1)}, f32[266,128]{1,0:T(8,128)S(1)}, u32[]{:S(2)}, u32[]{:S(2)}) collective-permute-start(f32[266,128]{1,0:T(8,128)S(1)} %add.292.left), channel_id=1, source_target_pairs={{0,8},{1,9},{2,10},{3,11},{4,12},{5,13},{6,14},{7,15},{8,0},{9,1},... | collective-permute-start | bytes 408584 | tf_op jit(solution)/shard_map/ppermute | solution.py:43
  382.3 10.3 %collective-permute-start.54 = (bf16[96,768]{1,0:T(8,128)(2,1)S(1)}, bf16[96,768]{1,0:T(8,128)(2,1)S(1)}, u32[]{:S(2)}, u32[]{:S(2)}) collective-permute-start(bf16[96,768]{1,0:T(8,128)(2,1)S(1)} %fusion.16.refs_0_), channel_id=1, source_target_pairs={{0,16},{16,0},{1,17},{17,1},{2,18},{18,2},{3,19},{19,3},{4,20},{20... | collective-permute-start | bytes 442376 | tf_op jit(solution)/shard_map/ppermute | solution.py:43
  384.0 10.2 %collective-permute-start.56 = (bf16[384,384]{1,0:T(8,128)(2,1)}, bf16[384,384]{1,0:T(8,128)(2,1)S(1)}, u32[]{:S(2)}, u32[]{:S(2)}) collective-permute-start(bf16[384,384]{1,0:T(8,128)(2,1)} %bitcast.87), channel_id=1, source_target_pairs={{0,16},{16,0},{1,17},{17,1},{2,18},{18,2},{3,19},{19,3},{4,20},{20... | collective-permute-start | bytes 884744 | tf_op jit(solution)/shard_map/ppermute | solution.py:43
  (91 other events, 793.1 us)
Sparse Core Ops, SparseCore 0:
  9.9 105.3 all-gather.2
  270.6 28.4 reduce-scatter.3
  310.1 26.1 reduce-scatter.5
  340.5 33.6 reduce-scatter.7
where the time goes:
time: 408 us; the launch traced here: 403 us
  Pallas kernels  204 us (50%)
  waiting for transfers between devices  86.2 us (21%)
  starting transfers between devices  49.1 us (12%)
  local copies, waits for them, and re-layouts  21.5 us (5%)
  other arithmetic  21.3 us (5%)
  between operations  15.1 us (4%)
  matrix products  5.82 us (1%)
    ppermute x59, starting transfers between devices, flipped(): return lax.ppermute(block, axis, [(i, i ^ 1 << bit) for i in range(count)])  48.9 us
    ppermute x59, waiting for transfers between devices, flipped(): return lax.ppermute(block, axis, [(i, i ^ 1 << bit) for i in range(count)])  47.7 us
    all_gather x1, waiting for transfers between devices, body(): gathered = lax.all_gather(packed, 'tp', axis=0)  36.8 us
    pallas_call x2, Pallas kernels, ffn_back(): pl.pallas_call(functools.partial(ffn_back_kernel, layer), out_shape=[half...  26.9 us
    pallas_call x2, Pallas kernels, ffn(): pl.pallas_call(functools.partial(ffn_kernel, layer, more), out_shape=out_...  26.6 us
    pallas_call x2, Pallas kernels, attend(): pl.pallas_call(functools.partial(attend_kernel, layer), grid=(PAIRS,), in...  25.5 us
    pallas_call x2, Pallas kernels, fold_table(): pl.pallas_call(table_kernel, out_shape=jax.ShapeDtypeStruct((count, 8, LA...  24.4 us
    pallas_call x2, Pallas kernels, projection_grads(): pl.pallas_call(functools.partial(projection_kernel, by_distance), out_sha...  23.3 us
  transfers between devices with their start and end apart: 63, of which 23 were waited for; matrix products, arithmetic and copies ran while one was open for 6% of the time, Pallas kernels for 37%

commit v1 on v0

--- a/solution.py
+++ b/solution.py
@@ -22,8 +22,11 @@
 ROWS = HALF_TEXT + HALF_SLOTS
 KEYS = 640
 PAIRS = HEADS // 2
+SLABS = 2
+STEPS = PAIRS // SLABS
 LANES = 128
 FOLDS = 2
+FOLD_HEADS = 2
 BLOCKS = 4
 HALF = BLOCKS // 2
 norm_epsilon = 1e-05
@@ -83,14 +86,11 @@
         self.seq = add_low(seq[:far], seq_came[:far])
         self.seq_came = flipped(add_low(seq[far:], seq_came[far:]), "tp", 1)
 
-    def scatter(self, *after):
+    def arrived(self, *after):
         near, near_came, seq, seq_came = tied(
             (self.near, self.near_came, self.seq, self.seq_came), after
         )
-        both = jnp.concatenate([add_low(near, near_came), add_low(seq, seq_came)], axis=1)
-        count = lax.axis_size("tp")
-        groups = [list(range(first, count, 4)) for first in range(4)]
-        self.shard = lax.psum_scatter(both, "tp", scatter_dimension=0, axis_index_groups=groups)
+        return add_low(near, near_came), add_low(seq, seq_came)
 
     def halve(self, *after):
         near, near_came, seq, seq_came = tied(
@@ -117,6 +117,29 @@
         self.shard = add_low(pick(shard, 0), pick(came, 0))
         self.came = flipped(add_low(pick(shard, 1), pick(came, 1)), "tp", self.bit)
         self.bit += 1
+
+    def join(self, *after):
+        (shard,) = tied((self.shard,), after)
+        for bit in range(1, mesh_bits("seq")):
+            shard = add_low(shard, flipped(shard, "seq", bit))
+        self.shard = shard
+        self.other = flipped(shard, "seq", 0)
+
+
+class Scattered:
+    def __init__(self, group, *after):
+        parts = [part for shards in group for part in shards.arrived(*after)]
+        columns = min(part.shape[-1] for part in parts)
+        pieces = [
+            part[..., start : start + columns]
+            for part in parts
+            for start in range(0, part.shape[-1], columns)
+        ]
+        count = lax.axis_size("tp")
+        groups = [list(range(first, count, 4)) for first in range(4)]
+        self.shard = lax.psum_scatter(
+            jnp.concatenate(pieces, axis=1), "tp", scatter_dimension=0, axis_index_groups=groups
+        )
 
     def join(self, *after):
         (shard,) = tied((self.shard,), after)
@@ -289,8 +312,12 @@
 
 
 def table_kernel(right, left, masks, ds_a, ds_b, *rest):
-    out = rest[-1]
-    total = (ds_a[0].astype(f32) + ds_b[0].astype(f32)).astype(bf16)
+    for head in range(ds_a.shape[0]):
+        fold_head(right, left, masks, ds_a[head], ds_b[head], rest[-1].at[head])
+
+
+def fold_head(right, left, masks, ds_a, ds_b, out):
+    total = (ds_a.astype(f32) + ds_b.astype(f32)).astype(bf16)
     hot = right[...]
     query_hot = left[...]
 
@@ -298,10 +325,15 @@
         inner = jnp.dot(values, hot[:, columns], preferred_element_type=f32).astype(bf16)
         return jnp.dot(query_hot[rows], inner, preferred_element_type=f32)
 
-    plain = fold(total, slice(0, 128), slice(0, 160))
     near = fold(total * masks[0], slice(128, 256), slice(160, 224))
-    by_x = fold(total * masks[1], slice(0, 128), slice(0, 64))
-    by_y = fold(total * masks[2], slice(0, 128), slice(64, 160))
+    together = jnp.concatenate([total, total * masks[1], total * masks[2]], axis=0)
+    inner = jnp.dot(together, hot[:, :128], preferred_element_type=f32).astype(bf16)
+    outer = lambda rows, which: jnp.dot(
+        query_hot[rows], inner[which * ROWS : (which + 1) * ROWS], preferred_element_type=f32
+    )
+    plain = outer(slice(0, 160), 0)
+    by_x = outer(slice(0, 64), 1)
+    by_y = outer(slice(64, 160), 2)
 
     def diagonals(square):
         lane = lax.broadcasted_iota(jnp.int32, square.shape, 1)
@@ -314,7 +346,7 @@
 
     above = jnp.sum((total * masks[3]).astype(f32), axis=0, keepdims=True)
     above = sum(above[:, t * LANES : (t + 1) * LANES] for t in range(KEYS // LANES))
-    out[0] = jnp.concatenate(
+    out[...] = jnp.concatenate(
         [
             diagonals(plain[:64]),
             diagonals(by_x),
@@ -355,15 +387,16 @@
 
 def fold_table(pairs, ds_a, ds_b, part, parts, after=()):
     count = HEADS // parts
-    head = pl.BlockSpec((1, ROWS, KEYS), lambda h: (h + part * count, 0, 0))
+    steps = count // FOLD_HEADS
+    head = pl.BlockSpec((FOLD_HEADS, ROWS, KEYS), lambda h: (h + part * steps, 0, 0))
     return pl.pallas_call(
         table_kernel,
         out_shape=jax.ShapeDtypeStruct((count, 8, LANES), f32),
-        grid=(count,),
+        grid=(steps,),
         in_specs=[full(array) for array in pairs]
         + [head, head]
         + [pl.BlockSpec(memory_space=pl.ANY)] * len(after),
-        out_specs=pl.BlockSpec((1, 8, LANES), lambda h: (h, 0, 0)),
+        out_specs=pl.BlockSpec((FOLD_HEADS, 8, LANES), lambda h: (h, 0, 0)),
         compiler_params=pltpu.CompilerParams(vmem_limit_bytes=58 * MIB),
         cost_estimate=brief,
         name="table_grad",
@@ -425,10 +458,10 @@
 
 
 def join_kernel(*refs):
-    out = refs[-1]
+    low, out = refs[-2:]
     out[...] = jnp.zeros_like(out)
     at = 0
-    for ref in refs[:-1]:
+    for ref in refs[:-2]:
         values = ref[...]
         if len(values.shape) == 3 and values.shape[1] > 1:
             for head in range(values.shape[0]):
@@ -443,6 +476,7 @@
         else:
             out[at : at + values.shape[0], :] = values
             at += values.shape[0]
+    low[...] = out[...].astype(bf16)
 
 
 def bin_rows(units):
@@ -456,12 +490,14 @@
             rows += part.shape[0] * bin_rows(part.shape[2])
         else:
             rows += part.size // LANES
+    rows += -rows % 16
     vmem = pl.BlockSpec(memory_space=pltpu.VMEM)
     return pl.pallas_call(
         join_kernel,
-        out_shape=jax.ShapeDtypeStruct((rows, LANES), f32),
+        out_shape=jax.ShapeDtypeStruct((rows, LANES), bf16),
         in_specs=[vmem] * len(parts),
         out_specs=vmem,
+        scratch_shapes=[pltpu.VMEM((rows, LANES), f32)],
         cost_estimate=brief,
         name="join",
     )(*parts)
@@ -490,7 +526,7 @@
     maps,
     total,
 ):
-    total[...] = left[...] + right[...]
+    total[...] = left[...].astype(f32) + right[...].astype(f32)
     units = hidden_bias.shape[1]
     width = out_bias.shape[1]
     channels = gain_grad.shape[1]
@@ -650,48 +686,75 @@
     pair,
     residual,
     normed,
+    x_s,
+    weight_s,
+    semaphores,
 ):
     step = pl.program_id(0)
-    q = q_ref[...] * jnp.asarray(HEAD_DIM**-0.5, bf16)
-    keys = whole_page(ko[...], kp[...])
-    values = whole_page(vo[...], vp[...])
+    later = Later([(x_ref, x_s), (weight.at[layer], weight_s)], semaphores)
+    pl.when(step == 0)(later.start)
     first = lax.broadcasted_iota(jnp.int32, (ROWS, LANES), 1) < HEAD_DIM
-    parts = []
-    for head in range(2):
-        mine = jnp.where(first if head == 0 else ~first, q, jnp.zeros_like(q))
-        scores = nt_dot(mine, keys) + bias[head]
-        raised = jnp.exp(scores - jnp.max(scores, axis=1, keepdims=True))
-        weights = (raised * (1.0 / jnp.sum(raised, axis=1, keepdims=True))).astype(bf16)
-        soft[head] = weights
-        parts.append(jnp.dot(weights, values, preferred_element_type=f32))
-    slab = pl.ds(pl.multiple_of(step * LANES, LANES), LANES)
-    pair[0, :, slab] = jnp.where(first, parts[0], parts[1]).astype(bf16)
-
-    @pl.when(step == PAIRS - 1)
+    for part in range(SLABS):
+        lanes = slice(part * LANES, (part + 1) * LANES)
+        q = q_ref[:, lanes] * jnp.asarray(HEAD_DIM**-0.5, bf16)
+        keys = whole_page(ko[:, lanes], kp[:, lanes])
+        values = whole_page(vo[:, lanes], vp[:, lanes])
+        found = []
+        for head in range(2):
+            mine = jnp.where(first if head == 0 else ~first, q, jnp.zeros_like(q))
+            scores = nt_dot(mine, keys) + bias[2 * part + head]
+            raised = jnp.exp(scores - jnp.max(scores, axis=1, keepdims=True))
+            weights = (raised * (1.0 / jnp.sum(raised, axis=1, keepdims=True))).astype(bf16)
+            soft[2 * part + head] = weights
+            found.append(jnp.dot(weights, values, preferred_element_type=f32))
+        slab = pl.ds(pl.multiple_of((step * SLABS + part) * LANES, LANES), LANES)
+        pair[0, :, slab] = jnp.where(first, found[0], found[1]).astype(bf16)
+
+    @pl.when(step == STEPS - 1)
     def _():
-        attended = jnp.dot(pair[0], weight[0], preferred_element_type=f32)
-        summed = x_ref[...] + (attended + attn_bias[layer, 2:3, :])
+        later.wait(0, 1)
+        attended = jnp.dot(pair[0], weight_s[...], preferred_element_type=f32)
+        summed = x_s[...] + (attended + attn_bias[layer, 2:3, :])
         residual[...] = summed
         out = centred(summed)[0] * gain[layer, 0:1, :] + shift[layer, 0:1, :]
         normed[...] = out
         pair[1] = out.astype(bf16)
 
 
+class Later:
+    def __init__(self, pairs, semaphores):
+        self.copies = [
+            pltpu.make_async_copy(source, target, semaphores.at[index])
+            for index, (source, target) in enumerate(pairs)
+        ]
+
+    def start(self):
+        for copy in self.copies:
+            copy.start()
+
+    def wait(self, *indices):
+        for index in indices:
+            self.copies[index].wait()
+
+
+anywhere = pl.BlockSpec(memory_space=pl.ANY)
+
+
 def full(array):
     return pl.BlockSpec(array.shape, lambda *at: (0,) * array.ndim)
 
 
 def attend(layer, q, kv, other_kv, bias, x, out_weight, attn_bias, gain, shift):
     rows, width = q.shape
-    slab = pl.BlockSpec((ROWS, LANES), lambda p: (0, p))
-    second = pl.BlockSpec((ROWS, LANES), lambda p: (0, p + PAIRS))
-    heads = pl.BlockSpec((2, ROWS, KEYS), lambda p: (p, 0, 0))
+    slab = pl.BlockSpec((ROWS, SLABS * LANES), lambda p: (0, p))
+    second = pl.BlockSpec((ROWS, SLABS * LANES), lambda p: (0, p + STEPS))
+    heads = pl.BlockSpec((2 * SLABS, ROWS, KEYS), lambda p: (p, 0, 0))
     whole = pl.BlockSpec((rows, width), lambda p: (0, 0))
     wide = jax.ShapeDtypeStruct((rows, width), f32)
     low = jax.ShapeDtypeStruct((2, rows, width), bf16)
     return pl.pallas_call(
         functools.partial(attend_kernel, layer),
-        grid=(PAIRS,),
+        grid=(STEPS,),
         in_specs=[
             slab,
             slab,
@@ -699,8 +762,8 @@
             second,
             second,
             heads,
-            whole,
-            pl.BlockSpec((1, width, width), lambda p: (layer, 0, 0)),
+            anywhere,
+            anywhere,
             full(attn_bias),
             full(gain),
             full(shift),
@@ -712,6 +775,11 @@
             whole,
         ],
         out_shape=[jax.ShapeDtypeStruct((HEADS, ROWS, KEYS), bf16), low, wide, wide],
+        scratch_shapes=[
+            pltpu.VMEM((rows, width), f32),
+            pltpu.VMEM((width, width), bf16),
+            pltpu.SemaphoreType.DMA((2,)),
+        ],
         compiler_params=pltpu.CompilerParams(vmem_limit_bytes=50 * MIB),
         cost_estimate=brief,
         name="attend",
@@ -721,42 +789,44 @@
 def attend_back_kernel(q_ref, ko, kp, vo, vp, dc_ref, soft, *rest):
     ds, *grads = rest[-6:]
     scale = HEAD_DIM**-0.5
-    q = q_ref[...]
-    dc = dc_ref[...]
-    keys = whole_page(ko[...], kp[...])
-    values = whole_page(vo[...], vp[...])
     first = lax.broadcasted_iota(jnp.int32, (ROWS, LANES), 1) < HEAD_DIM
-    q_turned = jnp.transpose(q.astype(f32), (1, 0)).astype(bf16)
-    dc_turned = jnp.transpose(dc.astype(f32), (1, 0)).astype(bf16)
-    dq_parts, dk_parts, dv_parts = [], [], []
-    for head in range(2):
-        span = slice(head * HEAD_DIM, (head + 1) * HEAD_DIM)
-        mine = jnp.where(first if head == 0 else ~first, dc, jnp.zeros_like(dc))
-        weights = soft[head]
-        weights_f = weights.astype(f32)
-        flow = nt_dot(mine, values)
-        share = jnp.sum(weights_f * flow, axis=1, keepdims=True)
-        score_grad = (weights_f * (flow - share)).astype(bf16)
-        ds[head] = score_grad
-        dq_parts.append(jnp.dot(score_grad, keys, preferred_element_type=f32))
-        dk_parts.append(jnp.dot(q_turned[span], score_grad, preferred_element_type=f32))
-        dv_parts.append(jnp.dot(dc_turned[span], weights, preferred_element_type=f32))
-    grads[0][...] = (jnp.where(first, dq_parts[0], dq_parts[1]) * scale).astype(bf16)
-    own, other = page_split(jnp.transpose(jnp.concatenate(dk_parts, axis=0) * scale, (1, 0)))
-    grads[1][...] = own.astype(bf16)
-    grads[2][...] = other.astype(bf16)
-    own, other = page_split(jnp.transpose(jnp.concatenate(dv_parts, axis=0), (1, 0)))
-    grads[3][...] = own.astype(bf16)
-    grads[4][...] = other.astype(bf16)
+    for part in range(SLABS):
+        lanes = slice(part * LANES, (part + 1) * LANES)
+        q = q_ref[:, lanes]
+        dc = dc_ref[:, lanes]
+        keys = whole_page(ko[:, lanes], kp[:, lanes])
+        values = whole_page(vo[:, lanes], vp[:, lanes])
+        q_turned = jnp.transpose(q.astype(f32), (1, 0)).astype(bf16)
+        dc_turned = jnp.transpose(dc.astype(f32), (1, 0)).astype(bf16)
+        dq_parts, dk_parts, dv_parts = [], [], []
+        for head in range(2):
+            span = slice(head * HEAD_DIM, (head + 1) * HEAD_DIM)
+            mine = jnp.where(first if head == 0 else ~first, dc, jnp.zeros_like(dc))
+            weights = soft[2 * part + head]
+            weights_f = weights.astype(f32)
+            flow = nt_dot(mine, values)
+            share = jnp.sum(weights_f * flow, axis=1, keepdims=True)
+            score_grad = (weights_f * (flow - share)).astype(bf16)
+            ds[2 * part + head] = score_grad
+            dq_parts.append(jnp.dot(score_grad, keys, preferred_element_type=f32))
+            dk_parts.append(jnp.dot(q_turned[span], score_grad, preferred_element_type=f32))
+            dv_parts.append(jnp.dot(dc_turned[span], weights, preferred_element_type=f32))
+        grads[0][:, lanes] = (jnp.where(first, dq_parts[0], dq_parts[1]) * scale).astype(bf16)
+        own, other = page_split(jnp.transpose(jnp.concatenate(dk_parts, axis=0) * scale, (1, 0)))
+        grads[1][:, lanes] = own.astype(bf16)
+        grads[2][:, lanes] = other.astype(bf16)
+        own, other = page_split(jnp.transpose(jnp.concatenate(dv_parts, axis=0), (1, 0)))
+        grads[3][:, lanes] = own.astype(bf16)
+        grads[4][:, lanes] = other.astype(bf16)
 
 
 def attend_back(q, kv, other_kv, dctx, soft, after=()):
-    slab = pl.BlockSpec((ROWS, LANES), lambda p: (0, p))
-    second = pl.BlockSpec((ROWS, LANES), lambda p: (0, p + PAIRS))
-    heads = pl.BlockSpec((2, ROWS, KEYS), lambda p: (p, 0, 0))
+    slab = pl.BlockSpec((ROWS, SLABS * LANES), lambda p: (0, p))
+    second = pl.BlockSpec((ROWS, SLABS * LANES), lambda p: (0, p + STEPS))
+    heads = pl.BlockSpec((2 * SLABS, ROWS, KEYS), lambda p: (p, 0, 0))
     return pl.pallas_call(
         attend_back_kernel,
-        grid=(PAIRS,),
+        grid=(STEPS,),
         in_specs=[slab, slab, slab, second, second, slab, heads]
         + [pl.BlockSpec(memory_space=pl.ANY)] * len(after),
         out_specs=[heads] + [slab] * 5,
@@ -775,7 +845,11 @@
     width = x_ref.shape[1]
     blocks, (bias, n_ref, out_bias, gain, shift), rest = refs[:BLOCKS], refs[BLOCKS:][:5], refs[BLOCKS + 5 :]
     units = blocks[0].shape[1]
-    own_act, mate_act, slope, residual = rest[-7 if more else -5 :][:4]
+    if more:
+        weight, attn_bias, *rest, weight_s, semaphores = rest
+        later = Later([(weight.at[layer + 1], weight_s)], semaphores)
+        pl.when(step == 0)(later.start)
+    own_act, mate_act, slope, residual = rest[:4]
     x = x_ref[...]
 
     total = None
@@ -804,11 +878,11 @@
         states = centred(residual[...])[0] * gain[layer, 1:2, :] + shift[layer, 1:2, :]
         rounded = states.astype(bf16)
         if more:
-            weight, attn_bias = rest[:2]
             wide, query, shared = rest[-3:]
             wide[...] = states
+            later.wait(0)
             project = lambda index: jnp.dot(
-                rounded, weight[0, index], preferred_element_type=f32
+                rounded, weight_s[index], preferred_element_type=f32
             )
             query[...] = (project(0) + attn_bias[layer + 1, 0:1, :]).astype(bf16)
             shared[:, :width] = project(1).astype(bf16)
@@ -855,7 +929,7 @@
     if more:
         inputs += [qkv_weight, attn_bias]
         in_specs += [
-            pl.BlockSpec((1, 3, width, width), lambda i, me: (layer + 1, 0, 0, 0)),
+            anywhere,
             full(attn_bias),
         ]
         out_specs += [whole, whole, pl.BlockSpec((rows, 3 * width), lambda i, me: (0, 0))]
@@ -867,7 +941,16 @@
         functools.partial(ffn_kernel, layer, more),
         out_shape=out_shape,
         grid_spec=pltpu.PrefetchScalarGridSpec(
-            num_scalar_prefetch=1, grid=(groups // BLOCKS,), in_specs=in_specs, out_specs=out_specs
+            num_scalar_prefetch=1,
+            grid=(groups // BLOCKS,),
+            in_specs=in_specs,
+            out_specs=out_specs,
+            scratch_shapes=[
+                pltpu.VMEM((3, width, width), bf16),
+                pltpu.SemaphoreType.DMA((1,)),
+            ]
+            if more
+            else [],
         ),
         compiler_params=pltpu.CompilerParams(vmem_limit_bytes=50 * MIB),
         cost_estimate=brief,
@@ -877,13 +960,15 @@
 
 def ffn_back_kernel(layer, me, grad_ref, r2_ref, r1_ref, *refs):
     blocks, (slope, gain, out_weight), rest = refs[:BLOCKS], refs[BLOCKS:][:3], refs[BLOCKS + 3 :]
-    own_dh, mate_dh, low_grads, bias_grad, sums, dx, dctx, total_s = rest
+    own_dh, mate_dh, low_grads, bias_grad, sums, dx, dctx, total_s, r1_s, weight_s, semaphores = rest
+    later = Later([(r1_ref, r1_s), (out_weight.at[layer], weight_s)], semaphores)
     step = pl.program_id(0)
     width = r2_ref.shape[1]
     column = lambda block: jnp.sum(block, axis=0, keepdims=True)
 
     @pl.when(step == 0)
     def _():
+        later.start()
         grad, gain_grad, shift_grad = norm_back(
             grad_ref[...].astype(f32), r2_ref[...], gain[layer, 1:2, :]
         )
@@ -908,11 +993,12 @@
 
     @pl.when(step == pl.num_programs(0) - 1)
     def _():
-        grad, gain_grad, shift_grad = norm_back(total_s[...], r1_ref[...], gain[layer, 0:1, :])
+        later.wait(0, 1)
+        grad, gain_grad, shift_grad = norm_back(total_s[...], r1_s[...], gain[layer, 0:1, :])
         low = grad.astype(bf16)
         dx[...] = grad
         low_grads[1] = low
-        dctx[...] = nt_dot(low, out_weight[0]).astype(bf16)
+        dctx[...] = nt_dot(low, weight_s[...]).astype(bf16)
         put_row(sums, 3, gain_grad)
         put_row(sums, 4, shift_grad)
         put_row(sums, 5, column(low.astype(f32)))
@@ -941,11 +1027,11 @@
             in_specs=[
                 whole,
                 whole,
-                whole,
+                anywhere,
                 *weight_blocks(layer, units, width),
                 pl.BlockSpec((BLOCKS, rows, units), lambda i, me: (i, 0, 0)),
                 full(gain),
-                pl.BlockSpec((1, width, width), lambda i, me: (layer, 0, 0)),
+                anywhere,
             ],
             out_specs=[
                 half,
@@ -956,7 +1042,12 @@
                 whole,
                 whole,
             ],
-            scratch_shapes=[pltpu.VMEM((rows, width), f32)],
+            scratch_shapes=[
+                pltpu.VMEM((rows, width), f32),
+                pltpu.VMEM((rows, width), f32),
+                pltpu.VMEM((width, width), bf16),
+                pltpu.SemaphoreType.DMA((2,)),
+            ],
         ),
         compiler_params=pltpu.CompilerParams(vmem_limit_bytes=50 * MIB),
         cost_estimate=brief,
@@ -967,8 +1058,8 @@
 def ffn_grads_kernel(me, n, n_mate, dy, dy_mate, dh, dh_mate, act, act_mate, *rest):
     near_keep, near_send, seq_keep, seq_send, n_s, dy_s = rest[-6:]
     rows, width = n.shape
+    far, units = near_keep.shape[:2]
     step = pl.program_id(0)
-    near = step < pl.num_programs(0) // 2
 
     @pl.when(step == 0)
     def _():
@@ -976,21 +1067,26 @@
             target[:rows] = own[...]
             target[rows:] = mate[...]
 
-    both = lambda own, mate: jnp.concatenate([own[0], mate[0]], axis=0)
-    into = tn_dot(both(dh, dh_mate), n_s[...]).astype(bf16)
-
-    @pl.when(near)
-    def _():
-        near_keep[0] = into
-
-    @pl.when(jnp.logical_not(near))
-    def _():
-        near_send[0] = into
-
-    out = tn_dot(both(act, act_mate), dy_s[...]).astype(bf16)
+    def product(own, mate, right):
+        turned = [
+            jnp.transpose(jnp.concatenate([own[i, 0], mate[i, 0]], axis=0), (1, 0))
+            for i in range(far)
+        ]
+        return jnp.dot(
+            jnp.concatenate(turned, axis=0), right[...], preferred_element_type=f32
+        ).astype(bf16)
+
+    def put(target, values):
+        for i in range(far):
+            target[(me[0] >> 2) ^ i] = values[i * units : (i + 1) * units]
+
+    into = product(dh, dh_mate, n_s)
+    pl.when(step == 0)(lambda: put(near_keep, into))
+    pl.when(step == 1)(lambda: put(near_send, into))
+    out = product(act, act_mate, dy_s)
     turn = me[1] % 2 == 0
-    seq_keep[0] = jnp.where(turn, out[:, : width // 2], out[:, width // 2 :])
-    seq_send[0] = jnp.where(turn, out[:, width // 2 :], out[:, : width // 2])
+    put(seq_keep, jnp.where(turn, out[:, : width // 2], out[:, width // 2 :]))
+    put(seq_send, jnp.where(turn, out[:, width // 2 :], out[:, : width // 2]))
 
 
 def ffn_grads(me, pair, pair_mate, low_grads, low_grads_mate, dh, dh_mate, act, act_mate):
@@ -998,42 +1094,40 @@
     width = pair.shape[2]
     far = groups // 2
     row_block = lambda which: pl.BlockSpec((None, rows, width), lambda i, me: (which, 0, 0))
-    hidden = pl.BlockSpec((1, rows, units), lambda i, me: ((i % far) * 2 + i // far, 0, 0))
-    place = lambda i, me: (me[0] >> 2) ^ i
+    hidden = pl.BlockSpec((far, 1, rows, units), lambda i, me: (0, i, 0, 0))
     near_shape = jax.ShapeDtypeStruct((far, units, width), bf16)
+    near_block = pl.BlockSpec((far, units, width), lambda i, me: (0, 0, 0))
     seq_shape = jax.ShapeDtypeStruct((groups, units, width // 2), bf16)
-    seq_block = pl.BlockSpec(
-        (1, units, width // 2), lambda i, me: (i // far * far + place(i % far, me), 0, 0)
-    )
+    seq_block = pl.BlockSpec((far, units, width // 2), lambda i, me: (i, 0, 0))
+    by_far = lambda block: block.reshape(far, 2, rows, units)
     return pl.pallas_call(
         ffn_grads_kernel,
         out_shape=[near_shape, near_shape, seq_shape, seq_shape],
         grid_spec=pltpu.PrefetchScalarGridSpec(
             num_scalar_prefetch=1,
-            grid=(groups,),
+            grid=(2,),
             in_specs=[row_block(1), row_block(1), row_block(0), row_block(0)] + [hidden] * 4,
-            out_specs=[
-                pl.BlockSpec(
-                    (1, units, width), lambda i, me: (place(jnp.minimum(i, far - 1), me), 0, 0)
-                ),
-                pl.BlockSpec(
-                    (1, units, width), lambda i, me: (place(jnp.maximum(i - far, 0), me), 0, 0)
-                ),
-                seq_block,
-                seq_block,
-            ],
+            out_specs=[near_block, near_block, seq_block, seq_block],
             scratch_shapes=[pltpu.VMEM((2 * rows, width), bf16)] * 2,
         ),
         compiler_params=pltpu.CompilerParams(vmem_limit_bytes=50 * MIB),
         cost_estimate=brief,
         name="feed_forward_grads",
-    )(me, pair, pair_mate, low_grads, low_grads_mate, dh, dh_mate, act, act_mate)
+    )(
+        me,
+        pair,
+        pair_mate,
+        low_grads,
+        low_grads_mate,
+        *[by_far(block) for block in (dh, dh_mate, act, act_mate)],
+    )
 
 
 def projection_kernel(by_distance, me, x, x_mate, ctx, ctx_mate, *refs):
     own, mate, refs = refs[:5], refs[5:10], refs[10:]
     da, da_mate, dr_ref, weight = refs[:4]
-    near_keep, near_send, seq_keep, seq_send, dx, sums, turned_s, left_s, right_s, shards_s = refs[-10:]
+    near_keep, near_send, seq_keep, seq_send, dx, sums = refs[-11:-5]
+    turned_s, picked_s, left_s, right_s, shards_s = refs[-5:]
     step = pl.program_id(0)
     far, shard = near_keep.shape[:2]
     rows, width = x.shape
@@ -1043,48 +1137,51 @@
         far_place = (me[0] >> 2) ^ place if by_distance else place
         return far_place * 4 + ((me[0] & 3) ^ (2 * near))
 
+    gap = -rows % LANES
+    mate_rows = slice(rows + gap, 2 * rows + gap)
+
     def pick_left(first, second):
-        for index, block in enumerate((first, second)):
+        for block, at_rows in ((first, slice(0, rows)), (second, mate_rows)):
             turned_s[...] = jnp.transpose(block[...].astype(f32), (1, 0))
             for near in range(2):
                 for place in range(far):
                     start = pl.multiple_of(place_of(place, near) * shard, 8)
                     at = (near * far + place) * shard
-                    left_s[index, at : at + shard, :] = turned_s[pl.ds(start, shard), :]
+                    picked_s[at : at + shard, at_rows] = turned_s[pl.ds(start, shard), :]
+        left_s[...] = picked_s[...].astype(bf16)
 
     @pl.when(step == 0)
     def _():
         dx[...] = dr_ref[...]
+        picked_s[:, rows : rows + gap] = jnp.zeros((width // 2, gap), f32)
+        right_s[rows : rows + gap] = jnp.zeros((gap, width), bf16)
         pick_left(x, x_mate)
-        right_s[0] = own[0][...]
-        right_s[1] = mate[0][...]
+        right_s[:rows] = own[0][...]
+        right_s[mate_rows] = mate[0][...]
         put_row(sums, 0, column(own[0][...]))
 
     for index in (1, 2):
 
         @pl.when(step == index)
         def _():
-            right_s[0] = add_low(own[2 * index - 1][...], mate[2 * index][...])
-            right_s[1] = add_low(mate[2 * index - 1][...], own[2 * index][...])
+            right_s[:rows] = add_low(own[2 * index - 1][...], mate[2 * index][...])
+            right_s[mate_rows] = add_low(mate[2 * index - 1][...], own[2 * index][...])
 
     @pl.when(step == 2)
     def _():
-        put_row(sums, 1, column(right_s[0]))
+        put_row(sums, 1, column(right_s[:rows]))
 
     @pl.when(step < 3)
     def _():
-        dx[...] += nt_dot(right_s[0], weight[0, 0])
+        dx[...] += nt_dot(right_s[:rows], weight[0, 0])
 
     @pl.when(step == 3)
     def _():
         pick_left(ctx, ctx_mate)
-        right_s[0] = da[...]
-        right_s[1] = da_mate[...]
-
-    shards_s[...] = sum(
-        jnp.dot(left_s[index].astype(bf16), right_s[index], preferred_element_type=f32)
-        for index in range(2)
-    )
+        right_s[:rows] = da[...]
+        right_s[mate_rows] = da_mate[...]
+
+    shards_s[...] = jnp.dot(left_s[...], right_s[...], preferred_element_type=f32)
 
     def put(target, first, near, columns):
         for place in range(far):
@@ -1165,8 +1262,9 @@
             ],
             scratch_shapes=[
                 pltpu.VMEM((width, rows), f32),
-                pltpu.VMEM((2, width // 2, rows), f32),
-                pltpu.VMEM((2, rows, width), bf16),
+                pltpu.VMEM((width // 2, 2 * rows + -rows % LANES), f32),
+                pltpu.VMEM((width // 2, 2 * rows + -rows % LANES), bf16),
+                pltpu.VMEM((2 * rows + -rows % LANES, width), bf16),
                 pltpu.VMEM((width // 2, width), f32),
             ],
         ),
@@ -1193,17 +1291,26 @@
     return jnp.where(turn, mine, other), jnp.where(turn, other, mine)
 
 
-def projection_out_kernel(me, *refs):
+def stacked_parts(block, start, rows, count):
+    return jnp.concatenate(
+        [block[start + i * rows : start + (i + 1) * rows] for i in range(count)], axis=1
+    )
+
+
+def projection_out_kernel(starts, me, *refs):
     qkv, out = refs[-2:]
-    shard, width = out.shape[1:]
+    rows, width = out.shape[1:]
     for layer in range(LAYERS):
         mine, other = refs[2 * layer : 2 * layer + 2]
+        count = width // mine.shape[1]
         first, second = ordered(me[1] % 2 == 0, mine[...], other[...])
-        low, high = first[:shard].astype(f32), second[:shard].astype(f32)
-        qkv[layer, 0] = low
-        qkv[layer, 1] = high
-        qkv[layer, 2] = first[shard:].astype(f32)
-        out[layer] = second[shard:].astype(f32)
+        take = lambda block, part: stacked_parts(
+            block, starts[layer] + part * rows * count, rows, count
+        ).astype(f32)
+        qkv[layer, 0] = take(first, 0)
+        qkv[layer, 1] = take(second, 0)
+        qkv[layer, 2] = take(first, 1)
+        out[layer] = take(second, 1)
 
 
 def ffn_out_kernel(me, *refs):
@@ -1214,7 +1321,7 @@
         for index, part in enumerate(ordered(me[1] % 2 == 0, mine[...], other[...])):
             columns = slice(index * (width // 2), (index + 1) * (width // 2))
             into[layer, :, columns] = part[:units].astype(f32)
-            out[layer, :, columns] = part[units:].astype(f32)
+            out[layer, :, columns] = part[units : 2 * units].astype(f32)
 
 
 def write_out(kernel, name, me, parts, shapes):
@@ -1352,7 +1459,7 @@
         if not last:
             weights = tied(weights, projections[-1].underway() + ffns[-1].underway())
             projections[-1].second(weights[0])
-            ffns[-1].scatter(weights[0])
+            upper = Scattered([ffns[-1]], weights[0])
         ffns[layer] = Shards(*weights)
         *weights, gradient, projection_rows[layer] = projection_grads(
             not last,
@@ -1386,42 +1493,38 @@
     folds = [fold(0, after=vis_sums.lefts)]
     folds[0], *weights = tied(
         (folds[0], *weights),
-        ffns[0].underway() + projections[-1].underway() + vis_sums.rights + [ffns[-1].shard],
+        ffns[0].underway() + projections[-1].underway() + vis_sums.rights + [upper.shard],
     )
     ffns[0].second(folds[0])
-    projections[-1].scatter(folds[0])
     projections[0] = Shards(*weights)
     vis_sums.step(folds[0])
     folds.append(fold(1, after=folds + vis_sums.lefts))
-    (folds[1],) = tied(
-        folds[1:], ffns[0].underway() + vis_sums.rights + [projections[-1].shard]
-    )
-    ffns[0].scatter(folds[1])
-    ffns[-1].join(folds[1])
+    (folds[1],) = tied(folds[1:], ffns[0].underway() + vis_sums.rights)
+    lower = Scattered([ffns[0], projections[-1]], folds[1])
     vis_sums.step(folds[1])
     small = join(norm_sums + projection_rows + bin_grads + [vis_rows, *folds])
     sizes = [part.shape[0] for part in norm_sums + projection_rows]
     sizes += [tp_size * bin_rows(units)] * LAYERS + [vis_rows.shape[0]]
     small_ways = [("tp", 0), ("tp", 1)] + seq_ways + far_ways
-    small_sums = Tree(small, small_ways, add=jnp.add)
+    small_sums = Tree(small, small_ways)
     small_sums.step()
     small_sums.step(*projections[0].underway())
     behind = small_sums.lefts[0]
     projections[0].second(behind)
-    projections[-1].join(behind)
     small_sums.step(*projections[0].underway(), *vis_sums.rights)
     behind = small_sums.lefts[0]
     projections[0].halve(behind)
     vis_sums.step(behind)
-    small_sums.step(projections[0].came, *vis_sums.rights)
+    upper.join(behind)
+    small_sums.step(*vis_sums.rights, upper.other)
     behind = small_sums.lefts[0]
     for _ in range(mesh_bits("tp") - 3):
         projections[0].halve_more(behind)
     while vis_sums.steps:
         vis_sums.step(behind)
-    ffns[0].join(behind)
+    lower.join(behind)
     while small_sums.steps:
-        small_sums.step(projections[0].came)
+        small_sums.step(lower.shard)
     behind = small_sums.lefts[0]
     projections[0].halve_more(behind)
     projections[0].join()
@@ -1451,17 +1554,17 @@
     bn_gain_grad, bn_shift_grad, bin_total, grad_maps = rest
     shard = width // tp_size
     qkv_total, out_total = write_out(
-        projection_out_kernel,
+        functools.partial(projection_out_kernel, (0, 2 * units)),
         "projections_out",
         me,
-        [part for shards in projections for part in (shards.shard, shards.other)],
+        [part for sums in (projections[0], lower) for part in (sums.shard, sums.other)],
         [(LAYERS, 3, shard, width), (LAYERS, shard, width)],
     )
     in_total, down_total = write_out(
         ffn_out_kernel,
         "feed_forward_out",
         me,
-        [part for shards in ffns for part in (shards.shard, shards.other)],
+        [part for sums in (lower, upper) for part in (sums.shard, sums.other)],
         [(LAYERS, units, width)] * 2,
     )
     return (

time: 408 us -> 398 us (0.975)
  Pallas kernels: 204 us -> 188 us
    pallas_call x2, Pallas kernels: 24.4 us -> 18 us  [fold_table(): pl.pallas_call(table_kernel, out_shape=jax.ShapeDtypeStruct((count, 8, LA...]
    convert_element_type x21 -> x23, other arithmetic: 11.9 us -> 16.2 us  [add_low(): return (left.astype(f32) + right.astype(f32)).astype(bf16)]
    ppermute x59 -> x58, starting transfers between devices: 48.9 us -> 52.4 us  [flipped(): return lax.ppermute(block, axis, [(i, i ^ 1 << bit) for i in range(count)])]
    unnamed x185 -> x186, local copies, waits for them, and re-layouts: 19.9 us -> 22.3 us
    ppermute x59 -> x58, waiting for transfers between devices: 47.7 us -> 48.7 us  [flipped(): return lax.ppermute(block, axis, [(i, i ^ 1 << bit) for i in range(count)])]
  transfers between devices with their start and end apart: 63 -> 61, of which waited for: 23 -> 22; matrix products, arithmetic and copies ran while one was open for 6% -> 6% of each run, Pallas kernels for 37% -> 35%
where the time goes in v1:
time: 398 us; the launch traced here: 395 us
  Pallas kernels  188 us (47%)
  waiting for transfers between devices  86.4 us (22%)
  starting transfers between devices  52.5 us (13%)
  local copies, waits for them, and re-layouts  23.9 us (6%)
  other arithmetic  23 us (6%)
  between operations  15.2 us (4%)
  matrix products  5.82 us (1%)
    ppermute x58, starting transfers between devices, flipped(): return lax.ppermute(block, axis, [(i, i ^ 1 << bit) for i in range(count)])  52.4 us
    ppermute x58, waiting for transfers between devices, flipped(): return lax.ppermute(block, axis, [(i, i ^ 1 << bit) for i in range(count)])  48.7 us
    all_gather x1, waiting for transfers between devices, body(): gathered = lax.all_gather(packed, 'tp', axis=0)  37.6 us
    pallas_call x2, Pallas kernels, ffn(): pl.pallas_call(functools.partial(ffn_kernel, layer, more), out_shape=out_...  25.7 us
    pallas_call x2, Pallas kernels, ffn_back(): pl.pallas_call(functools.partial(ffn_back_kernel, layer), out_shape=[half...  24.3 us
    pallas_call x2, Pallas kernels, attend(): pl.pallas_call(functools.partial(attend_kernel, layer), grid=(STEPS,), in...  23.7 us
    pallas_call x2, Pallas kernels, projection_grads(): pl.pallas_call(functools.partial(projection_kernel, by_distance), out_sha...  22.8 us
    unnamed x186, local copies, waits for them, and re-layouts  22.3 us
  transfers between devices with their start and end apart: 61, of which 22 were waited for; matrix products, arithmetic and copies ran while one was open for 6% of the time, Pallas kernels for 35%

profile of v1, /device:TPU:0, one launch (start us, length us, event | category | flops | bytes accessed | tf_op | source)
XLA Modules:
  0.0 394.8 jit_solution(7125815705479292000)
XLA Ops:
  7.2 1.3 pad_maximum_fusion.1
  11.9 2.9 collective-permute-start.1
  14.8 1.6 collective-permute-done.1
  16.4 2.1 collective-permute-start.2
  18.5 1.6 collective-permute-done.2
  20.1 3.0 collective-permute-start.3
  23.1 1.7 collective-permute-done.3
  24.8 1.8 collective-permute-start.4
  26.7 1.7 collective-permute-done.4
  30.0 2.0 convolution_convert_fusion
  31.9 1.8 fusion.2
  40.5 21.3 %score_bias.1.bias = f32[12,288,640]{2,1,0:T(8,128)} custom-call(s32[2]{0:T(128)S(1)} %pad_add_fusion.1.facts, s32[2,256]{1,0:T(2,128)S(1)} %copy-done.45, s32[2,256]{1,0:T(2,128)S(1)} %collective-permute-done.6.other_boxes, f32[12,8,128]{2,1,0:T(8,128)S(1)} %broadcast_in_dim.42.table_a, f32[12,8,128]{2,1,0:T(8,128)S(1)} %broadcast_in_dim.43.table_b), custom_call_target="tpu_custom_call" | custom-call | flops 1 | bytes 1 | tf_op jit(solution)/shard_map/score_bias/pallas_call | solution.py:246
  62.8 1.8 fusion.1.q_ref
  64.7 12.0 %attend.2 = (bf16[12,288,640]{2,1,0:T(8,128)(2,1)}, bf16[2,288,768]{2,1,0:T(8,128)(2,1)S(1)}, f32[288,768]{1,0:T(8,128)S(1)}, f32[288,768]{1,0:T(8,128)S(1)}) custom-call(bf16[288,768]{1,0:T(8,128)(2,1)S(1)} %fusion.1.q_ref, bf16[288,2304]{1,0:T(8,128)(2,1)} %copy-done.46, bf16[288,2304]{1,0:T(8,128)(2,1)} %collective-permute-done.5.kp.vp.x_mate, ...), custom_call_target="tpu_custom_call" | custom-call | flops 1 | bytes 1 | tf_op jit(solution)/shard_map/attend/pallas_call | solution.py:755
  77.7 37.6 %all-gather.3.cloned.1.call-done = bf16[6400,1536]{1,0:T(8,128)(2,1)} async-done(((bf16[400,1536]{1,0:T(8,128)(2,1)}), bf16[6400,1536]{1,0:T(8,128)(2,1)}) %all-gather.3.cloned.1.call-update) | async-done | bytes 19660816 | tf_op jit(solution)/shard_map/all_gather | solution.py:1378
  115.3 13.6 %feed_forward.2 = (bf16[8,288,192]{2,1,0:T(8,128)(2,1)}, bf16[8,288,192]{2,1,0:T(8,128)(2,1)}, bf16[16,288,192]{2,1,0:T(8,128)(2,1)}, f32[288,768]{1,0:T(8,128)S...) custom-call(s32[2]{0:T(128)S(1)} %pad_add_fusion.me, ...), custom_call_target="tpu_custom_call" | custom-call | flops 1 | bytes 1 | tf_op jit(solution)/shard_map/feed_forward/pallas_call | solution.py:940
  129.3 3.0 collective-permute-done.7.kp.vp.x_mate
  133.4 11.7 %attend.3 = (bf16[12,288,640]{2,1,0:T(8,128)(2,1)}, bf16[2,288,768]{2,1,0:T(8,128)(2,1)S(1)}, f32[288,768]{1,0:T(8,128)S(1)}, f32[288,768]{1,0:T(8,128)S(1)}) custom-call(bf16[288,768]{1,0:T(8,128)(2,1)S(1)} %get-tuple-element.200.q_ref, bf16[288,2304]{1,0:T(8,128)(2,1)} %get-tuple-element.201.ko.vo.x, bf16[288,2304]{1,0:T(8,128)(2,1)} %copy-done.47, ...), custom_call_target="tpu_custom_call" | custom-call | flops 1 | bytes 1 | tf_op jit(solution)/shard_map/attend/pallas_call | solution.py:755
  145.1 12.1 %feed_forward.3 = (bf16[8,288,192]{2,1,0:T(8,128)(2,1)S(1)}, bf16[8,288,192]{2,1,0:T(8,128)(2,1)}, bf16[16,288,192]{2,1,0:T(8,128)(2,1)}, f32[288,768]{1,0:T(8,128)S(1)}, bf16[288,768]{1,0:T(8,128)(2,1)}) custom-call(s32[2]{0:T(128)S(1)} %pad_add_fusion.me, bf16[2,288,768]{2,1,0:T(8,128)(2,1)S(1)} %get-tuple-element.203.x_ref.ctx.n, ...), custom_call_target="tpu_custom_call" | custom-call | flops 1 | bytes 1 | tf_op jit(solution)/shard_map/feed_forward/pallas_call | solution.py:940
  158.3 12.2 %feed_forward_back.2 = (bf16[8,288,192]{2,1,0:T(8,128)(2,1)}, bf16[8,288,192]{2,1,0:T(8,128)(2,1)}, bf16[2,288,768]{2,1,0:T(8,128)(2,1)S(1)}, f32[16,1,192]{2,1,...) custom-call(s32[2]{0:T(128)S(1)} %pad_add_fusion.me, ...), custom_call_target="tpu_custom_call" | custom-call | flops 1 | bytes 1 | tf_op jit(solution)/shard_map/feed_forward_back/pallas_call | solution.py:1013
  172.5 10.6 %attend_back.2 = (bf16[12,288,640]{2,1,0:T(8,128)(2,1)}, bf16[288,768]{1,0:T(8,128)(2,1)S(1)}, bf16[288,768]{1,0:T(8,128)(2,1)S(1)}, bf16[288,768]{1,0:T(8,128)(...) custom-call(bf16[288,768]{1,0:T(8,128)(2,1)S(1)} %get-tuple-element.200.q_ref, ...), custom_call_target="tpu_custom_call" | custom-call | flops 1 | bytes 1 | tf_op jit(solution)/shard_map/attend_back/pallas_call | solution.py:827
  184.7 9.8 %feed_forward_grads.2 = (bf16[4,192,768]{2,1,0:T(8,128)(2,1)}, bf16[4,192,768]{2,1,0:T(8,128)(2,1)}, bf16[8,192,384]{2,1,0:T(8,128)(2,1)}, bf16[8,192,384]{2,1,0:T(8,128)(2,1)}) custom-call(s32[2]{0:T(128)S(1)} %pad_add_fusion.me, bf16[2,288,768]{2,1,0:T(8,128)(2,1)S(1)} %get-tuple-element.203.x_ref.ctx.n, ...), custom_call_target="tpu_custom_call" | custom-call | flops 1 | bytes 1 | tf_op jit(solution)/shard_map/feed_forward_grads/pallas_call | solution.py:1103
  194.5 1.3 collective-permute-start.18
  195.9 1.5 collective-permute-start.19
  201.2 11.7 %projection_grads.2 = (bf16[4,48,1536]{2,1,0:T(8,128)(2,1)}, bf16[4,48,1536]{2,1,0:T(8,128)(2,1)}, bf16[8,48,768]{2,1,0:T(8,128)(2,1)}, bf16[8,48,768]{2,1,0:T(8...) custom-call(s32[2]{0:T(128)S(1)} %pad_add_fusion.me, bf16[288,2304]{1,0:T(8,128)(2,1)} %get-tuple-element.201.ko.vo.x, ...), custom_call_target="tpu_custom_call" | custom-call | flops 1 | bytes 1 | tf_op jit(solution)/shard_map/projection_grads/pallas_call | solution.py:1234
  214.1 12.1 %feed_forward_back.3 = (bf16[8,288,192]{2,1,0:T(8,128)(2,1)}, bf16[8,288,192]{2,1,0:T(8,128)(2,1)}, bf16[2,288,768]{2,1,0:T(8,128)(2,1)S(1)}, f32[16,1,192]{2,1,...) custom-call(s32[2]{0:T(128)S(1)} %pad_add_fusion.me, ...), custom_call_target="tpu_custom_call" | custom-call | flops 1 | bytes 1 | tf_op jit(solution)/shard_map/feed_forward_back/pallas_call | solution.py:1013
  230.2 2.0 add_convert_fusion.8
  232.2 1.8 add_convert_fusion.9
  235.9 1.5 collective-permute-start.31
  237.4 10.6 %attend_back.3 = (bf16[12,288,640]{2,1,0:T(8,128)(2,1)}, bf16[288,768]{1,0:T(8,128)(2,1)S(1)}, bf16[288,768]{1,0:T(8,128)(2,1)S(1)}, bf16[288,768]{1,0:T(8,128)(...) custom-call(bf16[288,768]{1,0:T(8,128)(2,1)S(1)} %copy-done.11, bf16[288,2304]{1,0:T(8,128)(2,1)} %copy-done.46, ...), custom_call_target="tpu_custom_call" | custom-call | flops 1 | bytes 1 | tf_op jit(solution)/shard_map/attend_back/pallas_call | solution.py:827
  249.8 10.0 %feed_forward_grads.3 = (bf16[4,192,768]{2,1,0:T(8,128)(2,1)}, bf16[4,192,768]{2,1,0:T(8,128)(2,1)}, bf16[8,192,384]{2,1,0:T(8,128)(2,1)}, bf16[8,192,384]{2,1,0:T(8,128)(2,1)}) custom-call(s32[2]{0:T(128)S(1)} %pad_add_fusion.me, bf16[2,288,768]{2,1,0:T(8,128)(2,1)S(1)} %get-tuple-element.194.x_ref.ctx.n, ...), custom_call_target="tpu_custom_call" | custom-call | flops 1 | bytes 1 | tf_op jit(solution)/shard_map/feed_forward_grads/pallas_call | solution.py:1103
  260.0 2.4 collective-permute-done.31
  267.8 2.2 add_convert_fusion.16
  271.6 11.1 %projection_grads.3 = (bf16[4,48,1536]{2,1,0:T(8,128)(2,1)}, bf16[4,48,1536]{2,1,0:T(8,128)(2,1)}, bf16[8,48,768]{2,1,0:T(8,128)(2,1)}, bf16[8,48,768]{2,1,0:T(8...) custom-call(s32[2]{0:T(128)S(1)} %pad_add_fusion.me, bf16[288,2304]{1,0:T(8,128)(2,1)} %copy-done.46, ...), custom_call_target="tpu_custom_call" | custom-call | flops 1 | bytes 1 | tf_op jit(solution)/shard_map/projection_grads/pallas_call | solution.py:1234
  282.8 2.2 visual_back.1
  285.3 1.5 collective-permute-start.35
  286.9 1.6 collective-permute-start.37
  288.5 9.0 %table_grad.2.rest_0_.refs_7_ = f32[6,8,128]{2,1,0:T(8,128)} custom-call(bf16[640,256]{1,0:T(8,128)(2,1)} %copy-done.12, bf16[224,288]{1,0:T(8,128)(2,1)} %copy-done.19, bf16[4,288,640]{2,1,0:T(8,128)(2,1)} %copy-done.2, bf16[12,288,640]{2,1,0:T(8,128)(2,1)} %get-tuple-element.269.ds_a, bf16[12,288,640]{2,1,0:T(8,128)(2,1)} %get-tuple-element.270.ds_b, ...), custom_call_target="tpu_custom_call" | custom-call | flops 1 | bytes 1 | tf_op jit(solution)/shard_map/table_grad/pallas_call | solution.py:392
  297.5 2.5 collective-permute-done.36
  302.8 1.7 add_convert_fusion.3
  305.2 2.5 collective-permute-start.40
  307.7 9.0 %table_grad.3.refs_8_ = f32[6,8,128]{2,1,0:T(8,128)} custom-call(bf16[640,256]{1,0:T(8,128)(2,1)} %copy-done.12, bf16[224,288]{1,0:T(8,128)(2,1)} %copy-done.19, bf16[4,288,640]{2,1,0:T(8,128)(2,1)} %copy-done.2, bf16[12,288,640]{2,1,0:T(8,128)(2,1)} %get-tuple-element.269.ds_a, bf16[12,288,640]{2,1,0:T(8,128)(2,1)} %get-tuple-element.270.ds_b, ...), custom_call_target="tpu_custom_call" | custom-call | flops 1 | bytes 1 | tf_op jit(solution)/shard_map/table_grad/pallas_call | solution.py:392
  316.8 1.3 collective-permute-start.42
  318.1 1.5 collective-permute-start.43
  323.8 1.6 join.1
  325.4 5.1 %collective-permute-done.42 = bf16[4,48,1536]{2,1,0:T(8,128)(2,1)S(1)} collective-permute-done((bf16[4,48,1536]{2,1,0:T(8,128)(2,1)}, bf16[4,48,1536]{2,1,0:T(8,128)(2,1)S(1)}, u32[]{:S(2)}, u32[]{:S(2)}) %collective-permute-start.42) | collective-permute-done | bytes 589856 | tf_op jit(solution)/shard_map/ppermute | solution.py:46
  331.6 1.5 add_convert_fusion.37
  333.1 1.9 add_convert_fusion.12
  338.2 1.3 collective-permute-start.47
  341.3 5.6 %collective-permute-done.44 = bf16[272,128]{1,0:T(8,128)(2,1)S(1)} collective-permute-done((bf16[272,128]{1,0:T(8,128)(2,1)}, bf16[272,128]{1,0:T(8,128)(2,1)S(1)}, u32[]{:S(2)}, u32[]{:S(2)}) %collective-permute-start.44) | collective-permute-done | bytes 69664 | tf_op jit(solution)/shard_map/ppermute | solution.py:46
  347.8 1.5 collective-permute-start.48
  350.0 1.5 collective-permute-start.49
  353.0 6.2 %collective-permute-done.49 = bf16[128,768]{1,0:T(8,128)(2,1)S(1)} collective-permute-done((bf16[128,768]{1,0:T(8,128)(2,1)S(1)}, bf16[128,768]{1,0:T(8,128)(2,1)S(1)}, u32[]{:S(2)}, u32[]{:S(2)}) %collective-permute-start.49) | collective-permute-done | bytes 196640 | tf_op jit(solution)/shard_map/ppermute | solution.py:46
  359.2 2.0 collective-permute-start.51
  361.3 5.1 %collective-permute-done.53 = bf16[2,96,768]{2,1,0:T(8,128)(2,1)S(1)} collective-permute-done((bf16[2,96,768]{2,1,0:T(8,128)(2,1)S(1)}, bf16[2,96,768]{2,1,0:T(8,128)(2,1)S(1)}, u32[]{:S(2)}, u32[]{:S(2)}) %collective-permute-start.53) | collective-permute-done | bytes 294944 | tf_op jit(solution)/shard_map/ppermute | solution.py:46
  366.5 3.0 collective-permute-start.54
  369.5 1.6 collective-permute-start.56
  371.1 3.1 collective-permute-done.54
  374.3 1.7 collective-permute-start.55
  376.0 1.3 collective-permute-start.52
  378.3 3.0 collective-permute-done.52.right
  381.9 2.3 split.1
  384.3 2.1 feed_forward_out.1
  386.4 1.6 projections_out.1
  (330 shorter events, 58.2 us)
Async XLA Ops:
  7.2 108.1 %all-gather.3.cloned.1.call-start = ((), (), s32[]{:S(2)}) async-start(), calls=%async_computation.4 | async-start | bytes 20889600 | tf_op jit(solution)/shard_map/all_gather | solution.py:1378
  9.8 291.1 %reduce-scatter.3.cloned.1.call-start = ((), (), s32[]{:S(2)}) async-start(), calls=%async_computation.2 | async-start | bytes 1474560 | tf_op jit(solution)/shard_map/reduce_scatter | solution.py:140
  10.5 1.3 collective-permute-start
  11.9 4.5 %collective-permute-start.1 = (f32[2,256]{1,0:T(2,128)S(1)}, f32[2,256]{1,0:T(2,128)S(1)}, u32[]{:S(2)}, u32[]{:S(2)}) collective-permute-start(f32[2,256]{1,0:T(2,128)S(1)} %fusion.25), channel_id=1, source_target_pairs={{0,2},{1,3},{2,0},{3,1},{4,6},{5,7},{6,4},{7,5},{8,10},{9,11},{10,... | collective-permute-start | bytes 6152 | tf_op jit(solution)/shard_map/ppermute | solution.py:46
  16.4 3.7 collective-permute-start.2
  20.1 4.7 %collective-permute-start.3 = (f32[2,256]{1,0:T(2,128)S(1)}, f32[2,256]{1,0:T(2,128)S(1)}, u32[]{:S(2)}, u32[]{:S(2)}) collective-permute-start(f32[2,256]{1,0:T(2,128)S(1)} %add.241), channel_id=1, source_target_pairs={{0,8},{1,9},{2,10},{3,11},{4,12},{5,13},{6,14},{7,15},{8,0},{9,1},... | collective-permute-start | bytes 6152 | tf_op jit(solution)/shard_map/ppermute | solution.py:46
  24.8 3.6 collective-permute-start.4
  33.9 30.7 %collective-permute-start.5 = (bf16[288,2304]{1,0:T(8,128)(2,1)S(1)}, bf16[288,2304]{1,0:T(8,128)(2,1)}, u32[]{:S(2)}, u32[]{:S(2)}) collective-permute-start(bf16[288,2304]{1,0:T(8,128)(2,1)S(1)} %pad_maximum_fusion.ko.vo.x), channel_id=1, source_target_pairs={{0,1},{1,0},{2,3},{3,2},{4,5},{5,4},{6,7},{7,6},{8,9},{9,8},{10,11... | collective-permute-start | bytes 3981320 | tf_op jit(solution)/shard_map/ppermute | solution.py:46
  34.5 2.2 collective-permute-start.6
  35.9 234.9 %copy-start.36 = (s32[2]{0:T(128)}, s32[2]{0:T(128)S(1)}, u32[]{:S(2)}) copy-start(s32[2]{0:T(128)S(1)} %pad_add_fusion.me) | copy-start | bytes 28
  64.7 50.7 %copy-start.38 = (f32[2,768]{1,0:T(2,128)S(1)}, f32[2,768]{1,0:T(2,128)}, u32[]{:S(2)}) copy-start(f32[2,768]{1,0:T(2,128)} %refs_6_.5) | copy-start | bytes 18436
  77.7 171.1 %copy-start = (bf16[2,288,768]{2,1,0:T(8,128)(2,1)}, bf16[2,288,768]{2,1,0:T(8,128)(2,1)S(1)}, u32[]{:S(2)}) copy-start(bf16[2,288,768]{2,1,0:T(8,128)(2,1)S(1)} %get-tuple-element.194.x_ref.ctx.n) | copy-start | bytes 2654212
  128.9 3.3 collective-permute-start.7
  171.4 11.6 %collective-permute-start.10 = (bf16[8,288,192]{2,1,0:T(8,128)(2,1)}, bf16[8,288,192]{2,1,0:T(8,128)(2,1)S(1)}, u32[]{:S(2)}, u32[]{:S(2)}) collective-permute-start(bf16[8,288,192]{2,1,0:T(8,128)(2,1)} %get-tuple-element.216), channel_id=1, source_target_pairs={{0,1},{1,0},{2,3},{3,2},{4,5},{5,4},{6,7},{7,6},{8,9},{9,8},{10,11... | collective-permute-start | bytes 2654216 | tf_op jit(solution)/shard_map/ppermute | solution.py:46
  171.7 11.4 %collective-permute-start.11 = (bf16[2,288,768]{2,1,0:T(8,128)(2,1)S(1)}, bf16[2,288,768]{2,1,0:T(8,128)(2,1)S(1)}, u32[]{:S(2)}, u32[]{:S(2)}) collective-permute-start(bf16[2,288,768]{2,1,0:T(8,128)(2,1)S(1)} %get-tuple-element.217.refs_10_.dy), channel_id=1, source_target_pairs={{0,1},{1,0},{2,3},{3,2},{4,5},{5,4},{6,7},{7,6},{8,9},{9,8},{10,11... | collective-permute-start | bytes 2654216 | tf_op jit(solution)/shard_map/ppermute | solution.py:46
  171.9 11.1 %collective-permute-start.12 = (bf16[8,288,192]{2,1,0:T(8,128)(2,1)S(1)}, bf16[8,288,192]{2,1,0:T(8,128)(2,1)S(1)}, u32[]{:S(2)}, u32[]{:S(2)}) collective-permute-start(bf16[8,288,192]{2,1,0:T(8,128)(2,1)S(1)} %copy-done.88), channel_id=1, source_target_pairs={{0,1},{1,0},{2,3},{3,2},{4,5},{5,4},{6,7},{7,6},{8,9},{9,8},{10,11... | collective-permute-start | bytes 2654216 | tf_op jit(solution)/shard_map/ppermute | solution.py:46
  172.2 10.9 %collective-permute-start.9 = (bf16[2,288,768]{2,1,0:T(8,128)(2,1)S(1)}, bf16[2,288,768]{2,1,0:T(8,128)(2,1)S(1)}, u32[]{:S(2)}, u32[]{:S(2)}) collective-permute-start(bf16[2,288,768]{2,1,0:T(8,128)(2,1)S(1)} %get-tuple-element.203.x_ref.ctx.n), channel_id=1, source_target_pairs={{0,1},{1,0},{2,3},{3,2},{4,5},{5,4},{6,7},{7,6},{8,9},{9,8},{10,11... | collective-permute-start | bytes 2654216 | tf_op jit(solution)/shard_map/ppermute | solution.py:46
  183.1 14.2 %collective-permute-start.13 = (bf16[288,768]{1,0:T(8,128)(2,1)S(1)}, bf16[288,768]{1,0:T(8,128)(2,1)S(1)}, u32[]{:S(2)}, u32[]{:S(2)}) collective-permute-start(bf16[288,768]{1,0:T(8,128)(2,1)S(1)} %get-tuple-element.219.refs_0_), channel_id=1, source_target_pairs={{0,1},{1,0},{2,3},{3,2},{4,5},{5,4},{6,7},{7,6},{8,9},{9,8},{10,11... | collective-permute-start | bytes 1327112 | tf_op jit(solution)/shard_map/ppermute | solution.py:46
  183.4 14.4 %collective-permute-start.14 = (bf16[288,768]{1,0:T(8,128)(2,1)S(1)}, bf16[288,768]{1,0:T(8,128)(2,1)S(1)}, u32[]{:S(2)}, u32[]{:S(2)}) collective-permute-start(bf16[288,768]{1,0:T(8,128)(2,1)S(1)} %get-tuple-element.220.refs_1_), channel_id=1, source_target_pairs={{0,1},{1,0},{2,3},{3,2},{4,5},{5,4},{6,7},{7,6},{8,9},{9,8},{10,11... | collective-permute-start | bytes 1327112 | tf_op jit(solution)/shard_map/ppermute | solution.py:46
  194.5 34.8 %collective-permute-start.18 = (bf16[4,192,768]{2,1,0:T(8,128)(2,1)}, bf16[4,192,768]{2,1,0:T(8,128)(2,1)}, u32[]{:S(2)}, u32[]{:S(2)}) collective-permute-start(bf16[4,192,768]{2,1,0:T(8,128)(2,1)} %get-tuple-element.238), channel_id=1, source_target_pairs={{0,2},{1,3},{2,0},{3,1},{4,6},{5,7},{6,4},{7,5},{8,10},{9,11},{10,... | collective-permute-start | bytes 3538952 | tf_op jit(solution)/shard_map/ppermute | solution.py:46
  195.9 34.3 %collective-permute-start.19 = (bf16[8,192,384]{2,1,0:T(8,128)(2,1)}, bf16[8,192,384]{2,1,0:T(8,128)(2,1)}, u32[]{:S(2)}, u32[]{:S(2)}) collective-permute-start(bf16[8,192,384]{2,1,0:T(8,128)(2,1)} %get-tuple-element.239), channel_id=1, source_target_pairs={{0,16},{16,0},{1,17},{17,1},{2,18},{18,2},{3,19},{19,3},{4,20},{20... | collective-permute-start | bytes 3538952 | tf_op jit(solution)/shard_map/ppermute | solution.py:46
  197.3 1.8 collective-permute-start.15
  197.4 2.4 collective-permute-start.16
  197.9 2.5 collective-permute-start.17
  199.1 34.9 %collective-permute-start.8 = (bf16[2,288,768]{2,1,0:T(8,128)(2,1)S(1)}, bf16[2,288,768]{2,1,0:T(8,128)(2,1)S(1)}, u32[]{:S(2)}, u32[]{:S(2)}) collective-permute-start(bf16[2,288,768]{2,1,0:T(8,128)(2,1)S(1)} %get-tuple-element.194.x_ref.ctx.n), channel_id=1, source_target_pairs={{0,1},{1,0},{2,3},{3,2},{4,5},{5,4},{6,7},{7,6},{8,9},{9,8},{10,11... | collective-permute-start | bytes 2654216 | tf_op jit(solution)/shard_map/ppermute | solution.py:46
  199.8 34.9 %collective-permute-start.22 = (bf16[8,288,192]{2,1,0:T(8,128)(2,1)}, bf16[8,288,192]{2,1,0:T(8,128)(2,1)}, u32[]{:S(2)}, u32[]{:S(2)}) collective-permute-start(bf16[8,288,192]{2,1,0:T(8,128)(2,1)} %get-tuple-element.249), channel_id=1, source_target_pairs={{0,1},{1,0},{2,3},{3,2},{4,5},{5,4},{6,7},{7,6},{8,9},{9,8},{10,11... | collective-permute-start | bytes 2654216 | tf_op jit(solution)/shard_map/ppermute | solution.py:46
  229.2 6.8 %collective-permute-start.21 = (bf16[2,288,768]{2,1,0:T(8,128)(2,1)S(1)}, bf16[2,288,768]{2,1,0:T(8,128)(2,1)S(1)}, u32[]{:S(2)}, u32[]{:S(2)}) collective-permute-start(bf16[2,288,768]{2,1,0:T(8,128)(2,1)S(1)} %get-tuple-element.248.refs_10_.dy), channel_id=1, source_target_pairs={{0,1},{1,0},{2,3},{3,2},{4,5},{5,4},{6,7},{7,6},{8,9},{9,8},{10,11... | collective-permute-start | bytes 2654216 | tf_op jit(solution)/shard_map/ppermute | solution.py:46
  229.4 30.5 %collective-permute-start.29 = (bf16[4,48,1536]{2,1,0:T(8,128)(2,1)}, bf16[4,48,1536]{2,1,0:T(8,128)(2,1)S(1)}, u32[]{:S(2)}, u32[]{:S(2)}) collective-permute-start(bf16[4,48,1536]{2,1,0:T(8,128)(2,1)} %get-tuple-element.286), channel_id=1, source_target_pairs={{0,2},{1,3},{2,0},{3,1},{4,6},{5,7},{6,4},{7,5},{8,10},{9,11},{10,... | collective-permute-start | bytes 1769480 | tf_op jit(solution)/shard_map/ppermute | solution.py:46
  230.1 18.6 %collective-permute-start.20 = (bf16[8,288,192]{2,1,0:T(8,128)(2,1)}, bf16[8,288,192]{2,1,0:T(8,128)(2,1)S(1)}, u32[]{:S(2)}, u32[]{:S(2)}) collective-permute-start(bf16[8,288,192]{2,1,0:T(8,128)(2,1)} %get-tuple-element.247), channel_id=1, source_target_pairs={{0,1},{1,0},{2,3},{3,2},{4,5},{5,4},{6,7},{7,6},{8,9},{9,8},{10,11... | collective-permute-start | bytes 2654216 | tf_op jit(solution)/shard_map/ppermute | solution.py:46
  234.0 25.9 %collective-permute-start.30 = (bf16[8,48,768]{2,1,0:T(8,128)(2,1)S(1)}, bf16[8,48,768]{2,1,0:T(8,128)(2,1)S(1)}, u32[]{:S(2)}, u32[]{:S(2)}) collective-permute-start(bf16[8,48,768]{2,1,0:T(8,128)(2,1)S(1)} %copy-done.89), channel_id=1, source_target_pairs={{0,16},{16,0},{1,17},{17,1},{2,18},{18,2},{3,19},{19,3},{4,20},{20... | collective-permute-start | bytes 1769480 | tf_op jit(solution)/shard_map/ppermute | solution.py:46
  234.7 25.3 %collective-permute-start.32 = (bf16[4,192,384]{2,1,0:T(8,128)(2,1)S(1)}, bf16[4,192,384]{2,1,0:T(8,128)(2,1)S(1)}, u32[]{:S(2)}, u32[]{:S(2)}) collective-permute-start(bf16[4,192,384]{2,1,0:T(8,128)(2,1)S(1)} %get-tuple-element.380), channel_id=1, source_target_pairs={{0,2},{1,3},{2,0},{3,1},{4,6},{5,7},{6,4},{7,5},{8,10},{9,11},{10,... | collective-permute-start | bytes 1769480 | tf_op jit(solution)/shard_map/ppermute | solution.py:46
  235.9 26.4 %collective-permute-start.31 = (bf16[4,192,384]{2,1,0:T(8,128)(2,1)S(1)}, bf16[4,192,384]{2,1,0:T(8,128)(2,1)S(1)}, u32[]{:S(2)}, u32[]{:S(2)}) collective-permute-start(bf16[4,192,384]{2,1,0:T(8,128)(2,1)S(1)} %get-tuple-element.382), channel_id=1, source_target_pairs={{0,16},{16,0},{1,17},{17,1},{2,18},{18,2},{3,19},{19,3},{4,20},{20... | collective-permute-start | bytes 1769480 | tf_op jit(solution)/shard_map/ppermute | solution.py:46
  263.9 105.6 %reduce-scatter.5.cloned.1.call-start = ((), (), s32[]{:S(2)}) async-start(), calls=%async_computation.3 | async-start | bytes 2211840 | tf_op jit(solution)/shard_map/reduce_scatter | solution.py:140
  264.8 2.3 collective-permute-start.23
  265.0 2.7 collective-permute-start.24
  265.4 35.5 %collective-permute-start.33 = (bf16[4,192,768]{2,1,0:T(8,128)(2,1)}, bf16[4,192,768]{2,1,0:T(8,128)(2,1)}, u32[]{:S(2)}, u32[]{:S(2)}) collective-permute-start(bf16[4,192,768]{2,1,0:T(8,128)(2,1)} %get-tuple-element.294), channel_id=1, source_target_pairs={{0,2},{1,3},{2,0},{3,1},{4,6},{5,7},{6,4},{7,5},{8,10},{9,11},{10,... | collective-permute-start | bytes 3538952 | tf_op jit(solution)/shard_map/ppermute | solution.py:46
  266.6 34.3 %collective-permute-start.34 = (bf16[8,192,384]{2,1,0:T(8,128)(2,1)}, bf16[8,192,384]{2,1,0:T(8,128)(2,1)S(1)}, u32[]{:S(2)}, u32[]{:S(2)}) collective-permute-start(bf16[8,192,384]{2,1,0:T(8,128)(2,1)} %get-tuple-element.295), channel_id=1, source_target_pairs={{0,16},{16,0},{1,17},{17,1},{2,18},{18,2},{3,19},{19,3},{4,20},{20... | collective-permute-start | bytes 3538952 | tf_op jit(solution)/shard_map/ppermute | solution.py:46
  267.2 2.8 collective-permute-start.25
  267.2 3.7 collective-permute-start.26
  267.7 3.2 collective-permute-start.27
  270.0 30.0 %collective-permute-start.36 = (bf16[4,48,768]{2,1,0:T(8,128)(2,1)}, bf16[4,48,768]{2,1,0:T(8,128)(2,1)}, u32[]{:S(2)}, u32[]{:S(2)}) collective-permute-start(bf16[4,48,768]{2,1,0:T(8,128)(2,1)} %get-tuple-element.388), channel_id=1, source_target_pairs={{0,2},{1,3},{2,0},{3,1},{4,6},{5,7},{6,4},{7,5},{8,10},{9,11},{10,... | collective-permute-start | bytes 884744 | tf_op jit(solution)/shard_map/ppermute | solution.py:46
  285.0 1.8 collective-permute-start.28
  285.3 15.5 %collective-permute-start.35 = (bf16[4,48,768]{2,1,0:T(8,128)(2,1)S(1)}, bf16[4,48,768]{2,1,0:T(8,128)(2,1)S(1)}, u32[]{:S(2)}, u32[]{:S(2)}) collective-permute-start(bf16[4,48,768]{2,1,0:T(8,128)(2,1)S(1)} %get-tuple-element.390), channel_id=1, source_target_pairs={{0,16},{16,0},{1,17},{17,1},{2,18},{18,2},{3,19},{19,3},{4,20},{20... | collective-permute-start | bytes 884744 | tf_op jit(solution)/shard_map/ppermute | solution.py:46
  286.9 14.0 %collective-permute-start.37 = (bf16[128,768]{1,0:T(8,128)(2,1)S(1)}, bf16[128,768]{1,0:T(8,128)(2,1)S(1)}, u32[]{:S(2)}, u32[]{:S(2)}) collective-permute-start(bf16[128,768]{1,0:T(8,128)(2,1)S(1)} %add_convert_fusion.26.rest_0_), channel_id=1, source_target_pairs={{0,4},{1,5},{2,6},{3,7},{4,0},{5,1},{6,2},{7,3},{8,12},{9,13},{10,... | collective-permute-start | bytes 589832 | tf_op jit(solution)/shard_map/ppermute | solution.py:46
  302.1 17.5 %collective-permute-start.39 = (bf16[4,192,384]{2,1,0:T(8,128)(2,1)}, bf16[4,192,384]{2,1,0:T(8,128)(2,1)S(1)}, u32[]{:S(2)}, u32[]{:S(2)}) collective-permute-start(bf16[4,192,384]{2,1,0:T(8,128)(2,1)} %get-tuple-element.376), channel_id=1, source_target_pairs={{0,2},{1,3},{2,0},{3,1},{4,6},{5,7},{6,4},{7,5},{8,10},{9,11},{10,... | collective-permute-start | bytes 1769480 | tf_op jit(solution)/shard_map/ppermute | solution.py:46
  304.6 15.0 %collective-permute-start.38 = (bf16[4,192,384]{2,1,0:T(8,128)(2,1)S(1)}, bf16[4,192,384]{2,1,0:T(8,128)(2,1)S(1)}, u32[]{:S(2)}, u32[]{:S(2)}) collective-permute-start(bf16[4,192,384]{2,1,0:T(8,128)(2,1)S(1)} %get-tuple-element.378), channel_id=1, source_target_pairs={{0,16},{16,0},{1,17},{17,1},{2,18},{18,2},{3,19},{19,3},{4,20},{20... | collective-permute-start | bytes 1769480 | tf_op jit(solution)/shard_map/ppermute | solution.py:46
  305.2 14.3 %collective-permute-start.40 = (bf16[128,768]{1,0:T(8,128)(2,1)S(1)}, bf16[128,768]{1,0:T(8,128)(2,1)S(1)}, u32[]{:S(2)}, u32[]{:S(2)}) collective-permute-start(bf16[128,768]{1,0:T(8,128)(2,1)S(1)} %add_convert_fusion.25.rest_1_), channel_id=1, source_target_pairs={{0,8},{1,9},{2,10},{3,11},{4,12},{5,13},{6,14},{7,15},{8,0},{9,1},... | collective-permute-start | bytes 589832 | tf_op jit(solution)/shard_map/ppermute | solution.py:46
  316.8 13.7 %collective-permute-start.42 = (bf16[4,48,1536]{2,1,0:T(8,128)(2,1)}, bf16[4,48,1536]{2,1,0:T(8,128)(2,1)S(1)}, u32[]{:S(2)}, u32[]{:S(2)}) collective-permute-start(bf16[4,48,1536]{2,1,0:T(8,128)(2,1)} %get-tuple-element.316), channel_id=1, source_target_pairs={{0,2},{1,3},{2,0},{3,1},{4,6},{5,7},{6,4},{7,5},{8,10},{9,11},{10,... | collective-permute-start | bytes 1769480 | tf_op jit(solution)/shard_map/ppermute | solution.py:46
  318.1 13.5 %collective-permute-start.43 = (bf16[8,48,768]{2,1,0:T(8,128)(2,1)}, bf16[8,48,768]{2,1,0:T(8,128)(2,1)}, u32[]{:S(2)}, u32[]{:S(2)}) collective-permute-start(bf16[8,48,768]{2,1,0:T(8,128)(2,1)} %get-tuple-element.317), channel_id=1, source_target_pairs={{0,16},{16,0},{1,17},{17,1},{2,18},{18,2},{3,19},{19,3},{4,20},{20... | collective-permute-start | bytes 1769480 | tf_op jit(solution)/shard_map/ppermute | solution.py:46
  325.4 6.2 %collective-permute-start.41 = (bf16[272,128]{1,0:T(8,128)(2,1)}, bf16[272,128]{1,0:T(8,128)(2,1)S(1)}, u32[]{:S(2)}, u32[]{:S(2)}) collective-permute-start(bf16[272,128]{1,0:T(8,128)(2,1)} %join.1), channel_id=1, source_target_pairs={{0,1},{1,0},{2,3},{3,2},{4,5},{5,4},{6,7},{7,6},{8,9},{9,8},{10,11... | collective-permute-start | bytes 208904 | tf_op jit(solution)/shard_map/ppermute | solution.py:46
  335.0 11.9 %collective-permute-start.46 = (bf16[4,48,768]{2,1,0:T(8,128)(2,1)}, bf16[4,48,768]{2,1,0:T(8,128)(2,1)S(1)}, u32[]{:S(2)}, u32[]{:S(2)}) collective-permute-start(bf16[4,48,768]{2,1,0:T(8,128)(2,1)} %get-tuple-element.384), channel_id=1, source_target_pairs={{0,2},{1,3},{2,0},{3,1},{4,6},{5,7},{6,4},{7,5},{8,10},{9,11},{10,... | collective-permute-start | bytes 884744 | tf_op jit(solution)/shard_map/ppermute | solution.py:46
  337.0 9.9 %collective-permute-start.45 = (bf16[4,48,768]{2,1,0:T(8,128)(2,1)}, bf16[4,48,768]{2,1,0:T(8,128)(2,1)S(1)}, u32[]{:S(2)}, u32[]{:S(2)}) collective-permute-start(bf16[4,48,768]{2,1,0:T(8,128)(2,1)} %get-tuple-element.386), channel_id=1, source_target_pairs={{0,16},{16,0},{1,17},{17,1},{2,18},{18,2},{3,19},{19,3},{4,20},{20... | collective-permute-start | bytes 884744 | tf_op jit(solution)/shard_map/ppermute | solution.py:46
  338.2 8.7 %collective-permute-start.47 = (bf16[128,768]{1,0:T(8,128)(2,1)S(1)}, bf16[128,768]{1,0:T(8,128)(2,1)S(1)}, u32[]{:S(2)}, u32[]{:S(2)}) collective-permute-start(bf16[128,768]{1,0:T(8,128)(2,1)S(1)} %add_convert_fusion.24), channel_id=1, source_target_pairs={{0,2},{1,3},{2,0},{3,1},{4,6},{5,7},{6,4},{7,5},{8,10},{9,11},{10,... | collective-permute-start | bytes 589832 | tf_op jit(solution)/shard_map/ppermute | solution.py:46
  339.6 7.3 %collective-permute-start.44 = (bf16[272,128]{1,0:T(8,128)(2,1)}, bf16[272,128]{1,0:T(8,128)(2,1)S(1)}, u32[]{:S(2)}, u32[]{:S(2)}) collective-permute-start(bf16[272,128]{1,0:T(8,128)(2,1)} %add_convert_fusion.37), channel_id=1, source_target_pairs={{0,2},{1,3},{2,0},{3,1},{4,6},{5,7},{6,4},{7,5},{8,10},{9,11},{10,... | collective-permute-start | bytes 208904 | tf_op jit(solution)/shard_map/ppermute | solution.py:46
  347.8 5.2 %collective-permute-start.48 = (bf16[272,128]{1,0:T(8,128)(2,1)S(1)}, bf16[272,128]{1,0:T(8,128)(2,1)S(1)}, u32[]{:S(2)}, u32[]{:S(2)}) collective-permute-start(bf16[272,128]{1,0:T(8,128)(2,1)S(1)} %add_convert_fusion.36), channel_id=1, source_target_pairs={{0,16},{16,0},{1,17},{17,1},{2,18},{18,2},{3,19},{19,3},{4,20},{20... | collective-permute-start | bytes 208904 | tf_op jit(solution)/shard_map/ppermute | solution.py:46
  349.4 9.8 %collective-permute-start.50 = (bf16[384,384]{1,0:T(8,128)(2,1)S(1)}, bf16[384,384]{1,0:T(8,128)(2,1)S(1)}, u32[]{:S(2)}, u32[]{:S(2)}) collective-permute-start(bf16[384,384]{1,0:T(8,128)(2,1)S(1)} %bitcast.96), channel_id=1, source_target_pairs={{0,16},{16,0},{1,17},{17,1},{2,18},{18,2},{3,19},{19,3},{4,20},{20... | collective-permute-start | bytes 884744 | tf_op jit(solution)/shard_map/ppermute | solution.py:46
  350.0 9.2 %collective-permute-start.49 = (bf16[128,768]{1,0:T(8,128)(2,1)S(1)}, bf16[128,768]{1,0:T(8,128)(2,1)S(1)}, u32[]{:S(2)}, u32[]{:S(2)}) collective-permute-start(bf16[128,768]{1,0:T(8,128)(2,1)S(1)} %add_convert_fusion.23), channel_id=1, source_target_pairs={{0,16},{16,0},{1,17},{17,1},{2,18},{18,2},{3,19},{19,3},{4,20},{20... | collective-permute-start | bytes 589832 | tf_op jit(solution)/shard_map/ppermute | solution.py:46
  351.7 14.7 %collective-permute-start.53 = (bf16[2,96,768]{2,1,0:T(8,128)(2,1)S(1)}, bf16[2,96,768]{2,1,0:T(8,128)(2,1)S(1)}, u32[]{:S(2)}, u32[]{:S(2)}) collective-permute-start(bf16[2,96,768]{2,1,0:T(8,128)(2,1)S(1)} %pad_maximum_fusion.5), channel_id=1, source_target_pairs={{0,4},{1,5},{2,6},{3,7},{4,0},{5,1},{6,2},{7,3},{8,12},{9,13},{10,... | collective-permute-start | bytes 884744 | tf_op jit(solution)/shard_map/ppermute | solution.py:46
  359.2 11.8 %collective-permute-start.51 = (bf16[272,128]{1,0:T(8,128)(2,1)S(1)}, bf16[272,128]{1,0:T(8,128)(2,1)S(1)}, u32[]{:S(2)}, u32[]{:S(2)}) collective-permute-start(bf16[272,128]{1,0:T(8,128)(2,1)S(1)} %add_convert_fusion.35), channel_id=1, source_target_pairs={{0,4},{1,5},{2,6},{3,7},{4,0},{5,1},{6,2},{7,3},{8,12},{9,13},{10,... | collective-permute-start | bytes 208904 | tf_op jit(solution)/shard_map/ppermute | solution.py:46
  361.2 14.7 %collective-permute-start.57 = (bf16[128,768]{1,0:T(8,128)(2,1)S(1)}, bf16[128,768]{1,0:T(8,128)(2,1)S(1)}, u32[]{:S(2)}, u32[]{:S(2)}) collective-permute-start(bf16[128,768]{1,0:T(8,128)(2,1)S(1)} %add_convert_fusion.22), channel_id=1, source_target_pairs={{0,1},{1,0},{2,3},{3,2},{4,5},{5,4},{6,7},{7,6},{8,9},{9,8},{10,11... | collective-permute-start | bytes 589832 | tf_op jit(solution)/shard_map/ppermute | solution.py:46
  366.5 7.7 %collective-permute-start.54 = (bf16[1,96,768]{2,1,0:T(8,128)(2,1)S(1)}, bf16[1,96,768]{2,1,0:T(8,128)(2,1)S(1)}, u32[]{:S(2)}, u32[]{:S(2)}) collective-permute-start(bf16[1,96,768]{2,1,0:T(8,128)(2,1)S(1)} %get-tuple-element.391), channel_id=1, source_target_pairs={{0,8},{1,9},{2,10},{3,11},{4,12},{5,13},{6,14},{7,15},{8,0},{9,1},... | collective-permute-start | bytes 442376 | tf_op jit(solution)/shard_map/ppermute | solution.py:46
  369.5 14.7 %collective-permute-start.56 = (bf16[576,384]{1,0:T(8,128)(2,1)}, bf16[576,384]{1,0:T(8,128)(2,1)S(1)}, u32[]{:S(2)}, u32[]{:S(2)}) collective-permute-start(bf16[576,384]{1,0:T(8,128)(2,1)} %bitcast.92), channel_id=1, source_target_pairs={{0,16},{16,0},{1,17},{17,1},{2,18},{18,2},{3,19},{19,3},{4,20},{20... | collective-permute-start | bytes 1327112 | tf_op jit(solution)/shard_map/ppermute | solution.py:46
  374.3 12.1 %collective-permute-start.55 = (bf16[96,768]{1,0:T(8,128)(2,1)S(1)}, bf16[96,768]{1,0:T(8,128)(2,1)S(1)}, u32[]{:S(2)}, u32[]{:S(2)}) collective-permute-start(bf16[96,768]{1,0:T(8,128)(2,1)S(1)} %fusion.18.refs_0_), channel_id=1, source_target_pairs={{0,16},{16,0},{1,17},{17,1},{2,18},{18,2},{3,19},{19,3},{4,20},{20... | collective-permute-start | bytes 442376 | tf_op jit(solution)/shard_map/ppermute | solution.py:46
  376.0 5.3 %collective-permute-start.52 = (bf16[272,128]{1,0:T(8,128)(2,1)S(1)}, bf16[272,128]{1,0:T(8,128)(2,1)S(1)}, u32[]{:S(2)}, u32[]{:S(2)}) collective-permute-start(bf16[272,128]{1,0:T(8,128)(2,1)S(1)} %add_convert_fusion.34.left), channel_id=1, source_target_pairs={{0,8},{1,9},{2,10},{3,11},{4,12},{5,13},{6,14},{7,15},{8,0},{9,1},... | collective-permute-start | bytes 208904 | tf_op jit(solution)/shard_map/ppermute | solution.py:46
  (88 other events, 570.7 us)
Sparse Core Ops, SparseCore 0:
  9.9 105.3 all-gather.2
  264.0 28.2 reduce-scatter.2
  323.9 42.7 reduce-scatter.4

commit v2 on v1

--- a/solution.py
+++ b/solution.py
@@ -855,8 +855,8 @@
     total = None
     for index, block in enumerate(blocks):
         weights = block[0]
-        row = bias[pl.ds(me[0] ^ (BLOCKS * step + index), 1), layer, :units]
-        hidden = nt_dot(x, weights[:, :width]) + row.astype(f32)
+        row = bias[pl.ds(BLOCKS * step + index, 1), layer, :]
+        hidden = nt_dot(x, weights[:, :width]) + row
         half_cdf = 0.5 + 0.5 * lax.erf(hidden * 0.5**0.5)
         low = (hidden * half_cdf).astype(bf16)
         (mate_act if index % 2 else own_act)[index // 2] = low
@@ -901,8 +901,8 @@
     return [pick(which) for which in range(BLOCKS)]
 
 
-def ffn(me, layer, pair, n, gathered, units, out_bias, gain, shift, qkv_weight, attn_bias):
-    groups = gathered.shape[0]
+def ffn(me, layer, pair, n, gathered, bias, out_bias, gain, shift, qkv_weight, attn_bias):
+    groups, _, units = bias.shape
     rows, width = n.shape
     more = layer < LAYERS - 1
     whole = pl.BlockSpec((rows, width), lambda i, me: (0, 0))
@@ -912,13 +912,11 @@
     low = jax.ShapeDtypeStruct((rows, width), bf16)
     half_act = pl.BlockSpec((HALF, rows, units), lambda i, me: (i, 0, 0))
     half_shape = jax.ShapeDtypeStruct((groups // 2, rows, units), bf16)
-    inputs = [pair] + [gathered] * (BLOCKS + 1) + [n, out_bias, gain, shift]
+    inputs = [pair] + [gathered] * BLOCKS + [bias, n, out_bias, gain, shift]
     in_specs = [
         pl.BlockSpec((None, rows, width), lambda i, me: (1, 0, 0)),
         *weight_blocks(layer, units, width),
-        pl.BlockSpec(
-            (groups, 16, 2 * width), lambda i, me: (0, LAYERS * units // 16, 0)
-        ),
+        full(bias),
         whole,
         full(out_bias),
         full(gain),
@@ -1367,15 +1365,11 @@
     width = text_states.shape[1]
     text_rows = text_states.shape[0]
 
-    bias_rows = jnp.pad(ffn_in_bias, ((0, 16 - LAYERS), (0, 2 * width - units)))
-    packed = jnp.concatenate(
-        [
-            jnp.concatenate([ffn_in, ffn_out], axis=2).reshape(LAYERS * units, 2 * width),
-            bias_rows,
-        ],
-        axis=0,
-    )
+    packed = jnp.concatenate([ffn_in, ffn_out], axis=2).reshape(LAYERS * units, 2 * width)
     gathered = lax.all_gather(packed, "tp", axis=0)
+    hidden_bias = ffn_in_bias.astype(f32)[None]
+    for bit in range(mesh_bits("tp")):
+        hidden_bias = jnp.concatenate([hidden_bias, flipped(hidden_bias, "tp", bit)], axis=0)
 
     other_boxes = flipped(text_boxes, "tp", 0)
     length = lax.dynamic_index_in_dim(text_lengths, page, 0, keepdims=False)
@@ -1419,7 +1413,7 @@
             pair,
             normed,
             gathered,
-            units,
+            hidden_bias,
             ffn_out_bias,
             norm_gain,
             norm_shift,

time: 398 us -> 394 us (0.990)
  waiting for transfers between devices: 86.4 us -> 79.9 us
  starting transfers between devices: 52.5 us -> 57.6 us
    all_gather x1, waiting for transfers between devices: 37.6 us -> 28.1 us  [body(): gathered = lax.all_gather(packed, 'tp', axis=0)]
    ppermute x58 -> x62, starting transfers between devices: 52.4 us -> 57.5 us  [flipped(): return lax.ppermute(block, axis, [(i, i ^ 1 << bit) for i in range(count)])]
    ppermute x58 -> x62, waiting for transfers between devices: 48.7 us -> 51.2 us  [flipped(): return lax.ppermute(block, axis, [(i, i ^ 1 << bit) for i in range(count)])]
    unnamed x186 -> x191, local copies, waits for them, and re-layouts: 22.3 us -> 21.5 us
  transfers between devices with their start and end apart: 61 -> 65, of which waited for: 22 -> 24; matrix products, arithmetic and copies ran while one was open for 6% -> 6% of each run, Pallas kernels for 35% -> 35%
where the time goes in v2:
time: 394 us; the launch traced here: 391 us
  Pallas kernels  187 us (47%)
  waiting for transfers between devices  79.9 us (20%)
  starting transfers between devices  57.6 us (15%)
  local copies, waits for them, and re-layouts  23.2 us (6%)
  other arithmetic  21.8 us (6%)
  between operations  15.2 us (4%)
  matrix products  5.81 us (1%)
    ppermute x62, starting transfers between devices, flipped(): return lax.ppermute(block, axis, [(i, i ^ 1 << bit) for i in range(count)])  57.5 us
    ppermute x62, waiting for transfers between devices, flipped(): return lax.ppermute(block, axis, [(i, i ^ 1 << bit) for i in range(count)])  51.2 us
    all_gather x1, waiting for transfers between devices, body(): gathered = lax.all_gather(packed, 'tp', axis=0)  28.1 us
    pallas_call x2, Pallas kernels, ffn(): pl.pallas_call(functools.partial(ffn_kernel, layer, more), out_shape=out_...  24.9 us
    pallas_call x2, Pallas kernels, ffn_back(): pl.pallas_call(functools.partial(ffn_back_kernel, layer), out_shape=[half...  24.3 us
    pallas_call x2, Pallas kernels, attend(): pl.pallas_call(functools.partial(attend_kernel, layer), grid=(STEPS,), in...  23.4 us
    pallas_call x2, Pallas kernels, projection_grads(): pl.pallas_call(functools.partial(projection_kernel, by_distance), out_sha...  22.8 us
    unnamed x191, local copies, waits for them, and re-layouts  21.5 us
  transfers between devices with their start and end apart: 65, of which 24 were waited for; matrix products, arithmetic and copies ran while one was open for 6% of the time, Pallas kernels for 35%

profile of v2, /device:TPU:0, one launch (start us, length us, event | category | flops | bytes accessed | tf_op | source)
XLA Modules:
  0.0 390.6 jit_solution(12416906540933091967)
XLA Ops:
  7.2 2.3 pad_maximum_fusion.1
  11.7 2.9 collective-permute-start.1
  14.7 1.6 collective-permute-done.1
  16.2 2.1 collective-permute-start.2
  18.4 1.6 collective-permute-done.2
  19.9 3.0 collective-permute-start.3
  23.0 1.7 collective-permute-done.3
  24.6 1.8 collective-permute-start.4
  29.8 1.8 convolution_convert_fusion
  31.6 1.9 fusion.1
  34.7 1.9 collective-permute-start.8
  40.3 21.4 %score_bias.1.bias = f32[12,288,640]{2,1,0:T(8,128)} custom-call(s32[2]{0:T(128)S(1)} %pad_add_fusion.1.facts, s32[2,256]{1,0:T(2,128)S(1)} %copy-done.45, s32[2,256]{1,0:T(2,128)S(1)} %collective-permute-done.6.other_boxes, f32[12,8,128]{2,1,0:T(8,128)S(1)} %broadcast_in_dim.48.table_a, f32[12,8,128]{2,1,0:T(8,128)S(1)} %broadcast_in_dim.49.table_b), custom_call_target="tpu_custom_call" | custom-call | flops 1 | bytes 1 | tf_op jit(solution)/shard_map/score_bias/pallas_call | solution.py:246
  61.7 1.6 collective-permute-start.9
  63.3 1.9 fusion.q_ref
  65.6 2.6 collective-permute-start.10
  68.2 2.4 collective-permute-done.10
  71.7 11.7 %attend.2 = (bf16[12,288,640]{2,1,0:T(8,128)(2,1)}, bf16[2,288,768]{2,1,0:T(8,128)(2,1)S(1)}, f32[288,768]{1,0:T(8,128)S(1)}, f32[288,768]{1,0:T(8,128)S(1)}) custom-call(bf16[288,768]{1,0:T(8,128)(2,1)S(1)} %fusion.q_ref, bf16[288,2304]{1,0:T(8,128)(2,1)} %copy-done.46, bf16[288,2304]{1,0:T(8,128)(2,1)} %copy-done.47, bf16[288,2304]{1,0:T(8,128)(2,1)} %copy-done.46, ...), custom_call_target="tpu_custom_call" | custom-call | flops 1 | bytes 1 | tf_op jit(solution)/shard_map/attend/pallas_call | solution.py:755
  84.4 28.1 %all-gather.2.cloned.1.call-done.refs_0_.refs_1_.refs_2_.refs_3_ = bf16[16,384,1536]{2,1,0:T(8,128)(2,1)} async-done(((bf16[1,384,1536]{2,1,0:T(8,128)(2,1)}), bf16[16,384,1536]{2,1,0:T(8,128)(2,1)}) %all-gather.2.cloned.1.call-update) | async-done | bytes 18874384 | tf_op jit(solution)/shard_map/all_gather | solution.py:1369
  112.5 13.2 %feed_forward.2 = (bf16[8,288,192]{2,1,0:T(8,128)(2,1)}, bf16[8,288,192]{2,1,0:T(8,128)(2,1)}, bf16[16,288,192]{2,1,0:T(8,128)(2,1)}, f32[288,768]{1,0:T(8,128)S...) custom-call(s32[2]{0:T(128)S(1)} %pad_add_fusion.me, ...), custom_call_target="tpu_custom_call" | custom-call | flops 1 | bytes 1 | tf_op jit(solution)/shard_map/feed_forward/pallas_call | solution.py:938
  126.0 3.0 collective-permute-done.11.kp.vp.x_mate
  130.1 11.7 %attend.3 = (bf16[12,288,640]{2,1,0:T(8,128)(2,1)}, bf16[2,288,768]{2,1,0:T(8,128)(2,1)S(1)}, f32[288,768]{1,0:T(8,128)S(1)}, f32[288,768]{1,0:T(8,128)S(1)}) custom-call(bf16[288,768]{1,0:T(8,128)(2,1)S(1)} %get-tuple-element.200.q_ref, bf16[288,2304]{1,0:T(8,128)(2,1)} %get-tuple-element.201.ko.vo.x, bf16[288,2304]{1,0:T(8,128)(2,1)} %copy-done.48, ...), custom_call_target="tpu_custom_call" | custom-call | flops 1 | bytes 1 | tf_op jit(solution)/shard_map/attend/pallas_call | solution.py:755
  141.8 11.8 %feed_forward.3 = (bf16[8,288,192]{2,1,0:T(8,128)(2,1)S(1)}, bf16[8,288,192]{2,1,0:T(8,128)(2,1)}, bf16[16,288,192]{2,1,0:T(8,128)(2,1)}, f32[288,768]{1,0:T(8,128)S(1)}, bf16[288,768]{1,0:T(8,128)(2,1)}) custom-call(s32[2]{0:T(128)S(1)} %pad_add_fusion.me, bf16[2,288,768]{2,1,0:T(8,128)(2,1)S(1)} %get-tuple-element.203.x_ref.ctx.n, ...), custom_call_target="tpu_custom_call" | custom-call | flops 1 | bytes 1 | tf_op jit(solution)/shard_map/feed_forward/pallas_call | solution.py:938
  154.6 12.1 %feed_forward_back.2 = (bf16[8,288,192]{2,1,0:T(8,128)(2,1)}, bf16[8,288,192]{2,1,0:T(8,128)(2,1)}, bf16[2,288,768]{2,1,0:T(8,128)(2,1)S(1)}, f32[16,1,192]{2,1,...) custom-call(s32[2]{0:T(128)S(1)} %pad_add_fusion.me, ...), custom_call_target="tpu_custom_call" | custom-call | flops 1 | bytes 1 | tf_op jit(solution)/shard_map/feed_forward_back/pallas_call | solution.py:1011
  168.7 10.6 %attend_back.2 = (bf16[12,288,640]{2,1,0:T(8,128)(2,1)}, bf16[288,768]{1,0:T(8,128)(2,1)S(1)}, bf16[288,768]{1,0:T(8,128)(2,1)S(1)}, bf16[288,768]{1,0:T(8,128)(...) custom-call(bf16[288,768]{1,0:T(8,128)(2,1)S(1)} %get-tuple-element.200.q_ref, ...), custom_call_target="tpu_custom_call" | custom-call | flops 1 | bytes 1 | tf_op jit(solution)/shard_map/attend_back/pallas_call | solution.py:827
  180.3 9.9 %feed_forward_grads.2 = (bf16[4,192,768]{2,1,0:T(8,128)(2,1)}, bf16[4,192,768]{2,1,0:T(8,128)(2,1)}, bf16[8,192,384]{2,1,0:T(8,128)(2,1)}, bf16[8,192,384]{2,1,0:T(8,128)(2,1)}) custom-call(s32[2]{0:T(128)S(1)} %pad_add_fusion.me, bf16[2,288,768]{2,1,0:T(8,128)(2,1)S(1)} %get-tuple-element.203.x_ref.ctx.n, ...), custom_call_target="tpu_custom_call" | custom-call | flops 1 | bytes 1 | tf_op jit(solution)/shard_map/feed_forward_grads/pallas_call | solution.py:1101
  190.2 1.3 collective-permute-start.22
  191.5 1.5 collective-permute-start.23
  196.8 11.8 %projection_grads.2 = (bf16[4,48,1536]{2,1,0:T(8,128)(2,1)}, bf16[4,48,1536]{2,1,0:T(8,128)(2,1)}, bf16[8,48,768]{2,1,0:T(8,128)(2,1)}, bf16[8,48,768]{2,1,0:T(8...) custom-call(s32[2]{0:T(128)S(1)} %pad_add_fusion.me, bf16[288,2304]{1,0:T(8,128)(2,1)} %get-tuple-element.201.ko.vo.x, ...), custom_call_target="tpu_custom_call" | custom-call | flops 1 | bytes 1 | tf_op jit(solution)/shard_map/projection_grads/pallas_call | solution.py:1232
  209.8 12.1 %feed_forward_back.3 = (bf16[8,288,192]{2,1,0:T(8,128)(2,1)}, bf16[8,288,192]{2,1,0:T(8,128)(2,1)}, bf16[2,288,768]{2,1,0:T(8,128)(2,1)S(1)}, f32[16,1,192]{2,1,...) custom-call(s32[2]{0:T(128)S(1)} %pad_add_fusion.me, ...), custom_call_target="tpu_custom_call" | custom-call | flops 1 | bytes 1 | tf_op jit(solution)/shard_map/feed_forward_back/pallas_call | solution.py:1011
  225.8 2.0 add_convert_fusion.8
  227.8 1.8 add_convert_fusion.9
  231.6 1.5 collective-permute-start.35
  233.1 10.6 %attend_back.3 = (bf16[12,288,640]{2,1,0:T(8,128)(2,1)}, bf16[288,768]{1,0:T(8,128)(2,1)S(1)}, bf16[288,768]{1,0:T(8,128)(2,1)S(1)}, bf16[288,768]{1,0:T(8,128)(...) custom-call(bf16[288,768]{1,0:T(8,128)(2,1)S(1)} %copy-done.11, bf16[288,2304]{1,0:T(8,128)(2,1)} %copy-done.46, ...), custom_call_target="tpu_custom_call" | custom-call | flops 1 | bytes 1 | tf_op jit(solution)/shard_map/attend_back/pallas_call | solution.py:827
  245.5 10.0 %feed_forward_grads.3 = (bf16[4,192,768]{2,1,0:T(8,128)(2,1)}, bf16[4,192,768]{2,1,0:T(8,128)(2,1)}, bf16[8,192,384]{2,1,0:T(8,128)(2,1)}, bf16[8,192,384]{2,1,0:T(8,128)(2,1)}) custom-call(s32[2]{0:T(128)S(1)} %pad_add_fusion.me, bf16[2,288,768]{2,1,0:T(8,128)(2,1)S(1)} %get-tuple-element.194.x_ref.ctx.n, ...), custom_call_target="tpu_custom_call" | custom-call | flops 1 | bytes 1 | tf_op jit(solution)/shard_map/feed_forward_grads/pallas_call | solution.py:1101
  255.6 2.4 collective-permute-done.35
  263.4 2.2 add_convert_fusion.16
  267.3 11.1 %projection_grads.3 = (bf16[4,48,1536]{2,1,0:T(8,128)(2,1)}, bf16[4,48,1536]{2,1,0:T(8,128)(2,1)}, bf16[8,48,768]{2,1,0:T(8,128)(2,1)}, bf16[8,48,768]{2,1,0:T(8...) custom-call(s32[2]{0:T(128)S(1)} %pad_add_fusion.me, bf16[288,2304]{1,0:T(8,128)(2,1)} %copy-done.46, ...), custom_call_target="tpu_custom_call" | custom-call | flops 1 | bytes 1 | tf_op jit(solution)/shard_map/projection_grads/pallas_call | solution.py:1232
  278.4 2.2 visual_back.1
  281.0 1.5 collective-permute-start.39
  282.5 1.8 collective-permute-start.41
  284.3 9.0 %table_grad.2.rest_0_.refs_7_ = f32[6,8,128]{2,1,0:T(8,128)} custom-call(bf16[640,256]{1,0:T(8,128)(2,1)} %copy-done.12, bf16[224,288]{1,0:T(8,128)(2,1)} %copy-done.19, bf16[4,288,640]{2,1,0:T(8,128)(2,1)} %copy-done.2, bf16[12,288,640]{2,1,0:T(8,128)(2,1)} %get-tuple-element.269.ds_a, bf16[12,288,640]{2,1,0:T(8,128)(2,1)} %get-tuple-element.270.ds_b, ...), custom_call_target="tpu_custom_call" | custom-call | flops 1 | bytes 1 | tf_op jit(solution)/shard_map/table_grad/pallas_call | solution.py:392
  293.2 2.4 collective-permute-done.40
  299.1 1.7 add_convert_fusion.3
  301.5 2.5 collective-permute-start.44
  304.0 9.1 %table_grad.3.refs_8_ = f32[6,8,128]{2,1,0:T(8,128)} custom-call(bf16[640,256]{1,0:T(8,128)(2,1)} %copy-done.12, bf16[224,288]{1,0:T(8,128)(2,1)} %copy-done.19, bf16[4,288,640]{2,1,0:T(8,128)(2,1)} %copy-done.2, bf16[12,288,640]{2,1,0:T(8,128)(2,1)} %get-tuple-element.269.ds_a, bf16[12,288,640]{2,1,0:T(8,128)(2,1)} %get-tuple-element.270.ds_b, ...), custom_call_target="tpu_custom_call" | custom-call | flops 1 | bytes 1 | tf_op jit(solution)/shard_map/table_grad/pallas_call | solution.py:392
  313.0 1.3 collective-permute-start.46
  314.4 1.4 collective-permute-start.47
  319.8 1.6 join.1
  321.4 5.5 %collective-permute-done.46 = bf16[4,48,1536]{2,1,0:T(8,128)(2,1)} collective-permute-done((bf16[4,48,1536]{2,1,0:T(8,128)(2,1)}, bf16[4,48,1536]{2,1,0:T(8,128)(2,1)}, u32[]{:S(2)}, u32[]{:S(2)}) %collective-permute-start.46) | collective-permute-done | bytes 589856 | tf_op jit(solution)/shard_map/ppermute | solution.py:46
  331.1 2.0 add_convert_fusion.13
  334.4 1.3 collective-permute-start.51
  337.4 5.1 %collective-permute-done.48 = bf16[272,128]{1,0:T(8,128)(2,1)S(1)} collective-permute-done((bf16[272,128]{1,0:T(8,128)(2,1)S(1)}, bf16[272,128]{1,0:T(8,128)(2,1)S(1)}, u32[]{:S(2)}, u32[]{:S(2)}) %collective-permute-start.48) | collective-permute-done | bytes 69664 | tf_op jit(solution)/shard_map/ppermute | solution.py:46
  346.0 1.3 collective-permute-start.57
  347.7 6.5 %collective-permute-done.53 = bf16[128,768]{1,0:T(8,128)(2,1)S(1)} collective-permute-done((bf16[128,768]{1,0:T(8,128)(2,1)S(1)}, bf16[128,768]{1,0:T(8,128)(2,1)S(1)}, u32[]{:S(2)}, u32[]{:S(2)}) %collective-permute-start.53) | collective-permute-done | bytes 196640 | tf_op jit(solution)/shard_map/ppermute | solution.py:46
  354.2 2.5 collective-permute-start.55
  356.9 4.7 %collective-permute-done.57 = bf16[2,96,768]{2,1,0:T(8,128)(2,1)S(1)} collective-permute-done((bf16[2,96,768]{2,1,0:T(8,128)(2,1)S(1)}, bf16[2,96,768]{2,1,0:T(8,128)(2,1)S(1)}, u32[]{:S(2)}, u32[]{:S(2)}) %collective-permute-start.57) | collective-permute-done | bytes 294944 | tf_op jit(solution)/shard_map/ppermute | solution.py:46
  361.7 2.4 collective-permute-start.58
  364.8 1.3 collective-permute-start.60
  366.1 4.0 %collective-permute-done.58 = bf16[1,96,768]{2,1,0:T(8,128)(2,1)S(1)} collective-permute-done((bf16[1,96,768]{2,1,0:T(8,128)(2,1)S(1)}, bf16[1,96,768]{2,1,0:T(8,128)(2,1)S(1)}, u32[]{:S(2)}, u32[]{:S(2)}) %collective-permute-start.58) | collective-permute-done | bytes 147488 | tf_op jit(solution)/shard_map/ppermute | solution.py:46
  370.2 1.6 collective-permute-start.59
  373.3 3.8 collective-permute-done.56.right
  377.7 2.3 split.1
  380.1 2.1 feed_forward_out.1
  382.2 1.6 projections_out.1
  (348 shorter events, 60.2 us)
Async XLA Ops:
  7.2 105.3 %all-gather.2.cloned.1.call-start = ((), (), s32[]{:S(2)}) async-start(), calls=%async_computation.2 | async-start | bytes 20054016 | tf_op jit(solution)/shard_map/all_gather | solution.py:1369
  9.7 287.5 %reduce-scatter.3.cloned.1.call-start = ((), (), s32[]{:S(2)}) async-start(), calls=%async_computation.3 | async-start | bytes 1474560 | tf_op jit(solution)/shard_map/reduce_scatter | solution.py:140
  10.9 25.7 %collective-permute-start.6 = (s32[2,256]{1,0:T(2,128)S(1)}, s32[2,256]{1,0:T(2,128)S(1)}, u32[]{:S(2)}, u32[]{:S(2)}) collective-permute-start(s32[2,256]{1,0:T(2,128)S(1)} %copy-done.45), channel_id=1, source_target_pairs={{0,1},{1,0},{2,3},{3,2},{4,5},{5,4},{6,7},{7,6},{8,9},{9,8},{10,11... | collective-permute-start | bytes 6152 | tf_op jit(solution)/shard_map/ppermute | solution.py:46
  11.7 4.5 %collective-permute-start.1 = (f32[2,256]{1,0:T(2,128)S(1)}, f32[2,256]{1,0:T(2,128)S(1)}, u32[]{:S(2)}, u32[]{:S(2)}) collective-permute-start(f32[2,256]{1,0:T(2,128)S(1)} %fusion.23), channel_id=1, source_target_pairs={{0,2},{1,3},{2,0},{3,1},{4,6},{5,7},{6,4},{7,5},{8,10},{9,11},{10,... | collective-permute-start | bytes 6152 | tf_op jit(solution)/shard_map/ppermute | solution.py:46
  14.7 20.0 %collective-permute-start.7 = (f32[1,2,192]{2,1,0:T(2,128)S(1)}, f32[1,2,192]{2,1,0:T(2,128)S(1)}, u32[]{:S(2)}, u32[]{:S(2)}) collective-permute-start(f32[1,2,192]{2,1,0:T(2,128)S(1)} %bitcast_convert_fusion), channel_id=1, source_target_pairs={{0,1},{1,0},{2,3},{3,2},{4,5},{5,4},{6,7},{7,6},{8,9},{9,8},{10,11... | collective-permute-start | bytes 4616 | tf_op jit(solution)/shard_map/ppermute | solution.py:46
  16.2 3.7 collective-permute-start.2
  19.9 4.7 %collective-permute-start.3 = (f32[2,256]{1,0:T(2,128)S(1)}, f32[2,256]{1,0:T(2,128)S(1)}, u32[]{:S(2)}, u32[]{:S(2)}) collective-permute-start(f32[2,256]{1,0:T(2,128)S(1)} %add.239), channel_id=1, source_target_pairs={{0,8},{1,9},{2,10},{3,11},{4,12},{5,13},{6,14},{7,15},{8,0},{9,1},... | collective-permute-start | bytes 6152 | tf_op jit(solution)/shard_map/ppermute | solution.py:46
  24.6 3.6 collective-permute-start.4
  33.7 36.9 %collective-permute-start.5 = (bf16[288,2304]{1,0:T(8,128)(2,1)S(1)}, bf16[288,2304]{1,0:T(8,128)(2,1)S(1)}, u32[]{:S(2)}, u32[]{:S(2)}) collective-permute-start(bf16[288,2304]{1,0:T(8,128)(2,1)S(1)} %pad_maximum_fusion.ko.vo.x), channel_id=1, source_target_pairs={{0,1},{1,0},{2,3},{3,2},{4,5},{5,4},{6,7},{7,6},{8,9},{9,8},{10,11... | collective-permute-start | bytes 3981320 | tf_op jit(solution)/shard_map/ppermute | solution.py:46
  34.7 27.0 %collective-permute-start.8 = (f32[2,2,192]{2,1,0:T(2,128)S(1)}, f32[2,2,192]{2,1,0:T(2,128)S(1)}, u32[]{:S(2)}, u32[]{:S(2)}) collective-permute-start(f32[2,2,192]{2,1,0:T(2,128)S(1)} %pad_maximum_fusion.8), channel_id=1, source_target_pairs={{0,2},{1,3},{2,0},{3,1},{4,6},{5,7},{6,4},{7,5},{8,10},{9,11},{10,... | collective-permute-start | bytes 9224 | tf_op jit(solution)/shard_map/ppermute | solution.py:46
  61.7 3.9 collective-permute-start.9
  65.6 5.0 %collective-permute-start.10 = (f32[8,2,192]{2,1,0:T(2,128)S(1)}, f32[8,2,192]{2,1,0:T(2,128)S(1)}, u32[]{:S(2)}, u32[]{:S(2)}) collective-permute-start(f32[8,2,192]{2,1,0:T(2,128)S(1)} %pad_maximum_fusion.6), channel_id=1, source_target_pairs={{0,8},{1,9},{2,10},{3,11},{4,12},{5,13},{6,14},{7,15},{8,0},{9,1},... | collective-permute-start | bytes 36872 | tf_op jit(solution)/shard_map/ppermute | solution.py:46
  125.6 3.3 collective-permute-start.11
  167.6 11.6 %collective-permute-start.14 = (bf16[8,288,192]{2,1,0:T(8,128)(2,1)}, bf16[8,288,192]{2,1,0:T(8,128)(2,1)S(1)}, u32[]{:S(2)}, u32[]{:S(2)}) collective-permute-start(bf16[8,288,192]{2,1,0:T(8,128)(2,1)} %get-tuple-element.216), channel_id=1, source_target_pairs={{0,1},{1,0},{2,3},{3,2},{4,5},{5,4},{6,7},{7,6},{8,9},{9,8},{10,11... | collective-permute-start | bytes 2654216 | tf_op jit(solution)/shard_map/ppermute | solution.py:46
  167.9 11.4 %collective-permute-start.15 = (bf16[2,288,768]{2,1,0:T(8,128)(2,1)S(1)}, bf16[2,288,768]{2,1,0:T(8,128)(2,1)S(1)}, u32[]{:S(2)}, u32[]{:S(2)}) collective-permute-start(bf16[2,288,768]{2,1,0:T(8,128)(2,1)S(1)} %get-tuple-element.217.refs_10_.dy), channel_id=1, source_target_pairs={{0,1},{1,0},{2,3},{3,2},{4,5},{5,4},{6,7},{7,6},{8,9},{9,8},{10,11... | collective-permute-start | bytes 2654216 | tf_op jit(solution)/shard_map/ppermute | solution.py:46
  168.2 11.2 %collective-permute-start.16 = (bf16[8,288,192]{2,1,0:T(8,128)(2,1)}, bf16[8,288,192]{2,1,0:T(8,128)(2,1)}, u32[]{:S(2)}, u32[]{:S(2)}) collective-permute-start(bf16[8,288,192]{2,1,0:T(8,128)(2,1)} %get-tuple-element.218), channel_id=1, source_target_pairs={{0,1},{1,0},{2,3},{3,2},{4,5},{5,4},{6,7},{7,6},{8,9},{9,8},{10,11... | collective-permute-start | bytes 2654216 | tf_op jit(solution)/shard_map/ppermute | solution.py:46
  168.4 10.9 %collective-permute-start.13 = (bf16[2,288,768]{2,1,0:T(8,128)(2,1)S(1)}, bf16[2,288,768]{2,1,0:T(8,128)(2,1)S(1)}, u32[]{:S(2)}, u32[]{:S(2)}) collective-permute-start(bf16[2,288,768]{2,1,0:T(8,128)(2,1)S(1)} %get-tuple-element.203.x_ref.ctx.n), channel_id=1, source_target_pairs={{0,1},{1,0},{2,3},{3,2},{4,5},{5,4},{6,7},{7,6},{8,9},{9,8},{10,11... | collective-permute-start | bytes 2654216 | tf_op jit(solution)/shard_map/ppermute | solution.py:46
  179.3 13.7 %collective-permute-start.17 = (bf16[288,768]{1,0:T(8,128)(2,1)S(1)}, bf16[288,768]{1,0:T(8,128)(2,1)S(1)}, u32[]{:S(2)}, u32[]{:S(2)}) collective-permute-start(bf16[288,768]{1,0:T(8,128)(2,1)S(1)} %get-tuple-element.219.refs_0_), channel_id=1, source_target_pairs={{0,1},{1,0},{2,3},{3,2},{4,5},{5,4},{6,7},{7,6},{8,9},{9,8},{10,11... | collective-permute-start | bytes 1327112 | tf_op jit(solution)/shard_map/ppermute | solution.py:46
  179.7 13.9 %collective-permute-start.18 = (bf16[288,768]{1,0:T(8,128)(2,1)S(1)}, bf16[288,768]{1,0:T(8,128)(2,1)S(1)}, u32[]{:S(2)}, u32[]{:S(2)}) collective-permute-start(bf16[288,768]{1,0:T(8,128)(2,1)S(1)} %get-tuple-element.220.refs_1_), channel_id=1, source_target_pairs={{0,1},{1,0},{2,3},{3,2},{4,5},{5,4},{6,7},{7,6},{8,9},{9,8},{10,11... | collective-permute-start | bytes 1327112 | tf_op jit(solution)/shard_map/ppermute | solution.py:46
  190.2 34.8 %collective-permute-start.22 = (bf16[4,192,768]{2,1,0:T(8,128)(2,1)}, bf16[4,192,768]{2,1,0:T(8,128)(2,1)}, u32[]{:S(2)}, u32[]{:S(2)}) collective-permute-start(bf16[4,192,768]{2,1,0:T(8,128)(2,1)} %get-tuple-element.238), channel_id=1, source_target_pairs={{0,2},{1,3},{2,0},{3,1},{4,6},{5,7},{6,4},{7,5},{8,10},{9,11},{10,... | collective-permute-start | bytes 3538952 | tf_op jit(solution)/shard_map/ppermute | solution.py:46
  191.5 34.2 %collective-permute-start.23 = (bf16[8,192,384]{2,1,0:T(8,128)(2,1)}, bf16[8,192,384]{2,1,0:T(8,128)(2,1)}, u32[]{:S(2)}, u32[]{:S(2)}) collective-permute-start(bf16[8,192,384]{2,1,0:T(8,128)(2,1)} %get-tuple-element.239), channel_id=1, source_target_pairs={{0,16},{16,0},{1,17},{17,1},{2,18},{18,2},{3,19},{19,3},{4,20},{20... | collective-permute-start | bytes 3538952 | tf_op jit(solution)/shard_map/ppermute | solution.py:46
  193.0 1.8 collective-permute-start.19
  193.0 2.4 collective-permute-start.20
  193.5 2.5 collective-permute-start.21
  194.8 34.8 %collective-permute-start.12 = (bf16[2,288,768]{2,1,0:T(8,128)(2,1)S(1)}, bf16[2,288,768]{2,1,0:T(8,128)(2,1)S(1)}, u32[]{:S(2)}, u32[]{:S(2)}) collective-permute-start(bf16[2,288,768]{2,1,0:T(8,128)(2,1)S(1)} %get-tuple-element.194.x_ref.ctx.n), channel_id=1, source_target_pairs={{0,1},{1,0},{2,3},{3,2},{4,5},{5,4},{6,7},{7,6},{8,9},{9,8},{10,11... | collective-permute-start | bytes 2654216 | tf_op jit(solution)/shard_map/ppermute | solution.py:46
  195.4 34.9 %collective-permute-start.26 = (bf16[8,288,192]{2,1,0:T(8,128)(2,1)}, bf16[8,288,192]{2,1,0:T(8,128)(2,1)}, u32[]{:S(2)}, u32[]{:S(2)}) collective-permute-start(bf16[8,288,192]{2,1,0:T(8,128)(2,1)} %get-tuple-element.249), channel_id=1, source_target_pairs={{0,1},{1,0},{2,3},{3,2},{4,5},{5,4},{6,7},{7,6},{8,9},{9,8},{10,11... | collective-permute-start | bytes 2654216 | tf_op jit(solution)/shard_map/ppermute | solution.py:46
  224.8 6.7 %collective-permute-start.25 = (bf16[2,288,768]{2,1,0:T(8,128)(2,1)S(1)}, bf16[2,288,768]{2,1,0:T(8,128)(2,1)S(1)}, u32[]{:S(2)}, u32[]{:S(2)}) collective-permute-start(bf16[2,288,768]{2,1,0:T(8,128)(2,1)S(1)} %get-tuple-element.248.refs_10_.dy), channel_id=1, source_target_pairs={{0,1},{1,0},{2,3},{3,2},{4,5},{5,4},{6,7},{7,6},{8,9},{9,8},{10,11... | collective-permute-start | bytes 2654216 | tf_op jit(solution)/shard_map/ppermute | solution.py:46
  225.0 30.6 %collective-permute-start.33 = (bf16[4,48,1536]{2,1,0:T(8,128)(2,1)}, bf16[4,48,1536]{2,1,0:T(8,128)(2,1)S(1)}, u32[]{:S(2)}, u32[]{:S(2)}) collective-permute-start(bf16[4,48,1536]{2,1,0:T(8,128)(2,1)} %get-tuple-element.286), channel_id=1, source_target_pairs={{0,2},{1,3},{2,0},{3,1},{4,6},{5,7},{6,4},{7,5},{8,10},{9,11},{10,... | collective-permute-start | bytes 1769480 | tf_op jit(solution)/shard_map/ppermute | solution.py:46
  225.8 18.7 %collective-permute-start.24 = (bf16[8,288,192]{2,1,0:T(8,128)(2,1)}, bf16[8,288,192]{2,1,0:T(8,128)(2,1)S(1)}, u32[]{:S(2)}, u32[]{:S(2)}) collective-permute-start(bf16[8,288,192]{2,1,0:T(8,128)(2,1)} %get-tuple-element.247), channel_id=1, source_target_pairs={{0,1},{1,0},{2,3},{3,2},{4,5},{5,4},{6,7},{7,6},{8,9},{9,8},{10,11... | collective-permute-start | bytes 2654216 | tf_op jit(solution)/shard_map/ppermute | solution.py:46
  229.7 25.9 %collective-permute-start.34 = (bf16[8,48,768]{2,1,0:T(8,128)(2,1)S(1)}, bf16[8,48,768]{2,1,0:T(8,128)(2,1)S(1)}, u32[]{:S(2)}, u32[]{:S(2)}) collective-permute-start(bf16[8,48,768]{2,1,0:T(8,128)(2,1)S(1)} %copy-done.90), channel_id=1, source_target_pairs={{0,16},{16,0},{1,17},{17,1},{2,18},{18,2},{3,19},{19,3},{4,20},{20... | collective-permute-start | bytes 1769480 | tf_op jit(solution)/shard_map/ppermute | solution.py:46
  230.3 25.3 %collective-permute-start.36 = (bf16[4,192,384]{2,1,0:T(8,128)(2,1)S(1)}, bf16[4,192,384]{2,1,0:T(8,128)(2,1)S(1)}, u32[]{:S(2)}, u32[]{:S(2)}) collective-permute-start(bf16[4,192,384]{2,1,0:T(8,128)(2,1)S(1)} %get-tuple-element.380), channel_id=1, source_target_pairs={{0,2},{1,3},{2,0},{3,1},{4,6},{5,7},{6,4},{7,5},{8,10},{9,11},{10,... | collective-permute-start | bytes 1769480 | tf_op jit(solution)/shard_map/ppermute | solution.py:46
  231.6 26.4 %collective-permute-start.35 = (bf16[4,192,384]{2,1,0:T(8,128)(2,1)S(1)}, bf16[4,192,384]{2,1,0:T(8,128)(2,1)S(1)}, u32[]{:S(2)}, u32[]{:S(2)}) collective-permute-start(bf16[4,192,384]{2,1,0:T(8,128)(2,1)S(1)} %get-tuple-element.382), channel_id=1, source_target_pairs={{0,16},{16,0},{1,17},{17,1},{2,18},{18,2},{3,19},{19,3},{4,20},{20... | collective-permute-start | bytes 1769480 | tf_op jit(solution)/shard_map/ppermute | solution.py:46
  259.5 105.3 %reduce-scatter.5.cloned.1.call-start = ((), (), s32[]{:S(2)}) async-start(), calls=%async_computation.4 | async-start | bytes 2211840 | tf_op jit(solution)/shard_map/reduce_scatter | solution.py:140
  260.5 2.3 collective-permute-start.27
  260.6 2.7 collective-permute-start.28
  261.0 36.3 %collective-permute-start.37 = (bf16[4,192,768]{2,1,0:T(8,128)(2,1)}, bf16[4,192,768]{2,1,0:T(8,128)(2,1)}, u32[]{:S(2)}, u32[]{:S(2)}) collective-permute-start(bf16[4,192,768]{2,1,0:T(8,128)(2,1)} %get-tuple-element.294), channel_id=1, source_target_pairs={{0,2},{1,3},{2,0},{3,1},{4,6},{5,7},{6,4},{7,5},{8,10},{9,11},{10,... | collective-permute-start | bytes 3538952 | tf_op jit(solution)/shard_map/ppermute | solution.py:46
  262.2 35.0 %collective-permute-start.38 = (bf16[8,192,384]{2,1,0:T(8,128)(2,1)}, bf16[8,192,384]{2,1,0:T(8,128)(2,1)S(1)}, u32[]{:S(2)}, u32[]{:S(2)}) collective-permute-start(bf16[8,192,384]{2,1,0:T(8,128)(2,1)} %get-tuple-element.295), channel_id=1, source_target_pairs={{0,16},{16,0},{1,17},{17,1},{2,18},{18,2},{3,19},{19,3},{4,20},{20... | collective-permute-start | bytes 3538952 | tf_op jit(solution)/shard_map/ppermute | solution.py:46
  262.8 2.8 collective-permute-start.29
  262.8 3.7 collective-permute-start.30
  263.3 3.2 collective-permute-start.31
  265.6 30.0 %collective-permute-start.40 = (bf16[4,48,768]{2,1,0:T(8,128)(2,1)}, bf16[4,48,768]{2,1,0:T(8,128)(2,1)}, u32[]{:S(2)}, u32[]{:S(2)}) collective-permute-start(bf16[4,48,768]{2,1,0:T(8,128)(2,1)} %get-tuple-element.388), channel_id=1, source_target_pairs={{0,2},{1,3},{2,0},{3,1},{4,6},{5,7},{6,4},{7,5},{8,10},{9,11},{10,... | collective-permute-start | bytes 884744 | tf_op jit(solution)/shard_map/ppermute | solution.py:46
  280.6 1.8 collective-permute-start.32
  281.0 15.5 %collective-permute-start.39 = (bf16[4,48,768]{2,1,0:T(8,128)(2,1)S(1)}, bf16[4,48,768]{2,1,0:T(8,128)(2,1)S(1)}, u32[]{:S(2)}, u32[]{:S(2)}) collective-permute-start(bf16[4,48,768]{2,1,0:T(8,128)(2,1)S(1)} %get-tuple-element.390), channel_id=1, source_target_pairs={{0,16},{16,0},{1,17},{17,1},{2,18},{18,2},{3,19},{19,3},{4,20},{20... | collective-permute-start | bytes 884744 | tf_op jit(solution)/shard_map/ppermute | solution.py:46
  282.5 14.0 %collective-permute-start.41 = (bf16[128,768]{1,0:T(8,128)(2,1)S(1)}, bf16[128,768]{1,0:T(8,128)(2,1)S(1)}, u32[]{:S(2)}, u32[]{:S(2)}) collective-permute-start(bf16[128,768]{1,0:T(8,128)(2,1)S(1)} %add_convert_fusion.26.rest_0_), channel_id=1, source_target_pairs={{0,4},{1,5},{2,6},{3,7},{4,0},{5,1},{6,2},{7,3},{8,12},{9,13},{10,... | collective-permute-start | bytes 589832 | tf_op jit(solution)/shard_map/ppermute | solution.py:46
  298.4 17.5 %collective-permute-start.43 = (bf16[4,192,384]{2,1,0:T(8,128)(2,1)}, bf16[4,192,384]{2,1,0:T(8,128)(2,1)S(1)}, u32[]{:S(2)}, u32[]{:S(2)}) collective-permute-start(bf16[4,192,384]{2,1,0:T(8,128)(2,1)} %get-tuple-element.376), channel_id=1, source_target_pairs={{0,2},{1,3},{2,0},{3,1},{4,6},{5,7},{6,4},{7,5},{8,10},{9,11},{10,... | collective-permute-start | bytes 1769480 | tf_op jit(solution)/shard_map/ppermute | solution.py:46
  300.8 15.0 %collective-permute-start.42 = (bf16[4,192,384]{2,1,0:T(8,128)(2,1)S(1)}, bf16[4,192,384]{2,1,0:T(8,128)(2,1)S(1)}, u32[]{:S(2)}, u32[]{:S(2)}) collective-permute-start(bf16[4,192,384]{2,1,0:T(8,128)(2,1)S(1)} %get-tuple-element.378), channel_id=1, source_target_pairs={{0,16},{16,0},{1,17},{17,1},{2,18},{18,2},{3,19},{19,3},{4,20},{20... | collective-permute-start | bytes 1769480 | tf_op jit(solution)/shard_map/ppermute | solution.py:46
  301.5 14.3 %collective-permute-start.44 = (bf16[128,768]{1,0:T(8,128)(2,1)S(1)}, bf16[128,768]{1,0:T(8,128)(2,1)S(1)}, u32[]{:S(2)}, u32[]{:S(2)}) collective-permute-start(bf16[128,768]{1,0:T(8,128)(2,1)S(1)} %add_convert_fusion.25.rest_1_), channel_id=1, source_target_pairs={{0,8},{1,9},{2,10},{3,11},{4,12},{5,13},{6,14},{7,15},{8,0},{9,1},... | collective-permute-start | bytes 589832 | tf_op jit(solution)/shard_map/ppermute | solution.py:46
  313.0 13.9 %collective-permute-start.46 = (bf16[4,48,1536]{2,1,0:T(8,128)(2,1)}, bf16[4,48,1536]{2,1,0:T(8,128)(2,1)}, u32[]{:S(2)}, u32[]{:S(2)}) collective-permute-start(bf16[4,48,1536]{2,1,0:T(8,128)(2,1)} %get-tuple-element.316), channel_id=1, source_target_pairs={{0,2},{1,3},{2,0},{3,1},{4,6},{5,7},{6,4},{7,5},{8,10},{9,11},{10,... | collective-permute-start | bytes 1769480 | tf_op jit(solution)/shard_map/ppermute | solution.py:46
  314.4 13.5 %collective-permute-start.47 = (bf16[8,48,768]{2,1,0:T(8,128)(2,1)}, bf16[8,48,768]{2,1,0:T(8,128)(2,1)}, u32[]{:S(2)}, u32[]{:S(2)}) collective-permute-start(bf16[8,48,768]{2,1,0:T(8,128)(2,1)} %get-tuple-element.317), channel_id=1, source_target_pairs={{0,16},{16,0},{1,17},{17,1},{2,18},{18,2},{3,19},{19,3},{4,20},{20... | collective-permute-start | bytes 1769480 | tf_op jit(solution)/shard_map/ppermute | solution.py:46
  321.4 6.5 %collective-permute-start.45 = (bf16[272,128]{1,0:T(8,128)(2,1)}, bf16[272,128]{1,0:T(8,128)(2,1)S(1)}, u32[]{:S(2)}, u32[]{:S(2)}) collective-permute-start(bf16[272,128]{1,0:T(8,128)(2,1)} %join.1), channel_id=1, source_target_pairs={{0,1},{1,0},{2,3},{3,2},{4,5},{5,4},{6,7},{7,6},{8,9},{9,8},{10,11... | collective-permute-start | bytes 208904 | tf_op jit(solution)/shard_map/ppermute | solution.py:46
  330.0 12.4 %collective-permute-start.50 = (bf16[4,48,768]{2,1,0:T(8,128)(2,1)S(1)}, bf16[4,48,768]{2,1,0:T(8,128)(2,1)S(1)}, u32[]{:S(2)}, u32[]{:S(2)}) collective-permute-start(bf16[4,48,768]{2,1,0:T(8,128)(2,1)S(1)} %get-tuple-element.384), channel_id=1, source_target_pairs={{0,2},{1,3},{2,0},{3,1},{4,6},{5,7},{6,4},{7,5},{8,10},{9,11},{10,... | collective-permute-start | bytes 884744 | tf_op jit(solution)/shard_map/ppermute | solution.py:46
  333.1 9.3 %collective-permute-start.49 = (bf16[4,48,768]{2,1,0:T(8,128)(2,1)}, bf16[4,48,768]{2,1,0:T(8,128)(2,1)S(1)}, u32[]{:S(2)}, u32[]{:S(2)}) collective-permute-start(bf16[4,48,768]{2,1,0:T(8,128)(2,1)} %get-tuple-element.386), channel_id=1, source_target_pairs={{0,16},{16,0},{1,17},{17,1},{2,18},{18,2},{3,19},{19,3},{4,20},{20... | collective-permute-start | bytes 884744 | tf_op jit(solution)/shard_map/ppermute | solution.py:46
  334.4 8.1 %collective-permute-start.51 = (bf16[128,768]{1,0:T(8,128)(2,1)S(1)}, bf16[128,768]{1,0:T(8,128)(2,1)S(1)}, u32[]{:S(2)}, u32[]{:S(2)}) collective-permute-start(bf16[128,768]{1,0:T(8,128)(2,1)S(1)} %add_convert_fusion.24), channel_id=1, source_target_pairs={{0,2},{1,3},{2,0},{3,1},{4,6},{5,7},{6,4},{7,5},{8,10},{9,11},{10,... | collective-permute-start | bytes 589832 | tf_op jit(solution)/shard_map/ppermute | solution.py:46
  335.7 6.8 %collective-permute-start.48 = (bf16[272,128]{1,0:T(8,128)(2,1)S(1)}, bf16[272,128]{1,0:T(8,128)(2,1)S(1)}, u32[]{:S(2)}, u32[]{:S(2)}) collective-permute-start(bf16[272,128]{1,0:T(8,128)(2,1)S(1)} %add_convert_fusion.37), channel_id=1, source_target_pairs={{0,2},{1,3},{2,0},{3,1},{4,6},{5,7},{6,4},{7,5},{8,10},{9,11},{10,... | collective-permute-start | bytes 208904 | tf_op jit(solution)/shard_map/ppermute | solution.py:46
  342.5 5.2 %collective-permute-start.52 = (bf16[272,128]{1,0:T(8,128)(2,1)S(1)}, bf16[272,128]{1,0:T(8,128)(2,1)S(1)}, u32[]{:S(2)}, u32[]{:S(2)}) collective-permute-start(bf16[272,128]{1,0:T(8,128)(2,1)S(1)} %add_convert_fusion.36), channel_id=1, source_target_pairs={{0,16},{16,0},{1,17},{17,1},{2,18},{18,2},{3,19},{19,3},{4,20},{20... | collective-permute-start | bytes 208904 | tf_op jit(solution)/shard_map/ppermute | solution.py:46
  343.6 10.6 %collective-permute-start.54 = (bf16[384,384]{1,0:T(8,128)(2,1)S(1)}, bf16[384,384]{1,0:T(8,128)(2,1)S(1)}, u32[]{:S(2)}, u32[]{:S(2)}) collective-permute-start(bf16[384,384]{1,0:T(8,128)(2,1)S(1)} %bitcast.100), channel_id=1, source_target_pairs={{0,16},{16,0},{1,17},{17,1},{2,18},{18,2},{3,19},{19,3},{4,20},{20... | collective-permute-start | bytes 884744 | tf_op jit(solution)/shard_map/ppermute | solution.py:46
  344.7 9.5 %collective-permute-start.53 = (bf16[128,768]{1,0:T(8,128)(2,1)S(1)}, bf16[128,768]{1,0:T(8,128)(2,1)S(1)}, u32[]{:S(2)}, u32[]{:S(2)}) collective-permute-start(bf16[128,768]{1,0:T(8,128)(2,1)S(1)} %add_convert_fusion.23), channel_id=1, source_target_pairs={{0,16},{16,0},{1,17},{17,1},{2,18},{18,2},{3,19},{19,3},{4,20},{20... | collective-permute-start | bytes 589832 | tf_op jit(solution)/shard_map/ppermute | solution.py:46
  346.0 15.6 %collective-permute-start.57 = (bf16[2,96,768]{2,1,0:T(8,128)(2,1)S(1)}, bf16[2,96,768]{2,1,0:T(8,128)(2,1)S(1)}, u32[]{:S(2)}, u32[]{:S(2)}) collective-permute-start(bf16[2,96,768]{2,1,0:T(8,128)(2,1)S(1)} %pad_maximum_fusion.5), channel_id=1, source_target_pairs={{0,4},{1,5},{2,6},{3,7},{4,0},{5,1},{6,2},{7,3},{8,12},{9,13},{10,... | collective-permute-start | bytes 884744 | tf_op jit(solution)/shard_map/ppermute | solution.py:46
  354.2 11.8 %collective-permute-start.55 = (bf16[272,128]{1,0:T(8,128)(2,1)S(1)}, bf16[272,128]{1,0:T(8,128)(2,1)S(1)}, u32[]{:S(2)}, u32[]{:S(2)}) collective-permute-start(bf16[272,128]{1,0:T(8,128)(2,1)S(1)} %add_convert_fusion.35), channel_id=1, source_target_pairs={{0,4},{1,5},{2,6},{3,7},{4,0},{5,1},{6,2},{7,3},{8,12},{9,13},{10,... | collective-permute-start | bytes 208904 | tf_op jit(solution)/shard_map/ppermute | solution.py:46
  356.8 15.0 %collective-permute-start.61 = (bf16[128,768]{1,0:T(8,128)(2,1)S(1)}, bf16[128,768]{1,0:T(8,128)(2,1)S(1)}, u32[]{:S(2)}, u32[]{:S(2)}) collective-permute-start(bf16[128,768]{1,0:T(8,128)(2,1)S(1)} %add_convert_fusion.22), channel_id=1, source_target_pairs={{0,1},{1,0},{2,3},{3,2},{4,5},{5,4},{6,7},{7,6},{8,9},{9,8},{10,11... | collective-permute-start | bytes 589832 | tf_op jit(solution)/shard_map/ppermute | solution.py:46
  361.7 8.4 %collective-permute-start.58 = (bf16[1,96,768]{2,1,0:T(8,128)(2,1)S(1)}, bf16[1,96,768]{2,1,0:T(8,128)(2,1)S(1)}, u32[]{:S(2)}, u32[]{:S(2)}) collective-permute-start(bf16[1,96,768]{2,1,0:T(8,128)(2,1)S(1)} %get-tuple-element.391), channel_id=1, source_target_pairs={{0,8},{1,9},{2,10},{3,11},{4,12},{5,13},{6,14},{7,15},{8,0},{9,1},... | collective-permute-start | bytes 442376 | tf_op jit(solution)/shard_map/ppermute | solution.py:46
  364.8 15.3 %collective-permute-start.60 = (bf16[576,384]{1,0:T(8,128)(2,1)}, bf16[576,384]{1,0:T(8,128)(2,1)S(1)}, u32[]{:S(2)}, u32[]{:S(2)}) collective-permute-start(bf16[576,384]{1,0:T(8,128)(2,1)} %bitcast.96), channel_id=1, source_target_pairs={{0,16},{16,0},{1,17},{17,1},{2,18},{18,2},{3,19},{19,3},{4,20},{20... | collective-permute-start | bytes 1327112 | tf_op jit(solution)/shard_map/ppermute | solution.py:46
  370.2 12.0 %collective-permute-start.59 = (bf16[96,768]{1,0:T(8,128)(2,1)S(1)}, bf16[96,768]{1,0:T(8,128)(2,1)S(1)}, u32[]{:S(2)}, u32[]{:S(2)}) collective-permute-start(bf16[96,768]{1,0:T(8,128)(2,1)S(1)} %fusion.16.refs_0_), channel_id=1, source_target_pairs={{0,16},{16,0},{1,17},{17,1},{2,18},{18,2},{3,19},{19,3},{4,20},{20... | collective-permute-start | bytes 442376 | tf_op jit(solution)/shard_map/ppermute | solution.py:46
  371.8 5.3 %collective-permute-start.56 = (bf16[272,128]{1,0:T(8,128)(2,1)S(1)}, bf16[272,128]{1,0:T(8,128)(2,1)S(1)}, u32[]{:S(2)}, u32[]{:S(2)}) collective-permute-start(bf16[272,128]{1,0:T(8,128)(2,1)S(1)} %add_convert_fusion.34.left), channel_id=1, source_target_pairs={{0,8},{1,9},{2,10},{3,11},{4,12},{5,13},{6,14},{7,15},{8,0},{9,1},... | collective-permute-start | bytes 208904 | tf_op jit(solution)/shard_map/ppermute | solution.py:46
  (93 other events, 1057.3 us)
Sparse Core Ops, SparseCore 0:
  10.2 102.2 all-gather.1
  259.6 28.2 reduce-scatter.2
  319.9 44.7 reduce-scatter.4

commit v3 on v2

--- a/solution.py
+++ b/solution.py
@@ -1450,7 +1450,11 @@
         )
         grads_mate = [flipped(part, "tp", 0) for part in grads]
         weights = ffn_grads(me, pair, pair_mate, low, low_mate, dh, dh_mate, act, act_mate)
-        if not last:
+        if last:
+            *weights, grads_mate = (lambda out: (*out[:4], list(out[4:])))(
+                tied((*weights, *grads_mate), ())
+            )
+        else:
             weights = tied(weights, projections[-1].underway() + ffns[-1].underway())
             projections[-1].second(weights[0])
             upper = Scattered([ffns[-1]], weights[0])

time: 394 us -> 391 us (level)
  transfers between devices with their start and end apart: 65 -> 65, of which waited for: 24 -> 21; matrix products, arithmetic and copies ran while one was open for 6% -> 6% of each run, Pallas kernels for 35% -> 35%
where the time goes in v3:
time: 391 us; the launch traced here: 388 us
  Pallas kernels  187 us (48%)
  waiting for transfers between devices  77.6 us (20%)
  starting transfers between devices  58.1 us (15%)
  local copies, waits for them, and re-layouts  22.1 us (6%)
  other arithmetic  21.8 us (6%)
  between operations  15.3 us (4%)
  matrix products  5.81 us (1%)
    ppermute x62, starting transfers between devices, flipped(): return lax.ppermute(block, axis, [(i, i ^ 1 << bit) for i in range(count)])  58 us
    ppermute x62, waiting for transfers between devices, flipped(): return lax.ppermute(block, axis, [(i, i ^ 1 << bit) for i in range(count)])  48.9 us
    all_gather x1, waiting for transfers between devices, body(): gathered = lax.all_gather(packed, 'tp', axis=0)  28.1 us
    pallas_call x2, Pallas kernels, ffn(): pl.pallas_call(functools.partial(ffn_kernel, layer, more), out_shape=out_...  24.9 us
    pallas_call x2, Pallas kernels, ffn_back(): pl.pallas_call(functools.partial(ffn_back_kernel, layer), out_shape=[half...  24.3 us
    pallas_call x2, Pallas kernels, attend(): pl.pallas_call(functools.partial(attend_kernel, layer), grid=(STEPS,), in...  23.4 us
    pallas_call x2, Pallas kernels, projection_grads(): pl.pallas_call(functools.partial(projection_kernel, by_distance), out_sha...  22.9 us
    pallas_call x1, Pallas kernels, make_bias(): pl.pallas_call(bias_kernel, out_shape=jax.ShapeDtypeStruct((HEADS, ROWS,...  21.4 us
  transfers between devices with their start and end apart: 65, of which 21 were waited for; matrix products, arithmetic and copies ran while one was open for 6% of the time, Pallas kernels for 35%

profile of v3, /device:TPU:0, one launch (start us, length us, event | category | flops | bytes accessed | tf_op | source)
XLA Modules:
  0.0 387.7 jit_solution(7123435764299307571)
XLA Ops:
  7.2 2.3 pad_maximum_fusion.1
  11.7 2.9 collective-permute-start.1
  14.7 1.6 collective-permute-done.1
  16.2 2.1 collective-permute-start.2
  18.4 1.6 collective-permute-done.2
  19.9 3.0 collective-permute-start.3
  23.0 1.7 collective-permute-done.3
  24.6 1.8 collective-permute-start.4
  29.8 1.8 convolution_convert_fusion
  31.6 1.9 fusion.1
  34.7 1.9 collective-permute-start.8
  40.3 21.4 %score_bias.1.bias = f32[12,288,640]{2,1,0:T(8,128)} custom-call(s32[2]{0:T(128)S(1)} %pad_add_fusion.1.facts, s32[2,256]{1,0:T(2,128)S(1)} %copy-done.45, s32[2,256]{1,0:T(2,128)S(1)} %collective-permute-done.6.other_boxes, f32[12,8,128]{2,1,0:T(8,128)S(1)} %broadcast_in_dim.48.table_a, f32[12,8,128]{2,1,0:T(8,128)S(1)} %broadcast_in_dim.49.table_b), custom_call_target="tpu_custom_call" | custom-call | flops 1 | bytes 1 | tf_op jit(solution)/shard_map/score_bias/pallas_call | solution.py:246
  61.7 1.6 collective-permute-start.9
  63.3 1.9 fusion.q_ref
  65.6 2.6 collective-permute-start.10
  68.2 2.4 collective-permute-done.10
  71.7 11.7 %attend.2 = (bf16[12,288,640]{2,1,0:T(8,128)(2,1)}, bf16[2,288,768]{2,1,0:T(8,128)(2,1)S(1)}, f32[288,768]{1,0:T(8,128)S(1)}, f32[288,768]{1,0:T(8,128)S(1)}) custom-call(bf16[288,768]{1,0:T(8,128)(2,1)S(1)} %fusion.q_ref, bf16[288,2304]{1,0:T(8,128)(2,1)} %copy-done.46, bf16[288,2304]{1,0:T(8,128)(2,1)} %copy-done.47, bf16[288,2304]{1,0:T(8,128)(2,1)} %copy-done.46, ...), custom_call_target="tpu_custom_call" | custom-call | flops 1 | bytes 1 | tf_op jit(solution)/shard_map/attend/pallas_call | solution.py:755
  84.4 28.1 %all-gather.2.cloned.1.call-done.refs_0_.refs_1_.refs_2_.refs_3_ = bf16[16,384,1536]{2,1,0:T(8,128)(2,1)} async-done(((bf16[1,384,1536]{2,1,0:T(8,128)(2,1)}), bf16[16,384,1536]{2,1,0:T(8,128)(2,1)}) %all-gather.2.cloned.1.call-update) | async-done | bytes 18874384 | tf_op jit(solution)/shard_map/all_gather | solution.py:1369
  112.5 13.2 %feed_forward.2 = (bf16[8,288,192]{2,1,0:T(8,128)(2,1)}, bf16[8,288,192]{2,1,0:T(8,128)(2,1)}, bf16[16,288,192]{2,1,0:T(8,128)(2,1)}, f32[288,768]{1,0:T(8,128)S...) custom-call(s32[2]{0:T(128)S(1)} %pad_add_fusion.me, ...), custom_call_target="tpu_custom_call" | custom-call | flops 1 | bytes 1 | tf_op jit(solution)/shard_map/feed_forward/pallas_call | solution.py:938
  126.0 3.0 collective-permute-done.11.kp.vp.x_mate
  130.1 11.7 %attend.3 = (bf16[12,288,640]{2,1,0:T(8,128)(2,1)}, bf16[2,288,768]{2,1,0:T(8,128)(2,1)S(1)}, f32[288,768]{1,0:T(8,128)S(1)}, f32[288,768]{1,0:T(8,128)S(1)}) custom-call(bf16[288,768]{1,0:T(8,128)(2,1)S(1)} %get-tuple-element.209.q_ref, bf16[288,2304]{1,0:T(8,128)(2,1)} %get-tuple-element.210.ko.vo.x, bf16[288,2304]{1,0:T(8,128)(2,1)} %copy-done.48, ...), custom_call_target="tpu_custom_call" | custom-call | flops 1 | bytes 1 | tf_op jit(solution)/shard_map/attend/pallas_call | solution.py:755
  141.8 11.8 %feed_forward.3 = (bf16[8,288,192]{2,1,0:T(8,128)(2,1)S(1)}, bf16[8,288,192]{2,1,0:T(8,128)(2,1)}, bf16[16,288,192]{2,1,0:T(8,128)(2,1)}, f32[288,768]{1,0:T(8,128)S(1)}, bf16[288,768]{1,0:T(8,128)(2,1)}) custom-call(s32[2]{0:T(128)S(1)} %pad_add_fusion.me, bf16[2,288,768]{2,1,0:T(8,128)(2,1)S(1)} %get-tuple-element.212.x_ref.n.ctx, ...), custom_call_target="tpu_custom_call" | custom-call | flops 1 | bytes 1 | tf_op jit(solution)/shard_map/feed_forward/pallas_call | solution.py:938
  154.6 12.1 %feed_forward_back.2 = (bf16[8,288,192]{2,1,0:T(8,128)(2,1)}, bf16[8,288,192]{2,1,0:T(8,128)(2,1)}, bf16[2,288,768]{2,1,0:T(8,128)(2,1)S(1)}, f32[16,1,192]{2,1,...) custom-call(s32[2]{0:T(128)S(1)} %pad_add_fusion.me, ...), custom_call_target="tpu_custom_call" | custom-call | flops 1 | bytes 1 | tf_op jit(solution)/shard_map/feed_forward_back/pallas_call | solution.py:1011
  168.7 10.6 %attend_back.2 = (bf16[12,288,640]{2,1,0:T(8,128)(2,1)}, bf16[288,768]{1,0:T(8,128)(2,1)S(1)}, bf16[288,768]{1,0:T(8,128)(2,1)S(1)}, bf16[288,768]{1,0:T(8,128)(...) custom-call(bf16[288,768]{1,0:T(8,128)(2,1)S(1)} %get-tuple-element.209.q_ref, ...), custom_call_target="tpu_custom_call" | custom-call | flops 1 | bytes 1 | tf_op jit(solution)/shard_map/attend_back/pallas_call | solution.py:827
  180.7 9.9 %feed_forward_grads.2 = (bf16[4,192,768]{2,1,0:T(8,128)(2,1)}, bf16[4,192,768]{2,1,0:T(8,128)(2,1)}, bf16[8,192,384]{2,1,0:T(8,128)(2,1)}, bf16[8,192,384]{2,1,0:T(8,128)(2,1)}) custom-call(s32[2]{0:T(128)S(1)} %pad_add_fusion.me, bf16[2,288,768]{2,1,0:T(8,128)(2,1)S(1)} %get-tuple-element.212.x_ref.n.ctx, ...), custom_call_target="tpu_custom_call" | custom-call | flops 1 | bytes 1 | tf_op jit(solution)/shard_map/feed_forward_grads/pallas_call | solution.py:1101
  190.6 1.3 collective-permute-start.22
  192.0 1.5 collective-permute-start.23
  194.0 11.8 %projection_grads.2 = (bf16[4,48,1536]{2,1,0:T(8,128)(2,1)}, bf16[4,48,1536]{2,1,0:T(8,128)(2,1)}, bf16[8,48,768]{2,1,0:T(8,128)(2,1)}, bf16[8,48,768]{2,1,0:T(8...) custom-call(s32[2]{0:T(128)S(1)} %pad_add_fusion.me, bf16[288,2304]{1,0:T(8,128)(2,1)} %get-tuple-element.210.ko.vo.x, ...), custom_call_target="tpu_custom_call" | custom-call | flops 1 | bytes 1 | tf_op jit(solution)/shard_map/projection_grads/pallas_call | solution.py:1232
  206.9 12.1 %feed_forward_back.3 = (bf16[8,288,192]{2,1,0:T(8,128)(2,1)}, bf16[8,288,192]{2,1,0:T(8,128)(2,1)}, bf16[2,288,768]{2,1,0:T(8,128)(2,1)S(1)}, f32[16,1,192]{2,1,...) custom-call(s32[2]{0:T(128)S(1)} %pad_add_fusion.me, ...), custom_call_target="tpu_custom_call" | custom-call | flops 1 | bytes 1 | tf_op jit(solution)/shard_map/feed_forward_back/pallas_call | solution.py:1011
  223.0 2.0 add_convert_fusion.8
  225.0 1.8 add_convert_fusion.9
  228.7 1.5 collective-permute-start.35
  230.2 10.6 %attend_back.3 = (bf16[12,288,640]{2,1,0:T(8,128)(2,1)}, bf16[288,768]{1,0:T(8,128)(2,1)S(1)}, bf16[288,768]{1,0:T(8,128)(2,1)S(1)}, bf16[288,768]{1,0:T(8,128)(...) custom-call(bf16[288,768]{1,0:T(8,128)(2,1)S(1)} %copy-done.11, bf16[288,2304]{1,0:T(8,128)(2,1)} %copy-done.46, ...), custom_call_target="tpu_custom_call" | custom-call | flops 1 | bytes 1 | tf_op jit(solution)/shard_map/attend_back/pallas_call | solution.py:827
  242.7 10.0 %feed_forward_grads.3 = (bf16[4,192,768]{2,1,0:T(8,128)(2,1)}, bf16[4,192,768]{2,1,0:T(8,128)(2,1)}, bf16[8,192,384]{2,1,0:T(8,128)(2,1)}, bf16[8,192,384]{2,1,0:T(8,128)(2,1)}) custom-call(s32[2]{0:T(128)S(1)} %pad_add_fusion.me, bf16[2,288,768]{2,1,0:T(8,128)(2,1)S(1)} %get-tuple-element.203.x_ref.ctx.n, ...), custom_call_target="tpu_custom_call" | custom-call | flops 1 | bytes 1 | tf_op jit(solution)/shard_map/feed_forward_grads/pallas_call | solution.py:1101
  252.8 2.3 collective-permute-done.35
  260.5 2.2 add_convert_fusion.16
  264.3 11.1 %projection_grads.3 = (bf16[4,48,1536]{2,1,0:T(8,128)(2,1)}, bf16[4,48,1536]{2,1,0:T(8,128)(2,1)}, bf16[8,48,768]{2,1,0:T(8,128)(2,1)}, bf16[8,48,768]{2,1,0:T(8...) custom-call(s32[2]{0:T(128)S(1)} %pad_add_fusion.me, bf16[288,2304]{1,0:T(8,128)(2,1)} %copy-done.46, ...), custom_call_target="tpu_custom_call" | custom-call | flops 1 | bytes 1 | tf_op jit(solution)/shard_map/projection_grads/pallas_call | solution.py:1232
  275.5 2.2 visual_back.1
  278.1 1.5 collective-permute-start.39
  279.6 1.8 collective-permute-start.41
  281.4 9.0 %table_grad.2.rest_0_.refs_7_ = f32[6,8,128]{2,1,0:T(8,128)} custom-call(bf16[640,256]{1,0:T(8,128)(2,1)} %copy-done.12, bf16[224,288]{1,0:T(8,128)(2,1)} %copy-done.19, bf16[4,288,640]{2,1,0:T(8,128)(2,1)} %copy-done.2, bf16[12,288,640]{2,1,0:T(8,128)(2,1)} %get-tuple-element.287.ds_a, bf16[12,288,640]{2,1,0:T(8,128)(2,1)} %get-tuple-element.288.ds_b, ...), custom_call_target="tpu_custom_call" | custom-call | flops 1 | bytes 1 | tf_op jit(solution)/shard_map/table_grad/pallas_call | solution.py:392
  290.3 2.4 collective-permute-done.40
  296.2 1.7 add_convert_fusion.3
  298.6 2.5 collective-permute-start.44
  301.1 9.1 %table_grad.3.refs_8_ = f32[6,8,128]{2,1,0:T(8,128)} custom-call(bf16[640,256]{1,0:T(8,128)(2,1)} %copy-done.12, bf16[224,288]{1,0:T(8,128)(2,1)} %copy-done.19, bf16[4,288,640]{2,1,0:T(8,128)(2,1)} %copy-done.2, bf16[12,288,640]{2,1,0:T(8,128)(2,1)} %get-tuple-element.287.ds_a, bf16[12,288,640]{2,1,0:T(8,128)(2,1)} %get-tuple-element.288.ds_b, ...), custom_call_target="tpu_custom_call" | custom-call | flops 1 | bytes 1 | tf_op jit(solution)/shard_map/table_grad/pallas_call | solution.py:392
  310.1 1.3 collective-permute-start.46
  311.5 1.5 collective-permute-start.47
  316.9 1.6 join.1
  318.5 5.5 %collective-permute-done.46 = bf16[4,48,1536]{2,1,0:T(8,128)(2,1)} collective-permute-done((bf16[4,48,1536]{2,1,0:T(8,128)(2,1)}, bf16[4,48,1536]{2,1,0:T(8,128)(2,1)}, u32[]{:S(2)}, u32[]{:S(2)}) %collective-permute-start.46) | collective-permute-done | bytes 589856 | tf_op jit(solution)/shard_map/ppermute | solution.py:46
  328.2 2.0 add_convert_fusion.13
  331.4 1.3 collective-permute-start.51
  334.5 5.1 %collective-permute-done.48 = bf16[272,128]{1,0:T(8,128)(2,1)S(1)} collective-permute-done((bf16[272,128]{1,0:T(8,128)(2,1)S(1)}, bf16[272,128]{1,0:T(8,128)(2,1)S(1)}, u32[]{:S(2)}, u32[]{:S(2)}) %collective-permute-start.48) | collective-permute-done | bytes 69664 | tf_op jit(solution)/shard_map/ppermute | solution.py:46
  343.0 1.3 collective-permute-start.57
  344.8 6.5 %collective-permute-done.53 = bf16[128,768]{1,0:T(8,128)(2,1)S(1)} collective-permute-done((bf16[128,768]{1,0:T(8,128)(2,1)S(1)}, bf16[128,768]{1,0:T(8,128)(2,1)S(1)}, u32[]{:S(2)}, u32[]{:S(2)}) %collective-permute-start.53) | collective-permute-done | bytes 196640 | tf_op jit(solution)/shard_map/ppermute | solution.py:46
  351.3 2.5 collective-permute-start.55
  353.9 4.7 %collective-permute-done.57 = bf16[2,96,768]{2,1,0:T(8,128)(2,1)S(1)} collective-permute-done((bf16[2,96,768]{2,1,0:T(8,128)(2,1)S(1)}, bf16[2,96,768]{2,1,0:T(8,128)(2,1)S(1)}, u32[]{:S(2)}, u32[]{:S(2)}) %collective-permute-start.57) | collective-permute-done | bytes 294944 | tf_op jit(solution)/shard_map/ppermute | solution.py:46
  358.8 2.5 collective-permute-start.58
  361.8 1.3 collective-permute-start.60
  363.1 4.0 %collective-permute-done.58 = bf16[1,96,768]{2,1,0:T(8,128)(2,1)S(1)} collective-permute-done((bf16[1,96,768]{2,1,0:T(8,128)(2,1)S(1)}, bf16[1,96,768]{2,1,0:T(8,128)(2,1)S(1)}, u32[]{:S(2)}, u32[]{:S(2)}) %collective-permute-start.58) | collective-permute-done | bytes 147488 | tf_op jit(solution)/shard_map/ppermute | solution.py:46
  367.2 1.6 collective-permute-start.59
  370.4 3.8 collective-permute-done.56.right
  374.8 2.3 split.1
  377.2 2.1 feed_forward_out.1
  379.3 1.6 projections_out.1
  (348 shorter events, 57.3 us)
Async XLA Ops:
  7.2 105.3 %all-gather.2.cloned.1.call-start = ((), (), s32[]{:S(2)}) async-start(), calls=%async_computation.2 | async-start | bytes 20054016 | tf_op jit(solution)/shard_map/all_gather | solution.py:1369
  9.7 284.6 %reduce-scatter.3.cloned.1.call-start = ((), (), s32[]{:S(2)}) async-start(), calls=%async_computation.3 | async-start | bytes 1474560 | tf_op jit(solution)/shard_map/reduce_scatter | solution.py:140
  10.9 25.7 %collective-permute-start.6 = (s32[2,256]{1,0:T(2,128)S(1)}, s32[2,256]{1,0:T(2,128)S(1)}, u32[]{:S(2)}, u32[]{:S(2)}) collective-permute-start(s32[2,256]{1,0:T(2,128)S(1)} %copy-done.45), channel_id=1, source_target_pairs={{0,1},{1,0},{2,3},{3,2},{4,5},{5,4},{6,7},{7,6},{8,9},{9,8},{10,11... | collective-permute-start | bytes 6152 | tf_op jit(solution)/shard_map/ppermute | solution.py:46
  11.7 4.5 %collective-permute-start.1 = (f32[2,256]{1,0:T(2,128)S(1)}, f32[2,256]{1,0:T(2,128)S(1)}, u32[]{:S(2)}, u32[]{:S(2)}) collective-permute-start(f32[2,256]{1,0:T(2,128)S(1)} %fusion.23), channel_id=1, source_target_pairs={{0,2},{1,3},{2,0},{3,1},{4,6},{5,7},{6,4},{7,5},{8,10},{9,11},{10,... | collective-permute-start | bytes 6152 | tf_op jit(solution)/shard_map/ppermute | solution.py:46
  14.7 20.0 %collective-permute-start.7 = (f32[1,2,192]{2,1,0:T(2,128)S(1)}, f32[1,2,192]{2,1,0:T(2,128)S(1)}, u32[]{:S(2)}, u32[]{:S(2)}) collective-permute-start(f32[1,2,192]{2,1,0:T(2,128)S(1)} %bitcast_convert_fusion), channel_id=1, source_target_pairs={{0,1},{1,0},{2,3},{3,2},{4,5},{5,4},{6,7},{7,6},{8,9},{9,8},{10,11... | collective-permute-start | bytes 4616 | tf_op jit(solution)/shard_map/ppermute | solution.py:46
  16.2 3.7 collective-permute-start.2
  19.9 4.7 %collective-permute-start.3 = (f32[2,256]{1,0:T(2,128)S(1)}, f32[2,256]{1,0:T(2,128)S(1)}, u32[]{:S(2)}, u32[]{:S(2)}) collective-permute-start(f32[2,256]{1,0:T(2,128)S(1)} %add.239), channel_id=1, source_target_pairs={{0,8},{1,9},{2,10},{3,11},{4,12},{5,13},{6,14},{7,15},{8,0},{9,1},... | collective-permute-start | bytes 6152 | tf_op jit(solution)/shard_map/ppermute | solution.py:46
  24.6 3.6 collective-permute-start.4
  33.7 36.9 %collective-permute-start.5 = (bf16[288,2304]{1,0:T(8,128)(2,1)S(1)}, bf16[288,2304]{1,0:T(8,128)(2,1)S(1)}, u32[]{:S(2)}, u32[]{:S(2)}) collective-permute-start(bf16[288,2304]{1,0:T(8,128)(2,1)S(1)} %pad_maximum_fusion.ko.vo.x), channel_id=1, source_target_pairs={{0,1},{1,0},{2,3},{3,2},{4,5},{5,4},{6,7},{7,6},{8,9},{9,8},{10,11... | collective-permute-start | bytes 3981320 | tf_op jit(solution)/shard_map/ppermute | solution.py:46
  34.7 27.0 %collective-permute-start.8 = (f32[2,2,192]{2,1,0:T(2,128)S(1)}, f32[2,2,192]{2,1,0:T(2,128)S(1)}, u32[]{:S(2)}, u32[]{:S(2)}) collective-permute-start(f32[2,2,192]{2,1,0:T(2,128)S(1)} %pad_maximum_fusion.8), channel_id=1, source_target_pairs={{0,2},{1,3},{2,0},{3,1},{4,6},{5,7},{6,4},{7,5},{8,10},{9,11},{10,... | collective-permute-start | bytes 9224 | tf_op jit(solution)/shard_map/ppermute | solution.py:46
  61.7 3.9 collective-permute-start.9
  65.6 5.0 %collective-permute-start.10 = (f32[8,2,192]{2,1,0:T(2,128)S(1)}, f32[8,2,192]{2,1,0:T(2,128)S(1)}, u32[]{:S(2)}, u32[]{:S(2)}) collective-permute-start(f32[8,2,192]{2,1,0:T(2,128)S(1)} %pad_maximum_fusion.6), channel_id=1, source_target_pairs={{0,8},{1,9},{2,10},{3,11},{4,12},{5,13},{6,14},{7,15},{8,0},{9,1},... | collective-permute-start | bytes 36872 | tf_op jit(solution)/shard_map/ppermute | solution.py:46
  125.6 3.3 collective-permute-start.11
  167.6 11.6 %collective-permute-start.14 = (bf16[8,288,192]{2,1,0:T(8,128)(2,1)}, bf16[8,288,192]{2,1,0:T(8,128)(2,1)S(1)}, u32[]{:S(2)}, u32[]{:S(2)}) collective-permute-start(bf16[8,288,192]{2,1,0:T(8,128)(2,1)} %get-tuple-element.225), channel_id=1, source_target_pairs={{0,1},{1,0},{2,3},{3,2},{4,5},{5,4},{6,7},{7,6},{8,9},{9,8},{10,11... | collective-permute-start | bytes 2654216 | tf_op jit(solution)/shard_map/ppermute | solution.py:46
  167.9 11.4 %collective-permute-start.15 = (bf16[2,288,768]{2,1,0:T(8,128)(2,1)S(1)}, bf16[2,288,768]{2,1,0:T(8,128)(2,1)S(1)}, u32[]{:S(2)}, u32[]{:S(2)}) collective-permute-start(bf16[2,288,768]{2,1,0:T(8,128)(2,1)S(1)} %get-tuple-element.226.dy.refs_10_), channel_id=1, source_target_pairs={{0,1},{1,0},{2,3},{3,2},{4,5},{5,4},{6,7},{7,6},{8,9},{9,8},{10,11... | collective-permute-start | bytes 2654216 | tf_op jit(solution)/shard_map/ppermute | solution.py:46
  168.2 11.2 %collective-permute-start.16 = (bf16[8,288,192]{2,1,0:T(8,128)(2,1)}, bf16[8,288,192]{2,1,0:T(8,128)(2,1)}, u32[]{:S(2)}, u32[]{:S(2)}) collective-permute-start(bf16[8,288,192]{2,1,0:T(8,128)(2,1)} %get-tuple-element.227), channel_id=1, source_target_pairs={{0,1},{1,0},{2,3},{3,2},{4,5},{5,4},{6,7},{7,6},{8,9},{9,8},{10,11... | collective-permute-start | bytes 2654216 | tf_op jit(solution)/shard_map/ppermute | solution.py:46
  168.4 10.9 %collective-permute-start.13 = (bf16[2,288,768]{2,1,0:T(8,128)(2,1)S(1)}, bf16[2,288,768]{2,1,0:T(8,128)(2,1)S(1)}, u32[]{:S(2)}, u32[]{:S(2)}) collective-permute-start(bf16[2,288,768]{2,1,0:T(8,128)(2,1)S(1)} %get-tuple-element.212.x_ref.n.ctx), channel_id=1, source_target_pairs={{0,1},{1,0},{2,3},{3,2},{4,5},{5,4},{6,7},{7,6},{8,9},{9,8},{10,11... | collective-permute-start | bytes 2654216 | tf_op jit(solution)/shard_map/ppermute | solution.py:46
  179.3 11.2 %collective-permute-start.17 = (bf16[288,768]{1,0:T(8,128)(2,1)S(1)}, bf16[288,768]{1,0:T(8,128)(2,1)S(1)}, u32[]{:S(2)}, u32[]{:S(2)}) collective-permute-start(bf16[288,768]{1,0:T(8,128)(2,1)S(1)} %get-tuple-element.228.refs_0_), channel_id=1, source_target_pairs={{0,1},{1,0},{2,3},{3,2},{4,5},{5,4},{6,7},{7,6},{8,9},{9,8},{10,11... | collective-permute-start | bytes 1327112 | tf_op jit(solution)/shard_map/ppermute | solution.py:46
  179.7 10.9 %collective-permute-start.18 = (bf16[288,768]{1,0:T(8,128)(2,1)S(1)}, bf16[288,768]{1,0:T(8,128)(2,1)S(1)}, u32[]{:S(2)}, u32[]{:S(2)}) collective-permute-start(bf16[288,768]{1,0:T(8,128)(2,1)S(1)} %get-tuple-element.229.refs_1_), channel_id=1, source_target_pairs={{0,1},{1,0},{2,3},{3,2},{4,5},{5,4},{6,7},{7,6},{8,9},{9,8},{10,11... | collective-permute-start | bytes 1327112 | tf_op jit(solution)/shard_map/ppermute | solution.py:46
  179.9 10.7 %collective-permute-start.19 = (bf16[288,768]{1,0:T(8,128)(2,1)S(1)}, bf16[288,768]{1,0:T(8,128)(2,1)S(1)}, u32[]{:S(2)}, u32[]{:S(2)}) collective-permute-start(bf16[288,768]{1,0:T(8,128)(2,1)S(1)} %get-tuple-element.230.refs_2_), channel_id=1, source_target_pairs={{0,1},{1,0},{2,3},{3,2},{4,5},{5,4},{6,7},{7,6},{8,9},{9,8},{10,11... | collective-permute-start | bytes 1327112 | tf_op jit(solution)/shard_map/ppermute | solution.py:46
  180.2 10.4 %collective-permute-start.20 = (bf16[288,768]{1,0:T(8,128)(2,1)S(1)}, bf16[288,768]{1,0:T(8,128)(2,1)S(1)}, u32[]{:S(2)}, u32[]{:S(2)}) collective-permute-start(bf16[288,768]{1,0:T(8,128)(2,1)S(1)} %get-tuple-element.231.refs_3_), channel_id=1, source_target_pairs={{0,1},{1,0},{2,3},{3,2},{4,5},{5,4},{6,7},{7,6},{8,9},{9,8},{10,11... | collective-permute-start | bytes 1327112 | tf_op jit(solution)/shard_map/ppermute | solution.py:46
  180.4 10.2 %collective-permute-start.21 = (bf16[288,768]{1,0:T(8,128)(2,1)S(1)}, bf16[288,768]{1,0:T(8,128)(2,1)S(1)}, u32[]{:S(2)}, u32[]{:S(2)}) collective-permute-start(bf16[288,768]{1,0:T(8,128)(2,1)S(1)} %get-tuple-element.232.refs_4_), channel_id=1, source_target_pairs={{0,1},{1,0},{2,3},{3,2},{4,5},{5,4},{6,7},{7,6},{8,9},{9,8},{10,11... | collective-permute-start | bytes 1327112 | tf_op jit(solution)/shard_map/ppermute | solution.py:46
  190.6 31.4 %collective-permute-start.22 = (bf16[4,192,768]{2,1,0:T(8,128)(2,1)}, bf16[4,192,768]{2,1,0:T(8,128)(2,1)}, u32[]{:S(2)}, u32[]{:S(2)}) collective-permute-start(bf16[4,192,768]{2,1,0:T(8,128)(2,1)} %get-tuple-element.256), channel_id=1, source_target_pairs={{0,2},{1,3},{2,0},{3,1},{4,6},{5,7},{6,4},{7,5},{8,10},{9,11},{10,... | collective-permute-start | bytes 3538952 | tf_op jit(solution)/shard_map/ppermute | solution.py:46
  192.0 30.8 %collective-permute-start.23 = (bf16[8,192,384]{2,1,0:T(8,128)(2,1)}, bf16[8,192,384]{2,1,0:T(8,128)(2,1)}, u32[]{:S(2)}, u32[]{:S(2)}) collective-permute-start(bf16[8,192,384]{2,1,0:T(8,128)(2,1)} %get-tuple-element.257), channel_id=1, source_target_pairs={{0,16},{16,0},{1,17},{17,1},{2,18},{18,2},{3,19},{19,3},{4,20},{20... | collective-permute-start | bytes 3538952 | tf_op jit(solution)/shard_map/ppermute | solution.py:46
  193.5 33.3 %collective-permute-start.12 = (bf16[2,288,768]{2,1,0:T(8,128)(2,1)S(1)}, bf16[2,288,768]{2,1,0:T(8,128)(2,1)S(1)}, u32[]{:S(2)}, u32[]{:S(2)}) collective-permute-start(bf16[2,288,768]{2,1,0:T(8,128)(2,1)S(1)} %get-tuple-element.203.x_ref.ctx.n), channel_id=1, source_target_pairs={{0,1},{1,0},{2,3},{3,2},{4,5},{5,4},{6,7},{7,6},{8,9},{9,8},{10,11... | collective-permute-start | bytes 2654216 | tf_op jit(solution)/shard_map/ppermute | solution.py:46
  193.5 34.0 %collective-permute-start.26 = (bf16[8,288,192]{2,1,0:T(8,128)(2,1)}, bf16[8,288,192]{2,1,0:T(8,128)(2,1)}, u32[]{:S(2)}, u32[]{:S(2)}) collective-permute-start(bf16[8,288,192]{2,1,0:T(8,128)(2,1)} %get-tuple-element.267), channel_id=1, source_target_pairs={{0,1},{1,0},{2,3},{3,2},{4,5},{5,4},{6,7},{7,6},{8,9},{9,8},{10,11... | collective-permute-start | bytes 2654216 | tf_op jit(solution)/shard_map/ppermute | solution.py:46
  222.0 6.7 %collective-permute-start.25 = (bf16[2,288,768]{2,1,0:T(8,128)(2,1)S(1)}, bf16[2,288,768]{2,1,0:T(8,128)(2,1)S(1)}, u32[]{:S(2)}, u32[]{:S(2)}) collective-permute-start(bf16[2,288,768]{2,1,0:T(8,128)(2,1)S(1)} %get-tuple-element.266.refs_10_.dy), channel_id=1, source_target_pairs={{0,1},{1,0},{2,3},{3,2},{4,5},{5,4},{6,7},{7,6},{8,9},{9,8},{10,11... | collective-permute-start | bytes 2654216 | tf_op jit(solution)/shard_map/ppermute | solution.py:46
  222.0 30.7 %collective-permute-start.33 = (bf16[4,48,1536]{2,1,0:T(8,128)(2,1)}, bf16[4,48,1536]{2,1,0:T(8,128)(2,1)S(1)}, u32[]{:S(2)}, u32[]{:S(2)}) collective-permute-start(bf16[4,48,1536]{2,1,0:T(8,128)(2,1)} %get-tuple-element.304), channel_id=1, source_target_pairs={{0,2},{1,3},{2,0},{3,1},{4,6},{5,7},{6,4},{7,5},{8,10},{9,11},{10,... | collective-permute-start | bytes 1769480 | tf_op jit(solution)/shard_map/ppermute | solution.py:46
  222.8 18.8 %collective-permute-start.24 = (bf16[8,288,192]{2,1,0:T(8,128)(2,1)}, bf16[8,288,192]{2,1,0:T(8,128)(2,1)S(1)}, u32[]{:S(2)}, u32[]{:S(2)}) collective-permute-start(bf16[8,288,192]{2,1,0:T(8,128)(2,1)} %get-tuple-element.265), channel_id=1, source_target_pairs={{0,1},{1,0},{2,3},{3,2},{4,5},{5,4},{6,7},{7,6},{8,9},{9,8},{10,11... | collective-permute-start | bytes 2654216 | tf_op jit(solution)/shard_map/ppermute | solution.py:46
  226.8 25.9 %collective-permute-start.34 = (bf16[8,48,768]{2,1,0:T(8,128)(2,1)S(1)}, bf16[8,48,768]{2,1,0:T(8,128)(2,1)S(1)}, u32[]{:S(2)}, u32[]{:S(2)}) collective-permute-start(bf16[8,48,768]{2,1,0:T(8,128)(2,1)S(1)} %copy-done.90), channel_id=1, source_target_pairs={{0,16},{16,0},{1,17},{17,1},{2,18},{18,2},{3,19},{19,3},{4,20},{20... | collective-permute-start | bytes 1769480 | tf_op jit(solution)/shard_map/ppermute | solution.py:46
  227.4 25.3 %collective-permute-start.36 = (bf16[4,192,384]{2,1,0:T(8,128)(2,1)S(1)}, bf16[4,192,384]{2,1,0:T(8,128)(2,1)S(1)}, u32[]{:S(2)}, u32[]{:S(2)}) collective-permute-start(bf16[4,192,384]{2,1,0:T(8,128)(2,1)S(1)} %get-tuple-element.398), channel_id=1, source_target_pairs={{0,2},{1,3},{2,0},{3,1},{4,6},{5,7},{6,4},{7,5},{8,10},{9,11},{10,... | collective-permute-start | bytes 1769480 | tf_op jit(solution)/shard_map/ppermute | solution.py:46
  228.7 26.3 %collective-permute-start.35 = (bf16[4,192,384]{2,1,0:T(8,128)(2,1)S(1)}, bf16[4,192,384]{2,1,0:T(8,128)(2,1)S(1)}, u32[]{:S(2)}, u32[]{:S(2)}) collective-permute-start(bf16[4,192,384]{2,1,0:T(8,128)(2,1)S(1)} %get-tuple-element.400), channel_id=1, source_target_pairs={{0,16},{16,0},{1,17},{17,1},{2,18},{18,2},{3,19},{19,3},{4,20},{20... | collective-permute-start | bytes 1769480 | tf_op jit(solution)/shard_map/ppermute | solution.py:46
  256.6 105.3 %reduce-scatter.5.cloned.1.call-start = ((), (), s32[]{:S(2)}) async-start(), calls=%async_computation.4 | async-start | bytes 2211840 | tf_op jit(solution)/shard_map/reduce_scatter | solution.py:140
  257.5 2.3 collective-permute-start.27
  257.7 2.7 collective-permute-start.28
  258.1 36.3 %collective-permute-start.37 = (bf16[4,192,768]{2,1,0:T(8,128)(2,1)}, bf16[4,192,768]{2,1,0:T(8,128)(2,1)}, u32[]{:S(2)}, u32[]{:S(2)}) collective-permute-start(bf16[4,192,768]{2,1,0:T(8,128)(2,1)} %get-tuple-element.312), channel_id=1, source_target_pairs={{0,2},{1,3},{2,0},{3,1},{4,6},{5,7},{6,4},{7,5},{8,10},{9,11},{10,... | collective-permute-start | bytes 3538952 | tf_op jit(solution)/shard_map/ppermute | solution.py:46
  259.3 35.0 %collective-permute-start.38 = (bf16[8,192,384]{2,1,0:T(8,128)(2,1)}, bf16[8,192,384]{2,1,0:T(8,128)(2,1)S(1)}, u32[]{:S(2)}, u32[]{:S(2)}) collective-permute-start(bf16[8,192,384]{2,1,0:T(8,128)(2,1)} %get-tuple-element.313), channel_id=1, source_target_pairs={{0,16},{16,0},{1,17},{17,1},{2,18},{18,2},{3,19},{19,3},{4,20},{20... | collective-permute-start | bytes 3538952 | tf_op jit(solution)/shard_map/ppermute | solution.py:46
  259.9 2.8 collective-permute-start.29
  259.9 3.7 collective-permute-start.30
  260.4 3.2 collective-permute-start.31
  262.7 30.0 %collective-permute-start.40 = (bf16[4,48,768]{2,1,0:T(8,128)(2,1)}, bf16[4,48,768]{2,1,0:T(8,128)(2,1)}, u32[]{:S(2)}, u32[]{:S(2)}) collective-permute-start(bf16[4,48,768]{2,1,0:T(8,128)(2,1)} %get-tuple-element.406), channel_id=1, source_target_pairs={{0,2},{1,3},{2,0},{3,1},{4,6},{5,7},{6,4},{7,5},{8,10},{9,11},{10,... | collective-permute-start | bytes 884744 | tf_op jit(solution)/shard_map/ppermute | solution.py:46
  277.7 1.8 collective-permute-start.32
  278.1 15.5 %collective-permute-start.39 = (bf16[4,48,768]{2,1,0:T(8,128)(2,1)S(1)}, bf16[4,48,768]{2,1,0:T(8,128)(2,1)S(1)}, u32[]{:S(2)}, u32[]{:S(2)}) collective-permute-start(bf16[4,48,768]{2,1,0:T(8,128)(2,1)S(1)} %get-tuple-element.408), channel_id=1, source_target_pairs={{0,16},{16,0},{1,17},{17,1},{2,18},{18,2},{3,19},{19,3},{4,20},{20... | collective-permute-start | bytes 884744 | tf_op jit(solution)/shard_map/ppermute | solution.py:46
  279.6 14.0 %collective-permute-start.41 = (bf16[128,768]{1,0:T(8,128)(2,1)S(1)}, bf16[128,768]{1,0:T(8,128)(2,1)S(1)}, u32[]{:S(2)}, u32[]{:S(2)}) collective-permute-start(bf16[128,768]{1,0:T(8,128)(2,1)S(1)} %add_convert_fusion.26.rest_0_), channel_id=1, source_target_pairs={{0,4},{1,5},{2,6},{3,7},{4,0},{5,1},{6,2},{7,3},{8,12},{9,13},{10,... | collective-permute-start | bytes 589832 | tf_op jit(solution)/shard_map/ppermute | solution.py:46
  295.5 17.5 %collective-permute-start.43 = (bf16[4,192,384]{2,1,0:T(8,128)(2,1)}, bf16[4,192,384]{2,1,0:T(8,128)(2,1)S(1)}, u32[]{:S(2)}, u32[]{:S(2)}) collective-permute-start(bf16[4,192,384]{2,1,0:T(8,128)(2,1)} %get-tuple-element.394), channel_id=1, source_target_pairs={{0,2},{1,3},{2,0},{3,1},{4,6},{5,7},{6,4},{7,5},{8,10},{9,11},{10,... | collective-permute-start | bytes 1769480 | tf_op jit(solution)/shard_map/ppermute | solution.py:46
  297.9 15.0 %collective-permute-start.42 = (bf16[4,192,384]{2,1,0:T(8,128)(2,1)S(1)}, bf16[4,192,384]{2,1,0:T(8,128)(2,1)S(1)}, u32[]{:S(2)}, u32[]{:S(2)}) collective-permute-start(bf16[4,192,384]{2,1,0:T(8,128)(2,1)S(1)} %get-tuple-element.396), channel_id=1, source_target_pairs={{0,16},{16,0},{1,17},{17,1},{2,18},{18,2},{3,19},{19,3},{4,20},{20... | collective-permute-start | bytes 1769480 | tf_op jit(solution)/shard_map/ppermute | solution.py:46
  298.6 14.3 %collective-permute-start.44 = (bf16[128,768]{1,0:T(8,128)(2,1)S(1)}, bf16[128,768]{1,0:T(8,128)(2,1)S(1)}, u32[]{:S(2)}, u32[]{:S(2)}) collective-permute-start(bf16[128,768]{1,0:T(8,128)(2,1)S(1)} %add_convert_fusion.25.rest_1_), channel_id=1, source_target_pairs={{0,8},{1,9},{2,10},{3,11},{4,12},{5,13},{6,14},{7,15},{8,0},{9,1},... | collective-permute-start | bytes 589832 | tf_op jit(solution)/shard_map/ppermute | solution.py:46
  310.1 13.9 %collective-permute-start.46 = (bf16[4,48,1536]{2,1,0:T(8,128)(2,1)}, bf16[4,48,1536]{2,1,0:T(8,128)(2,1)}, u32[]{:S(2)}, u32[]{:S(2)}) collective-permute-start(bf16[4,48,1536]{2,1,0:T(8,128)(2,1)} %get-tuple-element.334), channel_id=1, source_target_pairs={{0,2},{1,3},{2,0},{3,1},{4,6},{5,7},{6,4},{7,5},{8,10},{9,11},{10,... | collective-permute-start | bytes 1769480 | tf_op jit(solution)/shard_map/ppermute | solution.py:46
  311.5 13.5 %collective-permute-start.47 = (bf16[8,48,768]{2,1,0:T(8,128)(2,1)}, bf16[8,48,768]{2,1,0:T(8,128)(2,1)}, u32[]{:S(2)}, u32[]{:S(2)}) collective-permute-start(bf16[8,48,768]{2,1,0:T(8,128)(2,1)} %get-tuple-element.335), channel_id=1, source_target_pairs={{0,16},{16,0},{1,17},{17,1},{2,18},{18,2},{3,19},{19,3},{4,20},{20... | collective-permute-start | bytes 1769480 | tf_op jit(solution)/shard_map/ppermute | solution.py:46
  318.5 6.5 %collective-permute-start.45 = (bf16[272,128]{1,0:T(8,128)(2,1)}, bf16[272,128]{1,0:T(8,128)(2,1)S(1)}, u32[]{:S(2)}, u32[]{:S(2)}) collective-permute-start(bf16[272,128]{1,0:T(8,128)(2,1)} %join.1), channel_id=1, source_target_pairs={{0,1},{1,0},{2,3},{3,2},{4,5},{5,4},{6,7},{7,6},{8,9},{9,8},{10,11... | collective-permute-start | bytes 208904 | tf_op jit(solution)/shard_map/ppermute | solution.py:46
  327.1 12.5 %collective-permute-start.50 = (bf16[4,48,768]{2,1,0:T(8,128)(2,1)S(1)}, bf16[4,48,768]{2,1,0:T(8,128)(2,1)S(1)}, u32[]{:S(2)}, u32[]{:S(2)}) collective-permute-start(bf16[4,48,768]{2,1,0:T(8,128)(2,1)S(1)} %get-tuple-element.402), channel_id=1, source_target_pairs={{0,2},{1,3},{2,0},{3,1},{4,6},{5,7},{6,4},{7,5},{8,10},{9,11},{10,... | collective-permute-start | bytes 884744 | tf_op jit(solution)/shard_map/ppermute | solution.py:46
  330.2 9.3 %collective-permute-start.49 = (bf16[4,48,768]{2,1,0:T(8,128)(2,1)}, bf16[4,48,768]{2,1,0:T(8,128)(2,1)S(1)}, u32[]{:S(2)}, u32[]{:S(2)}) collective-permute-start(bf16[4,48,768]{2,1,0:T(8,128)(2,1)} %get-tuple-element.404), channel_id=1, source_target_pairs={{0,16},{16,0},{1,17},{17,1},{2,18},{18,2},{3,19},{19,3},{4,20},{20... | collective-permute-start | bytes 884744 | tf_op jit(solution)/shard_map/ppermute | solution.py:46
  331.4 8.1 %collective-permute-start.51 = (bf16[128,768]{1,0:T(8,128)(2,1)S(1)}, bf16[128,768]{1,0:T(8,128)(2,1)S(1)}, u32[]{:S(2)}, u32[]{:S(2)}) collective-permute-start(bf16[128,768]{1,0:T(8,128)(2,1)S(1)} %add_convert_fusion.24), channel_id=1, source_target_pairs={{0,2},{1,3},{2,0},{3,1},{4,6},{5,7},{6,4},{7,5},{8,10},{9,11},{10,... | collective-permute-start | bytes 589832 | tf_op jit(solution)/shard_map/ppermute | solution.py:46
  332.8 6.8 %collective-permute-start.48 = (bf16[272,128]{1,0:T(8,128)(2,1)S(1)}, bf16[272,128]{1,0:T(8,128)(2,1)S(1)}, u32[]{:S(2)}, u32[]{:S(2)}) collective-permute-start(bf16[272,128]{1,0:T(8,128)(2,1)S(1)} %add_convert_fusion.37), channel_id=1, source_target_pairs={{0,2},{1,3},{2,0},{3,1},{4,6},{5,7},{6,4},{7,5},{8,10},{9,11},{10,... | collective-permute-start | bytes 208904 | tf_op jit(solution)/shard_map/ppermute | solution.py:46
  339.6 5.2 %collective-permute-start.52 = (bf16[272,128]{1,0:T(8,128)(2,1)S(1)}, bf16[272,128]{1,0:T(8,128)(2,1)S(1)}, u32[]{:S(2)}, u32[]{:S(2)}) collective-permute-start(bf16[272,128]{1,0:T(8,128)(2,1)S(1)} %add_convert_fusion.36), channel_id=1, source_target_pairs={{0,16},{16,0},{1,17},{17,1},{2,18},{18,2},{3,19},{19,3},{4,20},{20... | collective-permute-start | bytes 208904 | tf_op jit(solution)/shard_map/ppermute | solution.py:46
  340.7 10.6 %collective-permute-start.54 = (bf16[384,384]{1,0:T(8,128)(2,1)S(1)}, bf16[384,384]{1,0:T(8,128)(2,1)S(1)}, u32[]{:S(2)}, u32[]{:S(2)}) collective-permute-start(bf16[384,384]{1,0:T(8,128)(2,1)S(1)} %bitcast.100), channel_id=1, source_target_pairs={{0,16},{16,0},{1,17},{17,1},{2,18},{18,2},{3,19},{19,3},{4,20},{20... | collective-permute-start | bytes 884744 | tf_op jit(solution)/shard_map/ppermute | solution.py:46
  341.7 9.5 %collective-permute-start.53 = (bf16[128,768]{1,0:T(8,128)(2,1)S(1)}, bf16[128,768]{1,0:T(8,128)(2,1)S(1)}, u32[]{:S(2)}, u32[]{:S(2)}) collective-permute-start(bf16[128,768]{1,0:T(8,128)(2,1)S(1)} %add_convert_fusion.23), channel_id=1, source_target_pairs={{0,16},{16,0},{1,17},{17,1},{2,18},{18,2},{3,19},{19,3},{4,20},{20... | collective-permute-start | bytes 589832 | tf_op jit(solution)/shard_map/ppermute | solution.py:46
  343.0 15.6 %collective-permute-start.57 = (bf16[2,96,768]{2,1,0:T(8,128)(2,1)S(1)}, bf16[2,96,768]{2,1,0:T(8,128)(2,1)S(1)}, u32[]{:S(2)}, u32[]{:S(2)}) collective-permute-start(bf16[2,96,768]{2,1,0:T(8,128)(2,1)S(1)} %pad_maximum_fusion.5), channel_id=1, source_target_pairs={{0,4},{1,5},{2,6},{3,7},{4,0},{5,1},{6,2},{7,3},{8,12},{9,13},{10,... | collective-permute-start | bytes 884744 | tf_op jit(solution)/shard_map/ppermute | solution.py:46
  351.3 11.8 %collective-permute-start.55 = (bf16[272,128]{1,0:T(8,128)(2,1)S(1)}, bf16[272,128]{1,0:T(8,128)(2,1)S(1)}, u32[]{:S(2)}, u32[]{:S(2)}) collective-permute-start(bf16[272,128]{1,0:T(8,128)(2,1)S(1)} %add_convert_fusion.35), channel_id=1, source_target_pairs={{0,4},{1,5},{2,6},{3,7},{4,0},{5,1},{6,2},{7,3},{8,12},{9,13},{10,... | collective-permute-start | bytes 208904 | tf_op jit(solution)/shard_map/ppermute | solution.py:46
  353.8 15.0 %collective-permute-start.61 = (bf16[128,768]{1,0:T(8,128)(2,1)S(1)}, bf16[128,768]{1,0:T(8,128)(2,1)S(1)}, u32[]{:S(2)}, u32[]{:S(2)}) collective-permute-start(bf16[128,768]{1,0:T(8,128)(2,1)S(1)} %add_convert_fusion.22), channel_id=1, source_target_pairs={{0,1},{1,0},{2,3},{3,2},{4,5},{5,4},{6,7},{7,6},{8,9},{9,8},{10,11... | collective-permute-start | bytes 589832 | tf_op jit(solution)/shard_map/ppermute | solution.py:46
  358.8 8.4 %collective-permute-start.58 = (bf16[1,96,768]{2,1,0:T(8,128)(2,1)S(1)}, bf16[1,96,768]{2,1,0:T(8,128)(2,1)S(1)}, u32[]{:S(2)}, u32[]{:S(2)}) collective-permute-start(bf16[1,96,768]{2,1,0:T(8,128)(2,1)S(1)} %get-tuple-element.409), channel_id=1, source_target_pairs={{0,8},{1,9},{2,10},{3,11},{4,12},{5,13},{6,14},{7,15},{8,0},{9,1},... | collective-permute-start | bytes 442376 | tf_op jit(solution)/shard_map/ppermute | solution.py:46
  361.8 15.3 %collective-permute-start.60 = (bf16[576,384]{1,0:T(8,128)(2,1)}, bf16[576,384]{1,0:T(8,128)(2,1)S(1)}, u32[]{:S(2)}, u32[]{:S(2)}) collective-permute-start(bf16[576,384]{1,0:T(8,128)(2,1)} %bitcast.96), channel_id=1, source_target_pairs={{0,16},{16,0},{1,17},{17,1},{2,18},{18,2},{3,19},{19,3},{4,20},{20... | collective-permute-start | bytes 1327112 | tf_op jit(solution)/shard_map/ppermute | solution.py:46
  367.2 12.0 %collective-permute-start.59 = (bf16[96,768]{1,0:T(8,128)(2,1)S(1)}, bf16[96,768]{1,0:T(8,128)(2,1)S(1)}, u32[]{:S(2)}, u32[]{:S(2)}) collective-permute-start(bf16[96,768]{1,0:T(8,128)(2,1)S(1)} %fusion.16.refs_0_), channel_id=1, source_target_pairs={{0,16},{16,0},{1,17},{17,1},{2,18},{18,2},{3,19},{19,3},{4,20},{20... | collective-permute-start | bytes 442376 | tf_op jit(solution)/shard_map/ppermute | solution.py:46
  368.9 5.3 %collective-permute-start.56 = (bf16[272,128]{1,0:T(8,128)(2,1)S(1)}, bf16[272,128]{1,0:T(8,128)(2,1)S(1)}, u32[]{:S(2)}, u32[]{:S(2)}) collective-permute-start(bf16[272,128]{1,0:T(8,128)(2,1)S(1)} %add_convert_fusion.34.left), channel_id=1, source_target_pairs={{0,8},{1,9},{2,10},{3,11},{4,12},{5,13},{6,14},{7,15},{8,0},{9,1},... | collective-permute-start | bytes 208904 | tf_op jit(solution)/shard_map/ppermute | solution.py:46
  (93 other events, 1056.8 us)
Sparse Core Ops, SparseCore 0:
  10.2 102.2 all-gather.1
  256.7 28.2 reduce-scatter.2
  317.0 44.7 reduce-scatter.4
